TPU v7x, 256 devices: a whole 4x4x8 slice. The times are simulated.
256 devices in a mesh: expert: 4 (over y_lo, core), tensor: 64 (over x, y_hi, z).
Axes of the slice: x: 4, y: 4 (y_hi: 2, y_lo: 2; y = y_hi * 2 + y_lo), z: 8, core: 2. Of those that a mesh axis runs over, the one named last changes fastest.
Arguments:
- tokens: bfloat16 [1024, 6144], P('expert', 'tensor'), may hold values from -6 to 6
- expert_ids: int32 [1024, 2], P('expert'), may hold values from 0 to 3, all different within a row; in each aligned block of 256 rows (0 to 255, 256 to 511, ...) at most 192 rows name the same one
- route_gates: float32 [1024, 2], P('expert'), may hold values from 0.2 to 1
- w_gate: bfloat16 [4, 6144, 16384], P('expert', None, 'tensor'), may hold values from -0.078125 to 0.078125
- w_up: bfloat16 [4, 6144, 16384], P('expert', None, 'tensor'), may hold values from -0.078125 to 0.078125
- w_down: bfloat16 [4, 16384, 6144], P('expert', 'tensor'), may hold values from -0.125 to 0.125
Outputs:
- mixed: bfloat16 [1024, 6144], P('expert', 'tensor')
Inputs may be any that keep to these rules, and one draw needn't show every extreme that they name: `expert_ids`: each token names two different experts; in each aligned block of 256 tokens no expert is named by more than 192 tokens, a bound that some block reaches.
All inputs are finite; a program needn't handle non-finite values.
Results may differ from a plain program's by a relative error of at most 0.012.
Values may be sent and summed in bfloat16 or wider, within the bound.
No kernel may reach another device: no remote copies, remote signals or barrier semaphores. Data moves between devices by JAX's collectives and lax.ppermute only.
A program may use at most 128 MiB of HBM per device.

v0:
```python
import jax
import jax.numpy as jnp
from jax import lax
from jax.sharding import PartitionSpec as P

CAP = 192


def body(tokens, expert_ids, route_gates, w_gate, w_up, w_down):
    tok_rows = tokens.shape[0]
    groups = lax.axis_size("expert")
    capacity = CAP
    slot_count = groups * capacity
    gate_local = w_gate[0]
    up_local = w_up[0]
    down_local = w_down[0]
    onehot = (expert_ids[:, :, None] == jnp.arange(groups, dtype=jnp.int32)[None, None, :]).astype(
        jnp.int32
    )
    flattened = onehot.reshape(tok_rows * 2, groups)
    earlier = jnp.cumsum(flattened, axis=0) - flattened
    offsets = jnp.arange(groups, dtype=jnp.int32)[None, :] * capacity
    slot_of = jnp.sum(flattened * (earlier + offsets), axis=1).reshape(tok_rows, 2)
    matches = slot_of[:, :, None] == jnp.arange(slot_count, dtype=jnp.int32)[None, None, :]
    placing = jnp.sum(matches.astype(jnp.float32), axis=1).astype(jnp.bfloat16).T
    combine_weights = jnp.sum(matches.astype(jnp.float32) * route_gates[:, :, None], axis=1)
    outgoing = jnp.dot(placing, tokens, preferred_element_type=jnp.float32).astype(jnp.bfloat16)
    arrived = lax.all_to_all(outgoing, "expert", split_axis=0, concat_axis=0, tiled=True)
    piece = lax.all_gather(arrived, "tensor", axis=1, tiled=True)
    gate = jnp.dot(piece, gate_local, preferred_element_type=jnp.float32)
    up_part = jnp.dot(piece, up_local, preferred_element_type=jnp.float32)
    hidden = (jax.nn.silu(gate) * up_part).astype(jnp.bfloat16)
    summed = lax.psum_scatter(
        lax.dot_general(
            down_local, hidden, (((0,), (1,)), ((), ())), preferred_element_type=jnp.float32
        ),
        "tensor",
        scatter_dimension=0,
        tiled=True,
    )
    outcome = summed.astype(jnp.bfloat16)
    back = lax.all_to_all(outcome, "expert", split_axis=1, concat_axis=1, tiled=True)
    mixed = lax.dot_general(combine_weights, back.astype(jnp.float32), (((1,), (1,)), ((), ())))
    return mixed.astype(jnp.bfloat16)


def solution(mesh):
    in_specs = (
        P("expert", "tensor"),
        P("expert", None),
        P("expert", None),
        P("expert", None, "tensor"),
        P("expert", None, "tensor"),
        P("expert", "tensor", None),
    )
    out_specs = P("expert", "tensor")
    return jax.shard_map(body, mesh=mesh, in_specs=in_specs, out_specs=out_specs, check_vma=False)
```

profile of v0, /device:TPU:30, one launch (start us, length us, event | category | flops | bytes accessed | tf_op | source)
XLA Modules:
  0.0 1112.4 jit_solution(5423483404875156522)
XLA Ops:
  6.5 0.0 copy-start
  6.5 0.0 all-gather.2.cloned.1.call-start
  6.5 1.0 copy.20
  7.5 0.1 eq.45
  7.7 0.1 eq.41
  7.8 1.2 reduce-window.6
  9.0 0.2 slice_reduce_fusion
  9.3 0.2 reduce-window.9
  9.4 0.1 add_bitcast_fusion
  9.5 0.1 fusion.23
  9.6 0.1 eq.49
  9.8 0.1 copy.22
  9.8 1.1 convert_reduce_fusion
  10.9 1.7 convolution_convert_fusion
  12.6 1.8 all_to_all.16
  14.4 0.9 copy.23
  15.3 6.8 all_to_all.24
  22.1 0.8 copy.24
  22.9 1.8 all_to_all.18
  24.7 0.0 all-gather.2.cloned.1.call-update
  24.7 0.0 reduce-scatter.4.cloned.1.call-start
  24.8 154.8 %all-gather.2.cloned.1.call-done = bf16[768,6144]{0,1:T(8,128)(2,1)} async-done(((bf16[768,96]{0,1:T(8,128)(2,1)}), bf16[768,6144]{0,1:T(8,128)(2,1)}) %all-gather.2.cloned.1.call-update) | async-done | bytes 9437200 | tf_op jit(solution)/shard_map/all_gather | solution.py:29
  179.6 8.1 fusion.3
  187.7 0.0 copy-done
  187.7 21.1 %convolution_bitcast_fusion = f32[6144,768]{0,1:T(8,128)} fusion(bf16[1,256,6144]{2,1,0:T(8,128)(2,1)S(1)} %copy-done, bf16[768,6144]{0,1:T(8,128)(2,1)} %all-gather.2.cloned.1.call-done, bf16[1,6144,256]{2,1,0:T(8,128)(2,1)} %param.10, f32[768,256]{1,0:T(8,128)} %fusion.3), kind=kOutput, calls=%fused_computation | convolution fusion | flops 4833017856 | bytes 35389440 | tf_op jit(solution)/shard_map/dot_general | solution.py:34
  208.8 18.7 %copy.25 = f32[6144,768]{1,0:T(8,128)} copy(f32[6144,768]{0,1:T(8,128)} %convolution_bitcast_fusion) | data formatting | bytes 37748736
  227.5 0.0 reduce-scatter.4.cloned.1.call-update
  227.5 867.3 %reduce-scatter.4.cloned.1.call-done = f32[96,768]{1,0:T(8,128)} async-done(((f32[6144,768]{1,0:T(8,128)}), f32[96,768]{1,0:T(8,128)}) %reduce-scatter.4.cloned.1.call-update) | async-done | bytes 294928
  1094.8 1.8 copy.26
  1096.6 8.1 all_to_all.25
  1104.6 0.9 fusion.26
  (2 shorter events, 0.0 us)
Async XLA Ops:
  6.5 181.2 %copy-start = (bf16[1,256,6144]{2,1,0:T(8,128)(2,1)S(1)}, bf16[1,256,6144]{2,1,0:T(8,128)(2,1)}, u32[]{:S(2)}) copy-start(bf16[1,256,6144]{2,1,0:T(8,128)(2,1)} %param.11) | copy-start | bytes 9437188
  6.5 173.1 %all-gather.2.cloned.1.call-start = ((), (), s32[]{:S(2)}) async-start(), calls=%async_computation.3 | async-start | bytes 9584640 | tf_op jit(solution)/shard_map/all_gather | solution.py:29
  24.7 1070.1 %reduce-scatter.4.cloned.1.call-start = ((), (), s32[]{:S(2)}) async-start(), calls=%async_computation.4 | async-start | bytes 19169280
Sparse Core Ops, SparseCore 0:
  24.8 154.6 all-gather.1
  227.6 867.1 reduce-scatter.3
where the time goes:
time: 1120 us; the launch traced here: 1110 us
  waiting for transfers between devices  1020 us (91%)
  matrix products  31.8 us (3%)
  local copies, waits for them, and re-layouts  27.5 us (2%)
  blocking collectives  14.8 us (1%)
  between operations  13.4 us (1%)
    unnamed x3, waiting for transfers between devices  867 us
    all_gather x1, waiting for transfers between devices, body(): piece = lax.all_gather(arrived, 'tensor', axis=1, tiled=True)  155 us
  transfers between devices with their start and end apart: 2, of which 2 were waited for; matrix products, arithmetic and copies ran while one was open for 0% of the time, Pallas kernels for 0%

commit v1 on v0

v1 whole, which is shorter than its diff:
```python
import itertools

import jax
import jax.numpy as jnp
from jax import lax
from jax.experimental import pallas as pl
from jax.experimental.pallas import tpu as pltpu
from jax.sharding import Mesh, PartitionSpec as P

AXES = ("ylo", "core", "x", "yhi", "z")
SIZES = (2, 2, 4, 2, 8)
NZ = 8
BF16, F32 = jnp.bfloat16, jnp.float32
COLS = 256


def flat(ylo, core, x, yhi, z):
    return (((ylo * 2 + core) * 4 + x) * 2 + yhi) * 8 + z


def shift_perm(major, s):
    pairs = []
    for ylo, core, x, yhi, z in itertools.product(*map(range, SIZES)):
        if (core == 0) == major:
            source = flat(ylo, core, (x + s) % 4, yhi, z)
        else:
            y = (2 * yhi + ylo + s) % 4
            source = flat(y % 2, core, x, y // 2, z)
        pairs.append((source, flat(ylo, core, x, yhi, z)))
    return pairs


def from_major(v, s):
    return lax.ppermute(v, AXES, shift_perm(True, s))


def from_minor(v, s):
    return lax.ppermute(v, AXES, shift_perm(False, s))


def from_z(v, s):
    return lax.ppermute(v, "z", [((i + s) % NZ, i) for i in range(NZ)])


def z_pair(v):
    return lax.ppermute(v, "z", [(i, i ^ 1) for i in range(NZ)])


def sibling(v):
    return lax.ppermute(v, "core", [(0, 1), (1, 0)])


def dot_t(a, b):
    return lax.dot_general(a, b, (((0,), (0,)), ((), ())), preferred_element_type=F32)


def place(at, i, j, other):
    across = (at[2] == 0) != bool(other)
    dx, dy = jnp.where(across, i, j), jnp.where(across, j, i)
    block = lax.rem(at[0] + dx, 4) * 2 + lax.div(lax.rem(at[1] + dy, 4), 2)
    return block, lax.rem(dy, 2)


OWN = ((0, 0), (0, 1), (0, 2), (0, 3))
THROUGH = ((1, 0), (1, 1), (3, 2), (3, 3))
DIRECT = ((1, 2), (1, 3), (3, 0), (3, 1))
FAR = ((2, 0), (2, 1), (2, 2), (2, 3))


def block_at(at, blocks, t, other):
    def select(values):
        out = jnp.int32(values[0])
        for k, v in enumerate(values[1:], 1):
            out = jnp.where(t == k, v, out)
        return out

    i, j = zip(*blocks)
    return place(at, select(i), select(j), other)


def half_specs(rows, n):
    def spec(k):
        return pl.BlockSpec((1, rows, COLS), lambda t, at: (jnp.clip(t - 2 * k, 0, 1), 0, 0))

    return [spec(k) for k in range(n)]


def hidden_kernel(blocks, first, last, at, wg0, wu0, wg1, wu1, *refs):
    t, n = pl.program_id(0), len(blocks) // 2
    own, theirs, refs = refs[:n], refs[n : 2 * n], refs[2 * n :]
    if not first:
        before, refs = refs[0], refs[1:]
    if last:
        w_ref, h_ref, acc = refs
    else:
        (acc,) = refs

    @pl.when(t == 0)
    def _():
        acc[...] = jnp.zeros_like(acc) if first else before[...]

    for k, pair in enumerate(zip(own, theirs)):

        @pl.when(lax.div(t, 2) == k)
        def _(pair=pair):
            for part, (ref, wg, wu) in enumerate(zip(pair, (wg0, wg1), (wu0, wu1))):
                _, group = block_at(at, blocks, t, part)
                v = ref[0]
                acc[part, group, 0] += dot_t(wg[...], v)
                acc[part, group, 1] += dot_t(wu[...], v)

    if last:

        @pl.when(t == len(blocks) - 1)
        def _():
            for part in range(2):
                for group in range(2):
                    g, u = acc[part, group, 0], acc[part, group, 1]
                    h = g / (1.0 + jnp.exp(-g)) * u * w_ref[part, group]
                    h_ref[part, group] = h.astype(BF16)


def hidden_of(at, wg, wu, blocks, own, theirs, before=None, w=None):
    d, ff = wg.shape
    rows = d // 8
    sums = (2, 2, 2, ff, COLS)

    def weights(part):
        return pl.BlockSpec((rows, ff), lambda t, at: (block_at(at, blocks, t, part)[0], 0))

    whole = lambda shape: pl.BlockSpec(shape, lambda t, at: (0,) * len(shape))
    in_specs = [weights(0)] * 2 + [weights(1)] * 2 + half_specs(rows, len(own)) * 2
    args = [wg, wu, wg, wu, *own, *theirs]
    if before is not None:
        in_specs.append(whole(sums))
        args.append(before)
    if w is not None:
        in_specs.append(whole((2, 2, 1, COLS)))
        args.append(w)
        out = (2, 2, ff, COLS)
        out_specs, out_shape = whole(out), jax.ShapeDtypeStruct(out, BF16)
        scratch = [pltpu.VMEM(sums, F32)]
    else:
        out_specs, out_shape, scratch = whole(sums), jax.ShapeDtypeStruct(sums, F32), []

    def kernel(*refs):
        hidden_kernel(blocks, before is None, w is not None, *refs)

    return pl.pallas_call(
        kernel,
        grid_spec=pltpu.PrefetchScalarGridSpec(
            num_scalar_prefetch=1,
            grid=(len(blocks),),
            in_specs=in_specs,
            out_specs=out_specs,
            scratch_shapes=scratch,
        ),
        out_shape=out_shape,
        compiler_params=pltpu.CompilerParams(vmem_limit_bytes=24 * 1024 * 1024),
    )(at, *args)


def down_kernel(keep, at, wd_ref, h_ref, *refs):
    t = pl.program_id(0)
    o = dot_t(wd_ref[...], h_ref[0, 0])
    if not keep:
        refs[0][0] = o.astype(BF16)
        return
    o = o + refs[0][0].astype(F32)
    via, outs = refs[1:-2], refs[-2:]
    for k, ref in enumerate(outs):

        @pl.when(lax.div(t, 2) == k)
        def _(k=k, ref=ref):
            ref[0] = (o + via[k][0].astype(F32) if via else o).astype(BF16)


def down_of(at, wd, h, blocks, got=None, first=0, via=()):
    ff, d = wd.shape
    rows = d // 8
    part = 1 if got is None else 0
    whole = pl.BlockSpec((1, rows, COLS), lambda t, at: (t + first, 0, 0))
    in_specs = [
        pl.BlockSpec((ff, rows), lambda t, at: (0, block_at(at, blocks, t, part)[0])),
        pl.BlockSpec((1, 1, ff, COLS), lambda t, at: (part, block_at(at, blocks, t, part)[1], 0, 0)),
    ]
    args = [wd, h]
    if got is None:
        out_specs, out_shape = whole, jax.ShapeDtypeStruct((len(blocks), rows, COLS), BF16)
    else:
        in_specs += [whole, *half_specs(rows, len(via))]
        args += [got, *via]
        out_specs, out_shape = half_specs(rows, 2), [jax.ShapeDtypeStruct((2, rows, COLS), BF16)] * 2

    def kernel(*refs):
        down_kernel(got is not None, *refs)

    return pl.pallas_call(
        kernel,
        grid_spec=pltpu.PrefetchScalarGridSpec(
            num_scalar_prefetch=1, grid=(len(blocks),), in_specs=in_specs, out_specs=out_specs
        ),
        out_shape=out_shape,
        compiler_params=pltpu.CompilerParams(vmem_limit_bytes=12 * 1024 * 1024),
    )(at, *args)


def at_index(i, ndim):
    return (jnp.asarray(i, jnp.int32),) + (jnp.int32(0),) * (ndim - 1)


def put(buf, piece, i):
    return lax.dynamic_update_slice(buf, piece, at_index(i, buf.ndim))


def take(buf, i):
    return lax.dynamic_slice(buf, at_index(i, buf.ndim), (1,) + buf.shape[1:])[0]


def total(*vs):
    out = vs[0].astype(F32)
    for v in vs[1:]:
        out = out + v.astype(F32)
    return out.astype(BF16)


def body(tokens, expert_ids, route_gates, w_gate, w_up, w_down):
    feats = tokens.shape[1]
    rows = NZ * feats
    ylo, core, x, yhi, z = (lax.axis_index(a).astype(jnp.int32) for a in AXES)
    zh, zl = z // 2, z % 2
    at = jnp.stack([x, 2 * yhi + ylo, core])
    wg, wu, wd = w_gate[0], w_up[0], w_down[0]

    own = tokens.T
    pair = z_pair(own)
    pair = jnp.stack([jnp.where(zl == 0, own, pair), jnp.where(zl == 0, pair, own)])
    start = jnp.zeros((NZ // 2, 2, feats, COLS), BF16)
    for s in range(NZ // 2):
        piece = from_z(pair, 2 * s) if s else pair
        start = put(start, piece[None], (zh + s) % 4)
    start = start.reshape(rows, COLS)

    experts = jnp.arange(4, dtype=jnp.int32)
    mine = jnp.sum(
        jnp.where(expert_ids[None, :, :] == experts[:, None, None], route_gates[None], 0.0), axis=2
    )
    near = jnp.stack([mine, sibling(mine)])
    other = lax.ppermute(near, "ylo", [(0, 1), (1, 0)])
    w = jnp.stack([near, other], axis=1)
    w = lax.dynamic_index_in_dim(w, 2 * ylo + core, axis=2)

    steps = {s: from_minor(start, s) for s in (1, 2, 3)}
    own = [jnp.stack([start, steps[1]]), jnp.stack([steps[2], steps[3]])]
    *own, w = lax.optimization_barrier((*own, w))

    through = [from_major(own[0], 1), from_major(own[1], 3)]
    direct = [from_major(own[1], 1), from_major(own[0], 3)]
    far = [from_major(through[0], 1), from_major(through[1], 3)]
    swap = lambda vs: [sibling(v) for v in vs]
    sums = hidden_of(at, wg, wu, OWN, own, swap(own))
    *near, sums = lax.optimization_barrier((*through, *direct, sums))
    sums = hidden_of(at, wg, wu, THROUGH + DIRECT, near, swap(near), sums)
    *far, sums = lax.optimization_barrier((*far, sums))
    h = hidden_of(at, wg, wu, FAR, far, swap(far), sums, w)

    def after(h, v):
        return lax.optimization_barrier((h, v))

    h, p = after(h, down_of(at, wd, h, FAR))
    got = sibling(p)
    h, give, rest = lax.optimization_barrier((h, down_of(at, wd, h, DIRECT), down_of(at, wd, h, THROUGH + OWN)))
    h, got = after(h, got)
    far = down_of(at, wd, h, FAR, got)
    h, give, rest, *far = lax.optimization_barrier((h, give, rest, *far))
    via = [from_major(far[0], 3), from_major(far[1], 1)]
    h, got = after(h, sibling(give))
    direct = down_of(at, wd, h, DIRECT, got)
    direct = [from_major(direct[0], 3), from_major(direct[1], 1)]
    got = sibling(rest)
    h, *moved = lax.optimization_barrier((h, *via, *direct))
    via, direct = moved[:2], moved[2:]
    h, through = after(h, down_of(at, wd, h, THROUGH, got, 0, via))
    through = [from_major(through[0], 3), from_major(through[1], 1)]
    own = down_of(at, wd, h, OWN, got, 4)
    low = [total(own[0][j], through[0][j], direct[1][j]) for j in range(2)]
    high = [total(own[1][j], direct[0][j], through[1][j]) for j in range(2)]

    c = [*low, *high]
    came = {s: from_minor(c[s], -s) for s in (2, 1, 3)}
    c = total(c[0], came[1], came[3], came[2])

    c = c.reshape(NZ // 2, 2, feats, COLS)
    chunk = lambda s: take(c, (zh + s) % 4)
    c = total(chunk(0), *[from_z(chunk(s), -2 * s) for s in (2, 1, 3)])
    c = total(take(c, zl), z_pair(take(c, 1 - zl)))
    return c.T


def solution(mesh):
    fine = Mesh(mesh.devices.reshape(SIZES), AXES)
    expert, tensor = ("ylo", "core"), ("x", "yhi", "z")
    in_specs = (
        P(expert, tensor),
        P(expert, None),
        P(expert, None),
        P(expert, None, tensor),
        P(expert, None, tensor),
        P(expert, tensor, None),
    )
    return jax.shard_map(
        body, mesh=fine, in_specs=in_specs, out_specs=P(expert, tensor), check_vma=False
    )
```

time: 1120 us -> 172 us (0.15)
  waiting for transfers between devices: 1020 us -> 73.8 us
  starting transfers between devices: 0.04 us -> 50.4 us
  Pallas kernels: 0 us -> 34.6 us
  matrix products: 31.8 us -> 0 us
  local copies, waits for them, and re-layouts: 27.5 us -> 4.02 us
  blocking collectives: 14.8 us -> 0 us
  between operations: 13.4 us -> 0.27 us
    unnamed x3 -> x0, waiting for transfers between devices: 867 us -> none
    all_gather x1 -> x0, waiting for transfers between devices: 155 us -> none  [body(): piece = lax.all_gather(arrived, 'tensor', axis=1, tiled=True)]
    ppermute x0 -> x39, waiting for transfers between devices: none -> 73.8 us  [the longest x12 30.4 us: from_major(): return lax.ppermute(v, AXES, shift_perm(True, s))]
    ppermute x0 -> x39, starting transfers between devices: none -> 50.4 us  [the longest x6 18.8 us: from_z(): return lax.ppermute(v, 'z', [((i + s) % NZ, i) for i in range(NZ)])]
    pallas_call x0 -> x10, Pallas kernels: none -> 34.6 us  [the longest x3 17.4 us: hidden_of(): pl.pallas_call(kernel, grid_spec=pltpu.PrefetchScalarGridSpec(num_scalar_...]
    dot_general x4 -> x0, matrix products: 31.8 us -> none  [the longest x1 21.1 us: body(): lax.dot_general(down_local, hidden, (((0,), (1,)), ((), ())), preferred_e...]
    unnamed x5 -> x10, local copies, waits for them, and re-layouts: 21.4 us -> 3.91 us
    all_to_all x2 -> x0, blocking collectives: 14.8 us -> none  [the longest x1 8.05 us: body(): lax.all_to_all(outcome, 'expert', split_axis=1, concat_axis=1, tiled=True)]
  transfers between devices with their start and end apart: 2 -> 39, of which waited for: 2 -> 24; matrix products, arithmetic and copies ran while one was open for 0% -> 3% of each run, Pallas kernels for 0% -> 14%
where the time goes in v1:
time: 172 us
  waiting for transfers between devices  73.8 us (43%)
  starting transfers between devices  50.4 us (29%)
  Pallas kernels  34.6 us (20%)
  other arithmetic  8.46 us (5%)
  local copies, waits for them, and re-layouts  4.02 us (2%)
    ppermute x12, waiting for transfers between devices, from_major(): return lax.ppermute(v, AXES, shift_perm(True, s))  30.4 us
    ppermute x6, starting transfers between devices, from_z(): return lax.ppermute(v, 'z', [((i + s) % NZ, i) for i in range(NZ)])  18.8 us
    pallas_call x3, Pallas kernels, hidden_of(): pl.pallas_call(kernel, grid_spec=pltpu.PrefetchScalarGridSpec(num_scalar_...  17.4 us
    pallas_call x7, Pallas kernels, down_of(): pl.pallas_call(kernel, grid_spec=pltpu.PrefetchScalarGridSpec(num_scalar_...  17.2 us
    ppermute x12, starting transfers between devices, from_major(): return lax.ppermute(v, AXES, shift_perm(True, s))  14.3 us
    ppermute x6, starting transfers between devices, from_minor(): return lax.ppermute(v, AXES, shift_perm(False, s))  11.4 us
    ppermute x12, waiting for transfers between devices, sibling(): return lax.ppermute(v, 'core', [(0, 1), (1, 0)])  11.2 us
    ppermute x6, waiting for transfers between devices, from_z(): return lax.ppermute(v, 'z', [((i + s) % NZ, i) for i in range(NZ)])  10.7 us
  transfers between devices with their start and end apart: 39, of which 24 were waited for; matrix products, arithmetic and copies ran while one was open for 3% of the time, Pallas kernels for 14%

profile of v1, /device:TPU:30, one launch (start us, length us, event | category | flops | bytes accessed | tf_op | source)
XLA Modules:
  0.0 171.6 jit_solution(13112232350513075888)
XLA Ops:
  1.9 2.4 %collective-permute-done = bf16[96,256]{1,0:T(8,128)(2,1)S(1)} collective-permute-done((bf16[96,256]{1,0:T(8,128)(2,1)}, bf16[96,256]{1,0:T(8,128)(2,1)S(1)}, u32[]{:S(2)}, u32[]{:S(2)}) %collective-permute-start) | collective-permute-done | bytes 49184 | tf_op jit(solution)/shard_map/ppermute | solution.py:46
  5.1 6.4 %collective-permute-start.1 = (bf16[2,96,256]{2,1,0:T(8,128)(2,1)S(1)}, bf16[2,96,256]{2,1,0:T(8,128)(2,1)S(1)}, u32[]{:S(2)}, u32[]{:S(2)}) collective-permute-start(bf16[2,96,256]{2,1,0:T(8,128)(2,1)S(1)} %pad_maximum_fusion.2), channel_id=1, source_target_pairs={{2,0},{3,1},{4,2},{5,3},{6,4},{7,5},{0,6},{1,7},{10,8},{11,9},{12,... | collective-permute-start | bytes 294920 | tf_op jit(solution)/shard_map/ppermute | solution.py:42
  12.5 2.8 %collective-permute-start.3 = (bf16[2,96,256]{2,1,0:T(8,128)(2,1)S(1)}, bf16[2,96,256]{2,1,0:T(8,128)(2,1)S(1)}, u32[]{:S(2)}, u32[]{:S(2)}) collective-permute-start(bf16[2,96,256]{2,1,0:T(8,128)(2,1)S(1)} %pad_maximum_fusion.2), channel_id=1, source_target_pairs={{6,0},{7,1},{0,2},{1,3},{2,4},{3,5},{4,6},{5,7},{14,8},{15,9},{8,1... | collective-permute-start | bytes 294920 | tf_op jit(solution)/shard_map/ppermute | solution.py:42
  15.4 3.4 %collective-permute-done.1 = bf16[2,96,256]{2,1,0:T(8,128)(2,1)S(1)} collective-permute-done((bf16[2,96,256]{2,1,0:T(8,128)(2,1)S(1)}, bf16[2,96,256]{2,1,0:T(8,128)(2,1)S(1)}, u32[]{:S(2)}, u32[]{:S(2)}) %collective-permute-start.1) | collective-permute-done | bytes 98336 | tf_op jit(solution)/shard_map/ppermute | solution.py:42
  18.8 3.3 %collective-permute-done.2 = bf16[2,96,256]{2,1,0:T(8,128)(2,1)S(1)} collective-permute-done((bf16[2,96,256]{2,1,0:T(8,128)(2,1)S(1)}, bf16[2,96,256]{2,1,0:T(8,128)(2,1)S(1)}, u32[]{:S(2)}, u32[]{:S(2)}) %collective-permute-start.2) | collective-permute-done | bytes 98336 | tf_op jit(solution)/shard_map/ppermute | solution.py:42
  23.4 2.2 %collective-permute-start.6 = (bf16[768,256]{1,0:T(8,128)(2,1)S(1)}, bf16[768,256]{1,0:T(8,128)(2,1)}, u32[]{:S(2)}, u32[]{:S(2)}) collective-permute-start(bf16[768,256]{1,0:T(8,128)(2,1)S(1)} %bitcast.81), channel_id=1, source_target_pairs={{136,0},{137,1},{138,2},{139,3},{140,4},{141,5},{142,6},{143,7},{1... | collective-permute-start | bytes 1179656 | tf_op jit(solution)/shard_map/ppermute | solution.py:38
  28.2 5.3 %collective-permute-done.8 = f32[2,4,256]{2,1,0:T(4,128)} collective-permute-done((f32[2,4,256]{2,1,0:T(4,128)}, f32[2,4,256]{2,1,0:T(4,128)}, u32[]{:S(2)}, u32[]{:S(2)}) %collective-permute-start.8) | collective-permute-done | bytes 8224 | tf_op jit(solution)/shard_map/ppermute | solution.py:249
  46.8 5.1 %shard_map.64.refs_13_ = f32[2,2,2,256,256]{4,3,2,1,0:T(8,128)S(1)} custom-call(s32[3]{0:T(128)S(1)} %pad_add_fusion.refs_0_, bf16[6144,256]{1,0:T(8,128)(2,1)S(1)} %bitcast.68, bf16[6144,256]{1,0:T(8,128)(2,1)S(1)} %bitcast.74, bf16[6144,256]{1,0:T(8,128)(2,1)S(1)} %bitcast.69, bf16[6144,256]{1,0:T(8,128)(2,1)S(1)} %bitcast.75, ...), custom_call_target="tpu_custom_call" | custom-call | tf_op jit(solution)/shard_map/pallas_call | solution.py:149
  52.7 6.8 %collective-permute-done.14.refs_8_ = bf16[2,768,256]{2,1,0:T(8,128)(2,1)} collective-permute-done((bf16[2,768,256]{2,1,0:T(8,128)(2,1)}, bf16[2,768,256]{2,1,0:T(8,128)(2,1)}, u32[]{:S(2)}, u32[]{:S(2)}) %collective-permute-start.14) | collective-permute-done | bytes 786464 | tf_op jit(solution)/shard_map/ppermute | solution.py:34
  67.8 8.5 %shard_map.65.refs_9_ = f32[2,2,2,256,256]{4,3,2,1,0:T(8,128)S(1)} custom-call(s32[3]{0:T(128)S(1)} %pad_add_fusion.refs_0_, bf16[6144,256]{1,0:T(8,128)(2,1)S(1)} %bitcast.70, bf16[6144,256]{1,0:T(8,128)(2,1)S(1)} %bitcast.76, bf16[6144,256]{1,0:T(8,128)(2,1)S(1)} %bitcast.71, bf16[6144,256]{1,0:T(8,128)(2,1)S(1)} %bitcast.77, ...), custom_call_target="tpu_custom_call" | custom-call | tf_op jit(solution)/shard_map/pallas_call | solution.py:149
  80.0 3.8 %shard_map.66.refs_2_ = bf16[2,2,256,256]{3,2,1,0:T(8,128)(2,1)S(1)} custom-call(s32[3]{0:T(128)S(1)} %pad_add_fusion.refs_0_, bf16[6144,256]{1,0:T(8,128)(2,1)S(1)} %bitcast.72, bf16[6144,256]{1,0:T(8,128)(2,1)S(1)} %bitcast.78, bf16[6144,256]{1,0:T(8,128)(2,1)S(1)} %bitcast.73, bf16[6144,256]{1,0:T(8,128)(2,1)S(1)} %bitcast.79, ...), custom_call_target="tpu_custom_call" | custom-call | tf_op jit(solution)/shard_map/pallas_call | solution.py:149
  86.2 3.7 %shard_map.69 = bf16[8,768,256]{2,1,0:T(8,128)(2,1)S(1)} custom-call(s32[3]{0:T(128)S(1)} %pad_add_fusion.refs_0_, bf16[256,6144]{1,0:T(8,128)(2,1)S(1)} %bitcast.62, bf16[2,2,256,256]{3,2,1,0:T(8,128)(2,1)S(1)} %shard_map.66.refs_2_), custom_call_target="tpu_custom_call" | custom-call | tf_op jit(solution)/shard_map/pallas_call | solution.py:198
  89.9 2.1 %shard_map.68 = bf16[4,768,256]{2,1,0:T(8,128)(2,1)S(1)} custom-call(s32[3]{0:T(128)S(1)} %pad_add_fusion.refs_0_, bf16[256,6144]{1,0:T(8,128)(2,1)S(1)} %bitcast.63, bf16[2,2,256,256]{3,2,1,0:T(8,128)(2,1)S(1)} %shard_map.66.refs_2_), custom_call_target="tpu_custom_call" | custom-call | tf_op jit(solution)/shard_map/pallas_call | solution.py:198
  92.1 2.2 %shard_map.70 = (bf16[2,768,256]{2,1,0:T(8,128)(2,1)S(1)}, bf16[2,768,256]{2,1,0:T(8,128)(2,1)S(1)}) custom-call(s32[3]{0:T(128)S(1)} %pad_add_fusion.refs_0_, bf16[256,6144]{1,0:T(8,128)(2,1)S(1)} %bitcast.64, bf16[2,2,256,256]{3,2,1,0:T(8,128)(2,1)S(1)} %shard_map.66.refs_2_, bf16[4,768,256]{2,1,0:T(8,128)(2,1)S(1)} %collective-permute-done.23.refs_3_), custom_call_target="tpu_custom_call" | custom-call | tf_op jit(solution)/shard_map/pallas_call | solution.py:198
  94.9 2.8 %collective-permute-start.25 = (bf16[2,768,256]{2,1,0:T(8,128)(2,1)S(1)}, bf16[2,768,256]{2,1,0:T(8,128)(2,1)S(1)}, u32[]{:S(2)}, u32[]{:S(2)}) collective-permute-start(bf16[2,768,256]{2,1,0:T(8,128)(2,1)S(1)} %get-tuple-element.69), channel_id=1, source_target_pairs={{48,0},{49,1},{50,2},{51,3},{52,4},{53,5},{54,6},{55,7},{56,8},{57... | collective-permute-start | bytes 2359304 | tf_op jit(solution)/shard_map/ppermute | solution.py:34
  97.7 4.6 %collective-permute-done.24.refs_3_ = bf16[4,768,256]{2,1,0:T(8,128)(2,1)S(1)} collective-permute-done((bf16[4,768,256]{2,1,0:T(8,128)(2,1)S(1)}, bf16[4,768,256]{2,1,0:T(8,128)(2,1)S(1)}, u32[]{:S(2)}, u32[]{:S(2)}) %collective-permute-start.24) | collective-permute-done | bytes 1572896 | tf_op jit(solution)/shard_map/ppermute | solution.py:50
  102.3 2.3 %shard_map.71 = (bf16[2,768,256]{2,1,0:T(8,128)(2,1)S(1)}, bf16[2,768,256]{2,1,0:T(8,128)(2,1)S(1)}) custom-call(s32[3]{0:T(128)S(1)} %pad_add_fusion.refs_0_, bf16[256,6144]{1,0:T(8,128)(2,1)S(1)} %bitcast.65, bf16[2,2,256,256]{3,2,1,0:T(8,128)(2,1)S(1)} %shard_map.66.refs_2_, bf16[4,768,256]{2,1,0:T(8,128)(2,1)S(1)} %collective-permute-done.24.refs_3_), custom_call_target="tpu_custom_call" | custom-call | tf_op jit(solution)/shard_map/pallas_call | solution.py:198
  104.6 2.9 %collective-permute-start.27 = (bf16[2,768,256]{2,1,0:T(8,128)(2,1)S(1)}, bf16[2,768,256]{2,1,0:T(8,128)(2,1)S(1)}, u32[]{:S(2)}, u32[]{:S(2)}) collective-permute-start(bf16[2,768,256]{2,1,0:T(8,128)(2,1)S(1)} %get-tuple-element.72), channel_id=1, source_target_pairs={{48,0},{49,1},{50,2},{51,3},{52,4},{53,5},{54,6},{55,7},{56,8},{57... | collective-permute-start | bytes 2359304 | tf_op jit(solution)/shard_map/ppermute | solution.py:34
  107.5 3.4 %collective-permute-done.26.refs_5_ = bf16[2,768,256]{2,1,0:T(8,128)(2,1)S(1)} collective-permute-done((bf16[2,768,256]{2,1,0:T(8,128)(2,1)S(1)}, bf16[2,768,256]{2,1,0:T(8,128)(2,1)S(1)}, u32[]{:S(2)}, u32[]{:S(2)}) %collective-permute-start.26) | collective-permute-done | bytes 786464 | tf_op jit(solution)/shard_map/ppermute | solution.py:34
  110.9 6.1 %collective-permute-done.27 = bf16[2,768,256]{2,1,0:T(8,128)(2,1)S(1)} collective-permute-done((bf16[2,768,256]{2,1,0:T(8,128)(2,1)S(1)}, bf16[2,768,256]{2,1,0:T(8,128)(2,1)S(1)}, u32[]{:S(2)}, u32[]{:S(2)}) %collective-permute-start.27) | collective-permute-done | bytes 786464 | tf_op jit(solution)/shard_map/ppermute | solution.py:34
  117.0 3.7 %collective-permute-done.28 = bf16[2,768,256]{2,1,0:T(8,128)(2,1)S(1)} collective-permute-done((bf16[2,768,256]{2,1,0:T(8,128)(2,1)S(1)}, bf16[2,768,256]{2,1,0:T(8,128)(2,1)S(1)}, u32[]{:S(2)}, u32[]{:S(2)}) %collective-permute-start.28) | collective-permute-done | bytes 786464 | tf_op jit(solution)/shard_map/ppermute | solution.py:34
  120.7 2.5 %shard_map.72 = (bf16[2,768,256]{2,1,0:T(8,128)(2,1)S(1)}, bf16[2,768,256]{2,1,0:T(8,128)(2,1)S(1)}) custom-call(s32[3]{0:T(128)S(1)} %pad_add_fusion.refs_0_, bf16[256,6144]{1,0:T(8,128)(2,1)S(1)} %bitcast.66, bf16[2,2,256,256]{3,2,1,0:T(8,128)(2,1)S(1)} %shard_map.66.refs_2_, bf16[8,768,256]{2,1,0:T(8,128)(2,1)S(1)} %collective-permute-done.29.refs_3_, ...), custom_call_target="tpu_custom_call" | custom-call | tf_op jit(solution)/shard_map/pallas_call | solution.py:198
  125.3 2.2 %shard_map.73 = (bf16[2,768,256]{2,1,0:T(8,128)(2,1)S(1)}, bf16[2,768,256]{2,1,0:T(8,128)(2,1)S(1)}) custom-call(s32[3]{0:T(128)S(1)} %pad_add_fusion.refs_0_, bf16[256,6144]{1,0:T(8,128)(2,1)S(1)} %bitcast.67, bf16[2,2,256,256]{3,2,1,0:T(8,128)(2,1)S(1)} %shard_map.66.refs_2_, bf16[8,768,256]{2,1,0:T(8,128)(2,1)S(1)} %collective-permute-done.29.refs_3_), custom_call_target="tpu_custom_call" | custom-call | tf_op jit(solution)/shard_map/pallas_call | solution.py:198
  127.6 7.7 %collective-permute-done.30 = bf16[2,768,256]{2,1,0:T(8,128)(2,1)S(1)} collective-permute-done((bf16[2,768,256]{2,1,0:T(8,128)(2,1)S(1)}, bf16[2,768,256]{2,1,0:T(8,128)(2,1)S(1)}, u32[]{:S(2)}, u32[]{:S(2)}) %collective-permute-start.30) | collective-permute-done | bytes 786464 | tf_op jit(solution)/shard_map/ppermute | solution.py:34
  135.5 2.3 %collective-permute-start.31 = (bf16[768,256]{1,0:T(8,128)(2,1)S(1)}, bf16[768,256]{1,0:T(8,128)(2,1)S(1)}, u32[]{:S(2)}, u32[]{:S(2)}) collective-permute-start(bf16[768,256]{1,0:T(8,128)(2,1)S(1)} %fusion.4), channel_id=1, source_target_pairs={{136,0},{137,1},{138,2},{139,3},{140,4},{141,5},{142,6},{143,7},{1... | collective-permute-start | bytes 1179656 | tf_op jit(solution)/shard_map/ppermute | solution.py:38
  138.6 5.1 %collective-permute-start.34 = (bf16[768,256]{1,0:T(8,128)(2,1)S(1)}, bf16[768,256]{1,0:T(8,128)(2,1)S(1)}, u32[]{:S(2)}, u32[]{:S(2)}) collective-permute-start(bf16[768,256]{1,0:T(8,128)(2,1)S(1)} %get-tuple-element.88), channel_id=1, source_target_pairs={{8,0},{9,1},{10,2},{11,3},{12,4},{13,5},{14,6},{15,7},{0,8},{1,9},... | collective-permute-start | bytes 1179656 | tf_op jit(solution)/shard_map/ppermute | solution.py:38
  143.9 4.1 %collective-permute-done.33 = bf16[768,256]{1,0:T(8,128)(2,1)S(1)} collective-permute-done((bf16[768,256]{1,0:T(8,128)(2,1)S(1)}, bf16[768,256]{1,0:T(8,128)(2,1)S(1)}, u32[]{:S(2)}, u32[]{:S(2)}) %collective-permute-start.33) | collective-permute-done | bytes 393248 | tf_op jit(solution)/shard_map/ppermute | solution.py:38
  148.0 5.7 %collective-permute-done.34 = bf16[768,256]{1,0:T(8,128)(2,1)S(1)} collective-permute-done((bf16[768,256]{1,0:T(8,128)(2,1)S(1)}, bf16[768,256]{1,0:T(8,128)(2,1)S(1)}, u32[]{:S(2)}, u32[]{:S(2)}) %collective-permute-start.34) | collective-permute-done | bytes 393248 | tf_op jit(solution)/shard_map/ppermute | solution.py:38
  154.0 4.5 %collective-permute-start.35 = (bf16[2,96,256]{2,1,0:T(8,128)(2,1)S(1)}, bf16[2,96,256]{2,1,0:T(8,128)(2,1)S(1)}, u32[]{:S(2)}, u32[]{:S(2)}) collective-permute-start(bf16[2,96,256]{2,1,0:T(8,128)(2,1)S(1)} %get-tuple-element.89), channel_id=1, source_target_pairs={{4,0},{5,1},{6,2},{7,3},{0,4},{1,5},{2,6},{3,7},{12,8},{13,9},{14,... | collective-permute-start | bytes 294920 | tf_op jit(solution)/shard_map/ppermute | solution.py:42
  158.6 4.0 %collective-permute-start.37 = (bf16[2,96,256]{2,1,0:T(8,128)(2,1)S(1)}, bf16[2,96,256]{2,1,0:T(8,128)(2,1)S(1)}, u32[]{:S(2)}, u32[]{:S(2)}) collective-permute-start(bf16[2,96,256]{2,1,0:T(8,128)(2,1)S(1)} %get-tuple-element.90), channel_id=1, source_target_pairs={{2,0},{3,1},{4,2},{5,3},{6,4},{7,5},{0,6},{1,7},{10,8},{11,9},{12,... | collective-permute-start | bytes 294920 | tf_op jit(solution)/shard_map/ppermute | solution.py:42
  162.6 4.1 %collective-permute-done.36 = bf16[2,96,256]{2,1,0:T(8,128)(2,1)S(1)} collective-permute-done((bf16[2,96,256]{2,1,0:T(8,128)(2,1)S(1)}, bf16[2,96,256]{2,1,0:T(8,128)(2,1)S(1)}, u32[]{:S(2)}, u32[]{:S(2)}) %collective-permute-start.36) | collective-permute-done | bytes 98336 | tf_op jit(solution)/shard_map/ppermute | solution.py:42
  167.0 4.0 %collective-permute-done.38 = bf16[96,256]{1,0:T(8,128)(2,1)S(1)} collective-permute-done((bf16[96,256]{1,0:T(8,128)(2,1)S(1)}, bf16[96,256]{1,0:T(8,128)(2,1)S(1)}, u32[]{:S(2)}, u32[]{:S(2)}) %collective-permute-start.38) | collective-permute-done | bytes 49184 | tf_op jit(solution)/shard_map/ppermute | solution.py:46
  (86 shorter events, 41.5 us)
Async XLA Ops:
  0.0 4.3 %collective-permute-start = (bf16[96,256]{1,0:T(8,128)(2,1)}, bf16[96,256]{1,0:T(8,128)(2,1)S(1)}, u32[]{:S(2)}, u32[]{:S(2)}) collective-permute-start(bf16[96,256]{1,0:T(8,128)(2,1)} %bitcast.86), channel_id=1, source_target_pairs={{0,1},{1,0},{2,3},{3,2},{4,5},{5,4},{6,7},{7,6},{8,9},{9,8},{10,11... | collective-permute-start | bytes 147464 | tf_op jit(solution)/shard_map/ppermute | solution.py:46
  5.1 13.6 %collective-permute-start.1 = (bf16[2,96,256]{2,1,0:T(8,128)(2,1)S(1)}, bf16[2,96,256]{2,1,0:T(8,128)(2,1)S(1)}, u32[]{:S(2)}, u32[]{:S(2)}) collective-permute-start(bf16[2,96,256]{2,1,0:T(8,128)(2,1)S(1)} %pad_maximum_fusion.2), channel_id=1, source_target_pairs={{2,0},{3,1},{4,2},{5,3},{6,4},{7,5},{0,6},{1,7},{10,8},{11,9},{12,... | collective-permute-start | bytes 294920 | tf_op jit(solution)/shard_map/ppermute | solution.py:42
  11.5 10.5 %collective-permute-start.2 = (bf16[2,96,256]{2,1,0:T(8,128)(2,1)S(1)}, bf16[2,96,256]{2,1,0:T(8,128)(2,1)S(1)}, u32[]{:S(2)}, u32[]{:S(2)}) collective-permute-start(bf16[2,96,256]{2,1,0:T(8,128)(2,1)S(1)} %pad_maximum_fusion.2), channel_id=1, source_target_pairs={{4,0},{5,1},{6,2},{7,3},{0,4},{1,5},{2,6},{3,7},{12,8},{13,9},{14,... | collective-permute-start | bytes 294920 | tf_op jit(solution)/shard_map/ppermute | solution.py:42
  12.5 9.5 %collective-permute-start.3 = (bf16[2,96,256]{2,1,0:T(8,128)(2,1)S(1)}, bf16[2,96,256]{2,1,0:T(8,128)(2,1)S(1)}, u32[]{:S(2)}, u32[]{:S(2)}) collective-permute-start(bf16[2,96,256]{2,1,0:T(8,128)(2,1)S(1)} %pad_maximum_fusion.2), channel_id=1, source_target_pairs={{6,0},{7,1},{0,2},{1,3},{2,4},{3,5},{4,6},{5,7},{14,8},{15,9},{8,1... | collective-permute-start | bytes 294920 | tf_op jit(solution)/shard_map/ppermute | solution.py:42
  22.1 12.1 %collective-permute-start.5 = (bf16[768,256]{1,0:T(8,128)(2,1)S(1)}, bf16[768,256]{1,0:T(8,128)(2,1)}, u32[]{:S(2)}, u32[]{:S(2)}) collective-permute-start(bf16[768,256]{1,0:T(8,128)(2,1)S(1)} %bitcast.80), channel_id=1, source_target_pairs={{8,0},{9,1},{10,2},{11,3},{12,4},{13,5},{14,6},{15,7},{0,8},{1,9},... | collective-permute-start | bytes 1179656 | tf_op jit(solution)/shard_map/ppermute | solution.py:38
  23.4 10.8 %collective-permute-start.6 = (bf16[768,256]{1,0:T(8,128)(2,1)S(1)}, bf16[768,256]{1,0:T(8,128)(2,1)}, u32[]{:S(2)}, u32[]{:S(2)}) collective-permute-start(bf16[768,256]{1,0:T(8,128)(2,1)S(1)} %bitcast.81), channel_id=1, source_target_pairs={{136,0},{137,1},{138,2},{139,3},{140,4},{141,5},{142,6},{143,7},{1... | collective-permute-start | bytes 1179656 | tf_op jit(solution)/shard_map/ppermute | solution.py:38
  25.6 10.7 %collective-permute-start.4 = (bf16[768,256]{1,0:T(8,128)(2,1)S(1)}, bf16[768,256]{1,0:T(8,128)(2,1)}, u32[]{:S(2)}, u32[]{:S(2)}) collective-permute-start(bf16[768,256]{1,0:T(8,128)(2,1)S(1)} %bitcast.82), channel_id=1, source_target_pairs={{128,0},{129,1},{130,2},{131,3},{132,4},{133,5},{134,6},{135,7},{1... | collective-permute-start | bytes 1179656 | tf_op jit(solution)/shard_map/ppermute | solution.py:38
  28.2 5.3 %collective-permute-start.8 = (f32[2,4,256]{2,1,0:T(4,128)}, f32[2,4,256]{2,1,0:T(4,128)}, u32[]{:S(2)}, u32[]{:S(2)}) collective-permute-start(f32[2,4,256]{2,1,0:T(4,128)} %get-tuple-element.94), channel_id=1, source_target_pairs={{0,128},{128,0},{1,129},{129,1},{2,130},{130,2},{3,131},{131,3},{4... | collective-permute-start | bytes 24584 | tf_op jit(solution)/shard_map/ppermute | solution.py:249
  38.3 5.5 %collective-permute-start.16 = (bf16[2,768,256]{2,1,0:T(8,128)(2,1)}, bf16[2,768,256]{2,1,0:T(8,128)(2,1)}, u32[]{:S(2)}, u32[]{:S(2)}) collective-permute-start(bf16[2,768,256]{2,1,0:T(8,128)(2,1)} %pad_maximum_fusion.1.refs_6_), channel_id=1, source_target_pairs={{0,64},{64,0},{1,65},{65,1},{2,66},{66,2},{3,67},{67,3},{4,68},{68... | collective-permute-start | bytes 2359304 | tf_op jit(solution)/shard_map/ppermute | solution.py:50
  38.8 13.1 %collective-permute-start.11 = (bf16[2,768,256]{2,1,0:T(8,128)(2,1)}, bf16[2,768,256]{2,1,0:T(8,128)(2,1)}, u32[]{:S(2)}, u32[]{:S(2)}) collective-permute-start(bf16[2,768,256]{2,1,0:T(8,128)(2,1)} %pad_maximum_fusion.1.refs_6_), channel_id=1, source_target_pairs={{48,0},{49,1},{50,2},{51,3},{52,4},{53,5},{54,6},{55,7},{56,8},{57... | collective-permute-start | bytes 2359304 | tf_op jit(solution)/shard_map/ppermute | solution.py:34
  39.2 13.5 %collective-permute-start.13 = (bf16[2,768,256]{2,1,0:T(8,128)(2,1)}, bf16[2,768,256]{2,1,0:T(8,128)(2,1)}, u32[]{:S(2)}, u32[]{:S(2)}) collective-permute-start(bf16[2,768,256]{2,1,0:T(8,128)(2,1)} %pad_maximum_fusion.1.refs_6_), channel_id=1, source_target_pairs={{16,0},{17,1},{18,2},{19,3},{20,4},{21,5},{22,6},{23,7},{24,8},{25... | collective-permute-start | bytes 2359304 | tf_op jit(solution)/shard_map/ppermute | solution.py:34
  40.8 18.7 %collective-permute-start.14 = (bf16[2,768,256]{2,1,0:T(8,128)(2,1)}, bf16[2,768,256]{2,1,0:T(8,128)(2,1)}, u32[]{:S(2)}, u32[]{:S(2)}) collective-permute-start(bf16[2,768,256]{2,1,0:T(8,128)(2,1)} %pad_maximum_fusion.refs_5_), channel_id=1, source_target_pairs={{48,0},{49,1},{50,2},{51,3},{52,4},{53,5},{54,6},{55,7},{56,8},{57... | collective-permute-start | bytes 2359304 | tf_op jit(solution)/shard_map/ppermute | solution.py:34
  43.3 17.8 %collective-permute-start.9 = (bf16[2,768,256]{2,1,0:T(8,128)(2,1)}, bf16[2,768,256]{2,1,0:T(8,128)(2,1)}, u32[]{:S(2)}, u32[]{:S(2)}) collective-permute-start(bf16[2,768,256]{2,1,0:T(8,128)(2,1)} %pad_maximum_fusion.refs_5_), channel_id=1, source_target_pairs={{16,0},{17,1},{18,2},{19,3},{20,4},{21,5},{22,6},{23,7},{24,8},{25... | collective-permute-start | bytes 2359304 | tf_op jit(solution)/shard_map/ppermute | solution.py:34
  62.3 4.4 %collective-permute-start.19 = (bf16[2,768,256]{2,1,0:T(8,128)(2,1)}, bf16[2,768,256]{2,1,0:T(8,128)(2,1)S(1)}, u32[]{:S(2)}, u32[]{:S(2)}) collective-permute-start(bf16[2,768,256]{2,1,0:T(8,128)(2,1)} %collective-permute-done.13.refs_7_), channel_id=1, source_target_pairs={{0,64},{64,0},{1,65},{65,1},{2,66},{66,2},{3,67},{67,3},{4,68},{68... | collective-permute-start | bytes 2359304 | tf_op jit(solution)/shard_map/ppermute | solution.py:50
  62.8 5.0 %collective-permute-start.20 = (bf16[2,768,256]{2,1,0:T(8,128)(2,1)}, bf16[2,768,256]{2,1,0:T(8,128)(2,1)S(1)}, u32[]{:S(2)}, u32[]{:S(2)}) collective-permute-start(bf16[2,768,256]{2,1,0:T(8,128)(2,1)} %collective-permute-done.14.refs_8_), channel_id=1, source_target_pairs={{0,64},{64,0},{1,65},{65,1},{2,66},{66,2},{3,67},{67,3},{4,68},{68... | collective-permute-start | bytes 2359304 | tf_op jit(solution)/shard_map/ppermute | solution.py:50
  62.8 13.5 %collective-permute-start.10 = (bf16[2,768,256]{2,1,0:T(8,128)(2,1)}, bf16[2,768,256]{2,1,0:T(8,128)(2,1)S(1)}, u32[]{:S(2)}, u32[]{:S(2)}) collective-permute-start(bf16[2,768,256]{2,1,0:T(8,128)(2,1)} %collective-permute-done.9.refs_5_), channel_id=1, source_target_pairs={{16,0},{17,1},{18,2},{19,3},{20,4},{21,5},{22,6},{23,7},{24,8},{25... | collective-permute-start | bytes 2359304 | tf_op jit(solution)/shard_map/ppermute | solution.py:34
  64.4 12.2 %collective-permute-start.12 = (bf16[2,768,256]{2,1,0:T(8,128)(2,1)}, bf16[2,768,256]{2,1,0:T(8,128)(2,1)S(1)}, u32[]{:S(2)}, u32[]{:S(2)}) collective-permute-start(bf16[2,768,256]{2,1,0:T(8,128)(2,1)} %collective-permute-done.11.refs_6_), channel_id=1, source_target_pairs={{48,0},{49,1},{50,2},{51,3},{52,4},{53,5},{54,6},{55,7},{56,8},{57... | collective-permute-start | bytes 2359304 | tf_op jit(solution)/shard_map/ppermute | solution.py:34
  86.0 6.1 %collective-permute-start.23 = (bf16[4,768,256]{2,1,0:T(8,128)(2,1)S(1)}, bf16[4,768,256]{2,1,0:T(8,128)(2,1)S(1)}, u32[]{:S(2)}, u32[]{:S(2)}) collective-permute-start(bf16[4,768,256]{2,1,0:T(8,128)(2,1)S(1)} %shard_map.67), channel_id=1, source_target_pairs={{0,64},{64,0},{1,65},{65,1},{2,66},{66,2},{3,67},{67,3},{4,68},{68... | collective-permute-start | bytes 4718600 | tf_op jit(solution)/shard_map/ppermute | solution.py:50
  94.3 26.4 %collective-permute-start.29 = (bf16[8,768,256]{2,1,0:T(8,128)(2,1)S(1)}, bf16[8,768,256]{2,1,0:T(8,128)(2,1)S(1)}, u32[]{:S(2)}, u32[]{:S(2)}) collective-permute-start(bf16[8,768,256]{2,1,0:T(8,128)(2,1)S(1)} %shard_map.69), channel_id=1, source_target_pairs={{0,64},{64,0},{1,65},{65,1},{2,66},{66,2},{3,67},{67,3},{4,68},{68... | collective-permute-start | bytes 9437192 | tf_op jit(solution)/shard_map/ppermute | solution.py:50
  94.7 7.6 %collective-permute-start.24 = (bf16[4,768,256]{2,1,0:T(8,128)(2,1)S(1)}, bf16[4,768,256]{2,1,0:T(8,128)(2,1)S(1)}, u32[]{:S(2)}, u32[]{:S(2)}) collective-permute-start(bf16[4,768,256]{2,1,0:T(8,128)(2,1)S(1)} %shard_map.68), channel_id=1, source_target_pairs={{0,64},{64,0},{1,65},{65,1},{2,66},{66,2},{3,67},{67,3},{4,68},{68... | collective-permute-start | bytes 4718600 | tf_op jit(solution)/shard_map/ppermute | solution.py:50
  94.9 12.6 %collective-permute-start.25 = (bf16[2,768,256]{2,1,0:T(8,128)(2,1)S(1)}, bf16[2,768,256]{2,1,0:T(8,128)(2,1)S(1)}, u32[]{:S(2)}, u32[]{:S(2)}) collective-permute-start(bf16[2,768,256]{2,1,0:T(8,128)(2,1)S(1)} %get-tuple-element.69), channel_id=1, source_target_pairs={{48,0},{49,1},{50,2},{51,3},{52,4},{53,5},{54,6},{55,7},{56,8},{57... | collective-permute-start | bytes 2359304 | tf_op jit(solution)/shard_map/ppermute | solution.py:34
  97.7 13.2 %collective-permute-start.26 = (bf16[2,768,256]{2,1,0:T(8,128)(2,1)S(1)}, bf16[2,768,256]{2,1,0:T(8,128)(2,1)S(1)}, u32[]{:S(2)}, u32[]{:S(2)}) collective-permute-start(bf16[2,768,256]{2,1,0:T(8,128)(2,1)S(1)} %get-tuple-element.70), channel_id=1, source_target_pairs={{16,0},{17,1},{18,2},{19,3},{20,4},{21,5},{22,6},{23,7},{24,8},{25... | collective-permute-start | bytes 2359304 | tf_op jit(solution)/shard_map/ppermute | solution.py:34
  104.6 12.4 %collective-permute-start.27 = (bf16[2,768,256]{2,1,0:T(8,128)(2,1)S(1)}, bf16[2,768,256]{2,1,0:T(8,128)(2,1)S(1)}, u32[]{:S(2)}, u32[]{:S(2)}) collective-permute-start(bf16[2,768,256]{2,1,0:T(8,128)(2,1)S(1)} %get-tuple-element.72), channel_id=1, source_target_pairs={{48,0},{49,1},{50,2},{51,3},{52,4},{53,5},{54,6},{55,7},{56,8},{57... | collective-permute-start | bytes 2359304 | tf_op jit(solution)/shard_map/ppermute | solution.py:34
  107.5 13.2 %collective-permute-start.28 = (bf16[2,768,256]{2,1,0:T(8,128)(2,1)S(1)}, bf16[2,768,256]{2,1,0:T(8,128)(2,1)S(1)}, u32[]{:S(2)}, u32[]{:S(2)}) collective-permute-start(bf16[2,768,256]{2,1,0:T(8,128)(2,1)S(1)} %get-tuple-element.73), channel_id=1, source_target_pairs={{16,0},{17,1},{18,2},{19,3},{20,4},{21,5},{22,6},{23,7},{24,8},{25... | collective-permute-start | bytes 2359304 | tf_op jit(solution)/shard_map/ppermute | solution.py:34
  123.2 12.1 %collective-permute-start.30 = (bf16[2,768,256]{2,1,0:T(8,128)(2,1)S(1)}, bf16[2,768,256]{2,1,0:T(8,128)(2,1)S(1)}, u32[]{:S(2)}, u32[]{:S(2)}) collective-permute-start(bf16[2,768,256]{2,1,0:T(8,128)(2,1)S(1)} %get-tuple-element.82), channel_id=1, source_target_pairs={{48,0},{49,1},{50,2},{51,3},{52,4},{53,5},{54,6},{55,7},{56,8},{57... | collective-permute-start | bytes 2359304 | tf_op jit(solution)/shard_map/ppermute | solution.py:34
  123.3 14.4 %collective-permute-start.32 = (bf16[2,768,256]{2,1,0:T(8,128)(2,1)S(1)}, bf16[2,768,256]{2,1,0:T(8,128)(2,1)S(1)}, u32[]{:S(2)}, u32[]{:S(2)}) collective-permute-start(bf16[2,768,256]{2,1,0:T(8,128)(2,1)S(1)} %get-tuple-element.86), channel_id=1, source_target_pairs={{16,0},{17,1},{18,2},{19,3},{20,4},{21,5},{22,6},{23,7},{24,8},{25... | collective-permute-start | bytes 2359304 | tf_op jit(solution)/shard_map/ppermute | solution.py:34
  135.5 8.5 %collective-permute-start.31 = (bf16[768,256]{1,0:T(8,128)(2,1)S(1)}, bf16[768,256]{1,0:T(8,128)(2,1)S(1)}, u32[]{:S(2)}, u32[]{:S(2)}) collective-permute-start(bf16[768,256]{1,0:T(8,128)(2,1)S(1)} %fusion.4), channel_id=1, source_target_pairs={{136,0},{137,1},{138,2},{139,3},{140,4},{141,5},{142,6},{143,7},{1... | collective-permute-start | bytes 1179656 | tf_op jit(solution)/shard_map/ppermute | solution.py:38
  138.0 10.0 %collective-permute-start.33 = (bf16[768,256]{1,0:T(8,128)(2,1)S(1)}, bf16[768,256]{1,0:T(8,128)(2,1)S(1)}, u32[]{:S(2)}, u32[]{:S(2)}) collective-permute-start(bf16[768,256]{1,0:T(8,128)(2,1)S(1)} %get-tuple-element.87), channel_id=1, source_target_pairs={{128,0},{129,1},{130,2},{131,3},{132,4},{133,5},{134,6},{135,7},{1... | collective-permute-start | bytes 1179656 | tf_op jit(solution)/shard_map/ppermute | solution.py:38
  138.6 15.1 %collective-permute-start.34 = (bf16[768,256]{1,0:T(8,128)(2,1)S(1)}, bf16[768,256]{1,0:T(8,128)(2,1)S(1)}, u32[]{:S(2)}, u32[]{:S(2)}) collective-permute-start(bf16[768,256]{1,0:T(8,128)(2,1)S(1)} %get-tuple-element.88), channel_id=1, source_target_pairs={{8,0},{9,1},{10,2},{11,3},{12,4},{13,5},{14,6},{15,7},{0,8},{1,9},... | collective-permute-start | bytes 1179656 | tf_op jit(solution)/shard_map/ppermute | solution.py:38
  154.0 8.6 %collective-permute-start.35 = (bf16[2,96,256]{2,1,0:T(8,128)(2,1)S(1)}, bf16[2,96,256]{2,1,0:T(8,128)(2,1)S(1)}, u32[]{:S(2)}, u32[]{:S(2)}) collective-permute-start(bf16[2,96,256]{2,1,0:T(8,128)(2,1)S(1)} %get-tuple-element.89), channel_id=1, source_target_pairs={{4,0},{5,1},{6,2},{7,3},{0,4},{1,5},{2,6},{3,7},{12,8},{13,9},{14,... | collective-permute-start | bytes 294920 | tf_op jit(solution)/shard_map/ppermute | solution.py:42
  158.5 8.2 %collective-permute-start.36 = (bf16[2,96,256]{2,1,0:T(8,128)(2,1)S(1)}, bf16[2,96,256]{2,1,0:T(8,128)(2,1)S(1)}, u32[]{:S(2)}, u32[]{:S(2)}) collective-permute-start(bf16[2,96,256]{2,1,0:T(8,128)(2,1)S(1)} %get-tuple-element.91), channel_id=1, source_target_pairs={{6,0},{7,1},{0,2},{1,3},{2,4},{3,5},{4,6},{5,7},{14,8},{15,9},{8,1... | collective-permute-start | bytes 294920 | tf_op jit(solution)/shard_map/ppermute | solution.py:42
  158.6 8.1 %collective-permute-start.37 = (bf16[2,96,256]{2,1,0:T(8,128)(2,1)S(1)}, bf16[2,96,256]{2,1,0:T(8,128)(2,1)S(1)}, u32[]{:S(2)}, u32[]{:S(2)}) collective-permute-start(bf16[2,96,256]{2,1,0:T(8,128)(2,1)S(1)} %get-tuple-element.90), channel_id=1, source_target_pairs={{2,0},{3,1},{4,2},{5,3},{6,4},{7,5},{0,6},{1,7},{10,8},{11,9},{12,... | collective-permute-start | bytes 294920 | tf_op jit(solution)/shard_map/ppermute | solution.py:42
  (12 other events, 58.3 us)

commit v2 on v1

--- a/solution.py
+++ b/solution.py
@@ -160,19 +160,28 @@
     )(at, *args)
 
 
-def down_kernel(keep, at, wd_ref, h_ref, *refs):
+def down_kernel(keep, via_n, at, wd_ref, h_ref, *refs):
     t = pl.program_id(0)
     o = dot_t(wd_ref[...], h_ref[0, 0])
     if not keep:
         refs[0][0] = o.astype(BF16)
         return
     o = o + refs[0][0].astype(F32)
-    via, outs = refs[1:-2], refs[-2:]
-    for k, ref in enumerate(outs):
+    if via_n:
+        via, outs = refs[1 : 1 + via_n], refs[1 + via_n :]
+        o = o + jnp.where(t < 2, via[0][0], via[1][0]).astype(F32)
+        for k, ref in enumerate(outs):
+
+            @pl.when(t == k)
+            def _(ref=ref):
+                ref[0] = o.astype(BF16)
+
+        return
+    for k, ref in enumerate(refs[1:]):
 
         @pl.when(lax.div(t, 2) == k)
-        def _(k=k, ref=ref):
-            ref[0] = (o + via[k][0].astype(F32) if via else o).astype(BF16)
+        def _(ref=ref):
+            ref[0] = o.astype(BF16)
 
 
 def down_of(at, wd, h, blocks, got=None, first=0, via=()):
@@ -191,9 +200,12 @@
         in_specs += [whole, *half_specs(rows, len(via))]
         args += [got, *via]
         out_specs, out_shape = half_specs(rows, 2), [jax.ShapeDtypeStruct((2, rows, COLS), BF16)] * 2
+        if via:
+            out_specs = [pl.BlockSpec((1, rows, COLS), lambda t, at: (0, 0, 0))] * 4
+            out_shape = [jax.ShapeDtypeStruct((1, rows, COLS), BF16)] * 4
 
     def kernel(*refs):
-        down_kernel(got is not None, *refs)
+        down_kernel(got is not None, len(via), *refs)
 
     return pl.pallas_call(
         kernel,
@@ -205,6 +217,21 @@
     )(at, *args)
 
 
+def join_kernel(a, b, c, d, low, high):
+    for out, pair in ((low, (a, b)), (high, (c, d))):
+        for i, v in enumerate(pair):
+            out[i] = v[...]
+
+
+def join(*pieces):
+    out = jax.ShapeDtypeStruct((2, *pieces[0].shape), BF16)
+    return pl.pallas_call(
+        join_kernel,
+        out_shape=[out, out],
+        compiler_params=pltpu.CompilerParams(vmem_limit_bytes=10 * 1024 * 1024),
+    )(*pieces)
+
+
 def at_index(i, ndim):
     return (jnp.asarray(i, jnp.int32),) + (jnp.int32(0),) * (ndim - 1)
 
@@ -251,7 +278,7 @@
     w = lax.dynamic_index_in_dim(w, 2 * ylo + core, axis=2)
 
     steps = {s: from_minor(start, s) for s in (1, 2, 3)}
-    own = [jnp.stack([start, steps[1]]), jnp.stack([steps[2], steps[3]])]
+    own = join(start, steps[1], steps[2], steps[3])
     *own, w = lax.optimization_barrier((*own, w))
 
     through = [from_major(own[0], 1), from_major(own[1], 3)]
@@ -278,13 +305,11 @@
     direct = down_of(at, wd, h, DIRECT, got)
     direct = [from_major(direct[0], 3), from_major(direct[1], 1)]
     got = sibling(rest)
-    h, *moved = lax.optimization_barrier((h, *via, *direct))
-    via, direct = moved[:2], moved[2:]
     h, through = after(h, down_of(at, wd, h, THROUGH, got, 0, via))
-    through = [from_major(through[0], 3), from_major(through[1], 1)]
+    through = [from_major(v, s) for v, s in zip(through, (3, 3, 1, 1))]
     own = down_of(at, wd, h, OWN, got, 4)
-    low = [total(own[0][j], through[0][j], direct[1][j]) for j in range(2)]
-    high = [total(own[1][j], direct[0][j], through[1][j]) for j in range(2)]
+    low = [total(own[0][j], through[j][0], direct[1][j]) for j in range(2)]
+    high = [total(own[1][j], direct[0][j], through[2 + j][0]) for j in range(2)]
 
     c = [*low, *high]
     came = {s: from_minor(c[s], -s) for s in (2, 1, 3)}

time: 172 us -> 162 us (0.942)
  waiting for transfers between devices: 73.8 us -> 66.1 us
  other arithmetic: 8.46 us -> 4.46 us
  Pallas kernels: 34.6 us -> 37 us
    ppermute x12 -> x14, waiting for transfers between devices: 30.4 us -> 19.2 us  [from_major(): return lax.ppermute(v, AXES, shift_perm(True, s))]
    another operation x2 -> x0, other arithmetic: 4.04 us -> none  [body(): own = [jnp.stack([start, steps[1]]), jnp.stack([steps[2], steps[3]])]]
    ppermute x6, starting transfers between devices: 11.4 us -> 8.8 us  [from_minor(): return lax.ppermute(v, AXES, shift_perm(False, s))]
    pallas_call x0 -> x1, Pallas kernels: none -> 2.46 us  [join(): pl.pallas_call(join_kernel, out_shape=[out, out], compiler_params=pltpu.C...]
    ppermute x1, waiting for transfers between devices: 5.26 us -> 7.72 us  [body(): other = lax.ppermute(near, 'ylo', [(0, 1), (1, 0)])]
    ppermute x12 -> x14, starting transfers between devices: 14.3 us -> 16.2 us  [from_major(): return lax.ppermute(v, AXES, shift_perm(True, s))]
  transfers between devices with their start and end apart: 39 -> 41, of which waited for: 24 -> 25; matrix products, arithmetic and copies ran while one was open for 3% -> 2% of each run, Pallas kernels for 14% -> 16%
where the time goes in v2:
time: 162 us; the launch traced here: 161 us
  waiting for transfers between devices  66.1 us (41%)
  starting transfers between devices  49.2 us (30%)
  Pallas kernels  37 us (23%)
  other arithmetic  4.46 us (3%)
  local copies, waits for them, and re-layouts  4.01 us (2%)
    ppermute x14, waiting for transfers between devices, from_major(): return lax.ppermute(v, AXES, shift_perm(True, s))  19.2 us
    ppermute x6, starting transfers between devices, from_z(): return lax.ppermute(v, 'z', [((i + s) % NZ, i) for i in range(NZ)])  18.8 us
    pallas_call x3, Pallas kernels, hidden_of(): pl.pallas_call(kernel, grid_spec=pltpu.PrefetchScalarGridSpec(num_scalar_...  17.4 us
    pallas_call x7, Pallas kernels, down_of(): pl.pallas_call(kernel, grid_spec=pltpu.PrefetchScalarGridSpec(num_scalar_...  17.1 us
    ppermute x14, starting transfers between devices, from_major(): return lax.ppermute(v, AXES, shift_perm(True, s))  16.2 us
    ppermute x6, waiting for transfers between devices, from_z(): return lax.ppermute(v, 'z', [((i + s) % NZ, i) for i in range(NZ)])  11.6 us
    ppermute x12, waiting for transfers between devices, sibling(): return lax.ppermute(v, 'core', [(0, 1), (1, 0)])  11.3 us
    ppermute x6, waiting for transfers between devices, from_minor(): return lax.ppermute(v, AXES, shift_perm(False, s))  10.1 us
  transfers between devices with their start and end apart: 41, of which 25 were waited for; matrix products, arithmetic and copies ran while one was open for 2% of the time, Pallas kernels for 16%

profile of v2, /device:TPU:30, one launch (start us, length us, event | category | flops | bytes accessed | tf_op | source)
XLA Modules:
  0.0 161.0 jit_solution(4919114669942712264)
XLA Ops:
  0.0 1.9 %collective-permute-start = (bf16[96,256]{1,0:T(8,128)(2,1)}, bf16[96,256]{1,0:T(8,128)(2,1)S(1)}, u32[]{:S(2)}, u32[]{:S(2)}) collective-permute-start(bf16[96,256]{1,0:T(8,128)(2,1)} %bitcast.82), channel_id=1, source_target_pairs={{0,1},{1,0},{2,3},{3,2},{4,5},{5,4},{6,7},{7,6},{8,9},{9,8},{10,11... | collective-permute-start | bytes 147464 | tf_op jit(solution)/shard_map/ppermute | solution.py:46
  1.9 2.4 %collective-permute-done = bf16[96,256]{1,0:T(8,128)(2,1)S(1)} collective-permute-done((bf16[96,256]{1,0:T(8,128)(2,1)}, bf16[96,256]{1,0:T(8,128)(2,1)S(1)}, u32[]{:S(2)}, u32[]{:S(2)}) %collective-permute-start) | collective-permute-done | bytes 49184 | tf_op jit(solution)/shard_map/ppermute | solution.py:46
  5.1 6.4 %collective-permute-start.1 = (bf16[2,96,256]{2,1,0:T(8,128)(2,1)S(1)}, bf16[2,96,256]{2,1,0:T(8,128)(2,1)S(1)}, u32[]{:S(2)}, u32[]{:S(2)}) collective-permute-start(bf16[2,96,256]{2,1,0:T(8,128)(2,1)S(1)} %pad_maximum_fusion), channel_id=1, source_target_pairs={{2,0},{3,1},{4,2},{5,3},{6,4},{7,5},{0,6},{1,7},{10,8},{11,9},{12,... | collective-permute-start | bytes 294920 | tf_op jit(solution)/shard_map/ppermute | solution.py:42
  12.5 2.8 %collective-permute-start.3 = (bf16[2,96,256]{2,1,0:T(8,128)(2,1)S(1)}, bf16[2,96,256]{2,1,0:T(8,128)(2,1)S(1)}, u32[]{:S(2)}, u32[]{:S(2)}) collective-permute-start(bf16[2,96,256]{2,1,0:T(8,128)(2,1)S(1)} %pad_maximum_fusion), channel_id=1, source_target_pairs={{6,0},{7,1},{0,2},{1,3},{2,4},{3,5},{4,6},{5,7},{14,8},{15,9},{8,1... | collective-permute-start | bytes 294920 | tf_op jit(solution)/shard_map/ppermute | solution.py:42
  15.4 3.4 %collective-permute-done.1 = bf16[2,96,256]{2,1,0:T(8,128)(2,1)S(1)} collective-permute-done((bf16[2,96,256]{2,1,0:T(8,128)(2,1)S(1)}, bf16[2,96,256]{2,1,0:T(8,128)(2,1)S(1)}, u32[]{:S(2)}, u32[]{:S(2)}) %collective-permute-start.1) | collective-permute-done | bytes 98336 | tf_op jit(solution)/shard_map/ppermute | solution.py:42
  18.8 3.3 %collective-permute-done.2 = bf16[2,96,256]{2,1,0:T(8,128)(2,1)S(1)} collective-permute-done((bf16[2,96,256]{2,1,0:T(8,128)(2,1)S(1)}, bf16[2,96,256]{2,1,0:T(8,128)(2,1)S(1)}, u32[]{:S(2)}, u32[]{:S(2)}) %collective-permute-start.2) | collective-permute-done | bytes 98336 | tf_op jit(solution)/shard_map/ppermute | solution.py:42
  23.8 2.2 %collective-permute-start.6 = (bf16[768,256]{1,0:T(8,128)(2,1)S(1)}, bf16[768,256]{1,0:T(8,128)(2,1)}, u32[]{:S(2)}, u32[]{:S(2)}) collective-permute-start(bf16[768,256]{1,0:T(8,128)(2,1)S(1)} %bitcast.78), channel_id=1, source_target_pairs={{136,0},{137,1},{138,2},{139,3},{140,4},{141,5},{142,6},{143,7},{1... | collective-permute-start | bytes 1179656 | tf_op jit(solution)/shard_map/ppermute | solution.py:38
  28.8 7.7 %collective-permute-done.8 = f32[2,4,256]{2,1,0:T(4,128)} collective-permute-done((f32[2,4,256]{2,1,0:T(4,128)}, f32[2,4,256]{2,1,0:T(4,128)}, u32[]{:S(2)}, u32[]{:S(2)}) %collective-permute-start.8) | collective-permute-done | bytes 8224 | tf_op jit(solution)/shard_map/ppermute | solution.py:276
  37.3 2.5 %shard_map.64 = (bf16[2,768,256]{2,1,0:T(8,128)(2,1)}, bf16[2,768,256]{2,1,0:T(8,128)(2,1)}) custom-call(bf16[768,256]{1,0:T(8,128)(2,1)S(1)} %bitcast.79, bf16[768,256]{1,0:T(8,128)(2,1)} %collective-permute-done.4.b, bf16[768,256]{1,0:T(8,128)(2,1)} %collective-permute-done.5.c, bf16[768,256]{1,0:T(8,128)(2,1)} %collective-permute-done.6.d), custom_call_target="tpu_custom_call" | custom-call | tf_op jit(solution)/shard_map/pallas_call | solution.py:228
  48.3 5.1 %shard_map.65.refs_13_ = f32[2,2,2,256,256]{4,3,2,1,0:T(8,128)S(1)} custom-call(s32[3]{0:T(128)S(1)} %pad_add_fusion.refs_0_, bf16[6144,256]{1,0:T(8,128)(2,1)S(1)} %bitcast.64, bf16[6144,256]{1,0:T(8,128)(2,1)S(1)} %bitcast.70, bf16[6144,256]{1,0:T(8,128)(2,1)S(1)} %bitcast.65, bf16[6144,256]{1,0:T(8,128)(2,1)S(1)} %bitcast.71, ...), custom_call_target="tpu_custom_call" | custom-call | tf_op jit(solution)/shard_map/pallas_call | solution.py:149
  54.2 6.7 %collective-permute-done.14.refs_8_ = bf16[2,768,256]{2,1,0:T(8,128)(2,1)} collective-permute-done((bf16[2,768,256]{2,1,0:T(8,128)(2,1)}, bf16[2,768,256]{2,1,0:T(8,128)(2,1)}, u32[]{:S(2)}, u32[]{:S(2)}) %collective-permute-start.14) | collective-permute-done | bytes 786464 | tf_op jit(solution)/shard_map/ppermute | solution.py:34
  68.5 8.6 %shard_map.66.refs_9_ = f32[2,2,2,256,256]{4,3,2,1,0:T(8,128)S(1)} custom-call(s32[3]{0:T(128)S(1)} %pad_add_fusion.refs_0_, bf16[6144,256]{1,0:T(8,128)(2,1)S(1)} %bitcast.66, bf16[6144,256]{1,0:T(8,128)(2,1)S(1)} %bitcast.72, bf16[6144,256]{1,0:T(8,128)(2,1)S(1)} %bitcast.67, bf16[6144,256]{1,0:T(8,128)(2,1)S(1)} %bitcast.73, ...), custom_call_target="tpu_custom_call" | custom-call | tf_op jit(solution)/shard_map/pallas_call | solution.py:149
  80.8 3.8 %shard_map.67.refs_2_ = bf16[2,2,256,256]{3,2,1,0:T(8,128)(2,1)S(1)} custom-call(s32[3]{0:T(128)S(1)} %pad_add_fusion.refs_0_, bf16[6144,256]{1,0:T(8,128)(2,1)S(1)} %bitcast.68, bf16[6144,256]{1,0:T(8,128)(2,1)S(1)} %bitcast.74, bf16[6144,256]{1,0:T(8,128)(2,1)S(1)} %bitcast.69, bf16[6144,256]{1,0:T(8,128)(2,1)S(1)} %bitcast.75, ...), custom_call_target="tpu_custom_call" | custom-call | tf_op jit(solution)/shard_map/pallas_call | solution.py:149
  84.6 2.1 %shard_map.68 = bf16[4,768,256]{2,1,0:T(8,128)(2,1)S(1)} custom-call(s32[3]{0:T(128)S(1)} %pad_add_fusion.refs_0_, bf16[256,6144]{1,0:T(8,128)(2,1)S(1)} %bitcast.57, bf16[2,2,256,256]{3,2,1,0:T(8,128)(2,1)S(1)} %shard_map.67.refs_2_), custom_call_target="tpu_custom_call" | custom-call | tf_op jit(solution)/shard_map/pallas_call | solution.py:210
  86.9 3.7 %shard_map.70 = bf16[8,768,256]{2,1,0:T(8,128)(2,1)S(1)} custom-call(s32[3]{0:T(128)S(1)} %pad_add_fusion.refs_0_, bf16[256,6144]{1,0:T(8,128)(2,1)S(1)} %bitcast.58, bf16[2,2,256,256]{3,2,1,0:T(8,128)(2,1)S(1)} %shard_map.67.refs_2_), custom_call_target="tpu_custom_call" | custom-call | tf_op jit(solution)/shard_map/pallas_call | solution.py:210
  90.6 2.1 %shard_map.69 = bf16[4,768,256]{2,1,0:T(8,128)(2,1)S(1)} custom-call(s32[3]{0:T(128)S(1)} %pad_add_fusion.refs_0_, bf16[256,6144]{1,0:T(8,128)(2,1)S(1)} %bitcast.59, bf16[2,2,256,256]{3,2,1,0:T(8,128)(2,1)S(1)} %shard_map.67.refs_2_), custom_call_target="tpu_custom_call" | custom-call | tf_op jit(solution)/shard_map/pallas_call | solution.py:210
  92.7 2.2 %shard_map.71 = (bf16[2,768,256]{2,1,0:T(8,128)(2,1)S(1)}, bf16[2,768,256]{2,1,0:T(8,128)(2,1)S(1)}) custom-call(s32[3]{0:T(128)S(1)} %pad_add_fusion.refs_0_, bf16[256,6144]{1,0:T(8,128)(2,1)S(1)} %bitcast.60, bf16[2,2,256,256]{3,2,1,0:T(8,128)(2,1)S(1)} %shard_map.67.refs_2_, bf16[4,768,256]{2,1,0:T(8,128)(2,1)S(1)} %collective-permute-done.23.refs_3_), custom_call_target="tpu_custom_call" | custom-call | tf_op jit(solution)/shard_map/pallas_call | solution.py:210
  95.6 3.0 %collective-permute-start.26 = (bf16[2,768,256]{2,1,0:T(8,128)(2,1)S(1)}, bf16[2,768,256]{2,1,0:T(8,128)(2,1)S(1)}, u32[]{:S(2)}, u32[]{:S(2)}) collective-permute-start(bf16[2,768,256]{2,1,0:T(8,128)(2,1)S(1)} %get-tuple-element.73), channel_id=1, source_target_pairs={{48,0},{49,1},{50,2},{51,3},{52,4},{53,5},{54,6},{55,7},{56,8},{57... | collective-permute-start | bytes 2359304 | tf_op jit(solution)/shard_map/ppermute | solution.py:34
  98.5 4.5 %collective-permute-done.24.refs_3_ = bf16[4,768,256]{2,1,0:T(8,128)(2,1)S(1)} collective-permute-done((bf16[4,768,256]{2,1,0:T(8,128)(2,1)S(1)}, bf16[4,768,256]{2,1,0:T(8,128)(2,1)S(1)}, u32[]{:S(2)}, u32[]{:S(2)}) %collective-permute-start.24) | collective-permute-done | bytes 1572896 | tf_op jit(solution)/shard_map/ppermute | solution.py:50
  103.0 2.3 %shard_map.74 = (bf16[2,768,256]{2,1,0:T(8,128)(2,1)S(1)}, bf16[2,768,256]{2,1,0:T(8,128)(2,1)S(1)}) custom-call(s32[3]{0:T(128)S(1)} %pad_add_fusion.refs_0_, bf16[256,6144]{1,0:T(8,128)(2,1)S(1)} %bitcast.61, bf16[2,2,256,256]{3,2,1,0:T(8,128)(2,1)S(1)} %shard_map.67.refs_2_, bf16[4,768,256]{2,1,0:T(8,128)(2,1)S(1)} %collective-permute-done.24.refs_3_), custom_call_target="tpu_custom_call" | custom-call | tf_op jit(solution)/shard_map/pallas_call | solution.py:210
  105.7 2.9 %collective-permute-start.32 = (bf16[2,768,256]{2,1,0:T(8,128)(2,1)S(1)}, bf16[2,768,256]{2,1,0:T(8,128)(2,1)S(1)}, u32[]{:S(2)}, u32[]{:S(2)}) collective-permute-start(bf16[2,768,256]{2,1,0:T(8,128)(2,1)S(1)} %get-tuple-element.86), channel_id=1, source_target_pairs={{48,0},{49,1},{50,2},{51,3},{52,4},{53,5},{54,6},{55,7},{56,8},{57... | collective-permute-start | bytes 2359304 | tf_op jit(solution)/shard_map/ppermute | solution.py:34
  108.6 3.1 %collective-permute-done.27.refs_5_ = bf16[2,768,256]{2,1,0:T(8,128)(2,1)S(1)} collective-permute-done((bf16[2,768,256]{2,1,0:T(8,128)(2,1)S(1)}, bf16[2,768,256]{2,1,0:T(8,128)(2,1)S(1)}, u32[]{:S(2)}, u32[]{:S(2)}) %collective-permute-start.27) | collective-permute-done | bytes 786464 | tf_op jit(solution)/shard_map/ppermute | solution.py:34
  111.7 2.4 %shard_map.72 = (bf16[1,768,256]{2,1,0:T(8,128)(2,1)S(1)}, bf16[1,768,256]{2,1,0:T(8,128)(2,1)S(1)}, bf16[1,768,256]{2,1,0:T(8,128)(2,1)S(1)}, bf16[1,768,256]{2,1,0:T(8,128)(2,1)S(1)}) custom-call(s32[3]{0:T(128)S(1)} %pad_add_fusion.refs_0_, bf16[256,6144]{1,0:T(8,128)(2,1)S(1)} %bitcast.62, bf16[2,2,256,256]{3,2,1,0:T(8,128)(2,1)S(1)} %shard_map.67.refs_2_, ...), custom_call_target="tpu_custom_call" | custom-call | tf_op jit(solution)/shard_map/pallas_call | solution.py:210
  114.2 2.0 %collective-permute-start.33 = (bf16[1,768,256]{2,1,0:T(8,128)(2,1)S(1)}, bf16[1,768,256]{2,1,0:T(8,128)(2,1)S(1)}, u32[]{:S(2)}, u32[]{:S(2)}) collective-permute-start(bf16[1,768,256]{2,1,0:T(8,128)(2,1)S(1)} %get-tuple-element.87), channel_id=1, source_target_pairs={{16,0},{17,1},{18,2},{19,3},{20,4},{21,5},{22,6},{23,7},{24,8},{25... | collective-permute-start | bytes 1179656 | tf_op jit(solution)/shard_map/ppermute | solution.py:34
  116.3 2.2 %shard_map.73 = (bf16[2,768,256]{2,1,0:T(8,128)(2,1)S(1)}, bf16[2,768,256]{2,1,0:T(8,128)(2,1)S(1)}) custom-call(s32[3]{0:T(128)S(1)} %pad_add_fusion.refs_0_, bf16[256,6144]{1,0:T(8,128)(2,1)S(1)} %bitcast.63, bf16[2,2,256,256]{3,2,1,0:T(8,128)(2,1)S(1)} %shard_map.67.refs_2_, bf16[8,768,256]{2,1,0:T(8,128)(2,1)S(1)} %collective-permute-done.25.refs_3_), custom_call_target="tpu_custom_call" | custom-call | tf_op jit(solution)/shard_map/pallas_call | solution.py:210
  124.4 4.2 %collective-permute-done.35 = bf16[1,768,256]{2,1,0:T(8,128)(2,1)S(1)} collective-permute-done((bf16[1,768,256]{2,1,0:T(8,128)(2,1)S(1)}, bf16[1,768,256]{2,1,0:T(8,128)(2,1)S(1)}, u32[]{:S(2)}, u32[]{:S(2)}) %collective-permute-start.35) | collective-permute-done | bytes 393248 | tf_op jit(solution)/shard_map/ppermute | solution.py:34
  129.0 3.1 %collective-permute-start.36 = (bf16[768,256]{1,0:T(8,128)(2,1)S(1)}, bf16[768,256]{1,0:T(8,128)(2,1)S(1)}, u32[]{:S(2)}, u32[]{:S(2)}) collective-permute-start(bf16[768,256]{1,0:T(8,128)(2,1)S(1)} %get-tuple-element.90), channel_id=1, source_target_pairs={{8,0},{9,1},{10,2},{11,3},{12,4},{13,5},{14,6},{15,7},{0,8},{1,9},... | collective-permute-start | bytes 1179656 | tf_op jit(solution)/shard_map/ppermute | solution.py:38
  132.1 10.1 %collective-permute-done.34 = bf16[768,256]{1,0:T(8,128)(2,1)S(1)} collective-permute-done((bf16[768,256]{1,0:T(8,128)(2,1)S(1)}, bf16[768,256]{1,0:T(8,128)(2,1)S(1)}, u32[]{:S(2)}, u32[]{:S(2)}) %collective-permute-start.34) | collective-permute-done | bytes 393248 | tf_op jit(solution)/shard_map/ppermute | solution.py:38
  142.6 4.5 %collective-permute-start.37 = (bf16[2,96,256]{2,1,0:T(8,128)(2,1)S(1)}, bf16[2,96,256]{2,1,0:T(8,128)(2,1)S(1)}, u32[]{:S(2)}, u32[]{:S(2)}) collective-permute-start(bf16[2,96,256]{2,1,0:T(8,128)(2,1)S(1)} %get-tuple-element.91), channel_id=1, source_target_pairs={{4,0},{5,1},{6,2},{7,3},{0,4},{1,5},{2,6},{3,7},{12,8},{13,9},{14,... | collective-permute-start | bytes 294920 | tf_op jit(solution)/shard_map/ppermute | solution.py:42
  147.2 4.1 %collective-permute-start.39 = (bf16[2,96,256]{2,1,0:T(8,128)(2,1)S(1)}, bf16[2,96,256]{2,1,0:T(8,128)(2,1)S(1)}, u32[]{:S(2)}, u32[]{:S(2)}) collective-permute-start(bf16[2,96,256]{2,1,0:T(8,128)(2,1)S(1)} %get-tuple-element.92), channel_id=1, source_target_pairs={{2,0},{3,1},{4,2},{5,3},{6,4},{7,5},{0,6},{1,7},{10,8},{11,9},{12,... | collective-permute-start | bytes 294920 | tf_op jit(solution)/shard_map/ppermute | solution.py:42
  153.8 2.3 %collective-permute-done.39 = bf16[2,96,256]{2,1,0:T(8,128)(2,1)S(1)} collective-permute-done((bf16[2,96,256]{2,1,0:T(8,128)(2,1)S(1)}, bf16[2,96,256]{2,1,0:T(8,128)(2,1)S(1)}, u32[]{:S(2)}, u32[]{:S(2)}) %collective-permute-start.39) | collective-permute-done | bytes 98336 | tf_op jit(solution)/shard_map/ppermute | solution.py:42
  156.6 3.8 %collective-permute-done.40 = bf16[96,256]{1,0:T(8,128)(2,1)S(1)} collective-permute-done((bf16[96,256]{1,0:T(8,128)(2,1)S(1)}, bf16[96,256]{1,0:T(8,128)(2,1)S(1)}, u32[]{:S(2)}, u32[]{:S(2)}) %collective-permute-start.40) | collective-permute-done | bytes 49184 | tf_op jit(solution)/shard_map/ppermute | solution.py:46
  (89 shorter events, 39.5 us)
Async XLA Ops:
  5.1 13.6 %collective-permute-start.1 = (bf16[2,96,256]{2,1,0:T(8,128)(2,1)S(1)}, bf16[2,96,256]{2,1,0:T(8,128)(2,1)S(1)}, u32[]{:S(2)}, u32[]{:S(2)}) collective-permute-start(bf16[2,96,256]{2,1,0:T(8,128)(2,1)S(1)} %pad_maximum_fusion), channel_id=1, source_target_pairs={{2,0},{3,1},{4,2},{5,3},{6,4},{7,5},{0,6},{1,7},{10,8},{11,9},{12,... | collective-permute-start | bytes 294920 | tf_op jit(solution)/shard_map/ppermute | solution.py:42
  11.5 10.5 %collective-permute-start.2 = (bf16[2,96,256]{2,1,0:T(8,128)(2,1)S(1)}, bf16[2,96,256]{2,1,0:T(8,128)(2,1)S(1)}, u32[]{:S(2)}, u32[]{:S(2)}) collective-permute-start(bf16[2,96,256]{2,1,0:T(8,128)(2,1)S(1)} %pad_maximum_fusion), channel_id=1, source_target_pairs={{4,0},{5,1},{6,2},{7,3},{0,4},{1,5},{2,6},{3,7},{12,8},{13,9},{14,... | collective-permute-start | bytes 294920 | tf_op jit(solution)/shard_map/ppermute | solution.py:42
  12.5 9.5 %collective-permute-start.3 = (bf16[2,96,256]{2,1,0:T(8,128)(2,1)S(1)}, bf16[2,96,256]{2,1,0:T(8,128)(2,1)S(1)}, u32[]{:S(2)}, u32[]{:S(2)}) collective-permute-start(bf16[2,96,256]{2,1,0:T(8,128)(2,1)S(1)} %pad_maximum_fusion), channel_id=1, source_target_pairs={{6,0},{7,1},{0,2},{1,3},{2,4},{3,5},{4,6},{5,7},{14,8},{15,9},{8,1... | collective-permute-start | bytes 294920 | tf_op jit(solution)/shard_map/ppermute | solution.py:42
  22.1 15.2 %collective-permute-start.4 = (bf16[768,256]{1,0:T(8,128)(2,1)S(1)}, bf16[768,256]{1,0:T(8,128)(2,1)}, u32[]{:S(2)}, u32[]{:S(2)}) collective-permute-start(bf16[768,256]{1,0:T(8,128)(2,1)S(1)} %bitcast.76), channel_id=1, source_target_pairs={{128,0},{129,1},{130,2},{131,3},{132,4},{133,5},{134,6},{135,7},{1... | collective-permute-start | bytes 1179656 | tf_op jit(solution)/shard_map/ppermute | solution.py:38
  22.9 14.4 %collective-permute-start.5 = (bf16[768,256]{1,0:T(8,128)(2,1)S(1)}, bf16[768,256]{1,0:T(8,128)(2,1)}, u32[]{:S(2)}, u32[]{:S(2)}) collective-permute-start(bf16[768,256]{1,0:T(8,128)(2,1)S(1)} %bitcast.77), channel_id=1, source_target_pairs={{8,0},{9,1},{10,2},{11,3},{12,4},{13,5},{14,6},{15,7},{0,8},{1,9},... | collective-permute-start | bytes 1179656 | tf_op jit(solution)/shard_map/ppermute | solution.py:38
  23.8 13.4 %collective-permute-start.6 = (bf16[768,256]{1,0:T(8,128)(2,1)S(1)}, bf16[768,256]{1,0:T(8,128)(2,1)}, u32[]{:S(2)}, u32[]{:S(2)}) collective-permute-start(bf16[768,256]{1,0:T(8,128)(2,1)S(1)} %bitcast.78), channel_id=1, source_target_pairs={{136,0},{137,1},{138,2},{139,3},{140,4},{141,5},{142,6},{143,7},{1... | collective-permute-start | bytes 1179656 | tf_op jit(solution)/shard_map/ppermute | solution.py:38
  28.6 8.0 %collective-permute-start.8 = (f32[2,4,256]{2,1,0:T(4,128)}, f32[2,4,256]{2,1,0:T(4,128)}, u32[]{:S(2)}, u32[]{:S(2)}) collective-permute-start(f32[2,4,256]{2,1,0:T(4,128)} %get-tuple-element.96), channel_id=1, source_target_pairs={{0,128},{128,0},{1,129},{129,1},{2,130},{130,2},{3,131},{131,3},{4... | collective-permute-start | bytes 24584 | tf_op jit(solution)/shard_map/ppermute | solution.py:276
  39.7 5.5 %collective-permute-start.16 = (bf16[2,768,256]{2,1,0:T(8,128)(2,1)}, bf16[2,768,256]{2,1,0:T(8,128)(2,1)}, u32[]{:S(2)}, u32[]{:S(2)}) collective-permute-start(bf16[2,768,256]{2,1,0:T(8,128)(2,1)} %get-tuple-element.50.refs_6_), channel_id=1, source_target_pairs={{0,64},{64,0},{1,65},{65,1},{2,66},{66,2},{3,67},{67,3},{4,68},{68... | collective-permute-start | bytes 2359304 | tf_op jit(solution)/shard_map/ppermute | solution.py:50
  40.2 13.1 %collective-permute-start.11 = (bf16[2,768,256]{2,1,0:T(8,128)(2,1)}, bf16[2,768,256]{2,1,0:T(8,128)(2,1)}, u32[]{:S(2)}, u32[]{:S(2)}) collective-permute-start(bf16[2,768,256]{2,1,0:T(8,128)(2,1)} %get-tuple-element.50.refs_6_), channel_id=1, source_target_pairs={{48,0},{49,1},{50,2},{51,3},{52,4},{53,5},{54,6},{55,7},{56,8},{57... | collective-permute-start | bytes 2359304 | tf_op jit(solution)/shard_map/ppermute | solution.py:34
  40.7 13.5 %collective-permute-start.13 = (bf16[2,768,256]{2,1,0:T(8,128)(2,1)}, bf16[2,768,256]{2,1,0:T(8,128)(2,1)}, u32[]{:S(2)}, u32[]{:S(2)}) collective-permute-start(bf16[2,768,256]{2,1,0:T(8,128)(2,1)} %get-tuple-element.50.refs_6_), channel_id=1, source_target_pairs={{16,0},{17,1},{18,2},{19,3},{20,4},{21,5},{22,6},{23,7},{24,8},{25... | collective-permute-start | bytes 2359304 | tf_op jit(solution)/shard_map/ppermute | solution.py:34
  42.3 18.7 %collective-permute-start.14 = (bf16[2,768,256]{2,1,0:T(8,128)(2,1)}, bf16[2,768,256]{2,1,0:T(8,128)(2,1)}, u32[]{:S(2)}, u32[]{:S(2)}) collective-permute-start(bf16[2,768,256]{2,1,0:T(8,128)(2,1)} %get-tuple-element.49.refs_5_), channel_id=1, source_target_pairs={{48,0},{49,1},{50,2},{51,3},{52,4},{53,5},{54,6},{55,7},{56,8},{57... | collective-permute-start | bytes 2359304 | tf_op jit(solution)/shard_map/ppermute | solution.py:34
  44.8 17.8 %collective-permute-start.9 = (bf16[2,768,256]{2,1,0:T(8,128)(2,1)}, bf16[2,768,256]{2,1,0:T(8,128)(2,1)}, u32[]{:S(2)}, u32[]{:S(2)}) collective-permute-start(bf16[2,768,256]{2,1,0:T(8,128)(2,1)} %get-tuple-element.49.refs_5_), channel_id=1, source_target_pairs={{16,0},{17,1},{18,2},{19,3},{20,4},{21,5},{22,6},{23,7},{24,8},{25... | collective-permute-start | bytes 2359304 | tf_op jit(solution)/shard_map/ppermute | solution.py:34
  63.3 5.2 %collective-permute-start.20 = (bf16[2,768,256]{2,1,0:T(8,128)(2,1)}, bf16[2,768,256]{2,1,0:T(8,128)(2,1)S(1)}, u32[]{:S(2)}, u32[]{:S(2)}) collective-permute-start(bf16[2,768,256]{2,1,0:T(8,128)(2,1)} %collective-permute-done.14.refs_8_), channel_id=1, source_target_pairs={{0,64},{64,0},{1,65},{65,1},{2,66},{66,2},{3,67},{67,3},{4,68},{68... | collective-permute-start | bytes 2359304 | tf_op jit(solution)/shard_map/ppermute | solution.py:50
  63.7 13.4 %collective-permute-start.10 = (bf16[2,768,256]{2,1,0:T(8,128)(2,1)}, bf16[2,768,256]{2,1,0:T(8,128)(2,1)S(1)}, u32[]{:S(2)}, u32[]{:S(2)}) collective-permute-start(bf16[2,768,256]{2,1,0:T(8,128)(2,1)} %collective-permute-done.9.refs_5_), channel_id=1, source_target_pairs={{16,0},{17,1},{18,2},{19,3},{20,4},{21,5},{22,6},{23,7},{24,8},{25... | collective-permute-start | bytes 2359304 | tf_op jit(solution)/shard_map/ppermute | solution.py:34
  65.2 12.2 %collective-permute-start.12 = (bf16[2,768,256]{2,1,0:T(8,128)(2,1)}, bf16[2,768,256]{2,1,0:T(8,128)(2,1)S(1)}, u32[]{:S(2)}, u32[]{:S(2)}) collective-permute-start(bf16[2,768,256]{2,1,0:T(8,128)(2,1)} %collective-permute-done.11.refs_6_), channel_id=1, source_target_pairs={{48,0},{49,1},{50,2},{51,3},{52,4},{53,5},{54,6},{55,7},{56,8},{57... | collective-permute-start | bytes 2359304 | tf_op jit(solution)/shard_map/ppermute | solution.py:34
  86.7 6.0 %collective-permute-start.23 = (bf16[4,768,256]{2,1,0:T(8,128)(2,1)S(1)}, bf16[4,768,256]{2,1,0:T(8,128)(2,1)S(1)}, u32[]{:S(2)}, u32[]{:S(2)}) collective-permute-start(bf16[4,768,256]{2,1,0:T(8,128)(2,1)S(1)} %shard_map.68), channel_id=1, source_target_pairs={{0,64},{64,0},{1,65},{65,1},{2,66},{66,2},{3,67},{67,3},{4,68},{68... | collective-permute-start | bytes 4718600 | tf_op jit(solution)/shard_map/ppermute | solution.py:50
  95.0 16.8 %collective-permute-start.25 = (bf16[8,768,256]{2,1,0:T(8,128)(2,1)S(1)}, bf16[8,768,256]{2,1,0:T(8,128)(2,1)S(1)}, u32[]{:S(2)}, u32[]{:S(2)}) collective-permute-start(bf16[8,768,256]{2,1,0:T(8,128)(2,1)S(1)} %shard_map.70), channel_id=1, source_target_pairs={{0,64},{64,0},{1,65},{65,1},{2,66},{66,2},{3,67},{67,3},{4,68},{68... | collective-permute-start | bytes 9437192 | tf_op jit(solution)/shard_map/ppermute | solution.py:50
  95.5 7.5 %collective-permute-start.24 = (bf16[4,768,256]{2,1,0:T(8,128)(2,1)S(1)}, bf16[4,768,256]{2,1,0:T(8,128)(2,1)S(1)}, u32[]{:S(2)}, u32[]{:S(2)}) collective-permute-start(bf16[4,768,256]{2,1,0:T(8,128)(2,1)S(1)} %shard_map.69), channel_id=1, source_target_pairs={{0,64},{64,0},{1,65},{65,1},{2,66},{66,2},{3,67},{67,3},{4,68},{68... | collective-permute-start | bytes 4718600 | tf_op jit(solution)/shard_map/ppermute | solution.py:50
  95.6 13.0 %collective-permute-start.26 = (bf16[2,768,256]{2,1,0:T(8,128)(2,1)S(1)}, bf16[2,768,256]{2,1,0:T(8,128)(2,1)S(1)}, u32[]{:S(2)}, u32[]{:S(2)}) collective-permute-start(bf16[2,768,256]{2,1,0:T(8,128)(2,1)S(1)} %get-tuple-element.73), channel_id=1, source_target_pairs={{48,0},{49,1},{50,2},{51,3},{52,4},{53,5},{54,6},{55,7},{56,8},{57... | collective-permute-start | bytes 2359304 | tf_op jit(solution)/shard_map/ppermute | solution.py:34
  98.5 13.2 %collective-permute-start.27 = (bf16[2,768,256]{2,1,0:T(8,128)(2,1)S(1)}, bf16[2,768,256]{2,1,0:T(8,128)(2,1)S(1)}, u32[]{:S(2)}, u32[]{:S(2)}) collective-permute-start(bf16[2,768,256]{2,1,0:T(8,128)(2,1)S(1)} %get-tuple-element.74), channel_id=1, source_target_pairs={{16,0},{17,1},{18,2},{19,3},{20,4},{21,5},{22,6},{23,7},{24,8},{25... | collective-permute-start | bytes 2359304 | tf_op jit(solution)/shard_map/ppermute | solution.py:34
  105.3 14.9 %collective-permute-start.29 = (bf16[2,768,256]{2,1,0:T(8,128)(2,1)S(1)}, bf16[2,768,256]{2,1,0:T(8,128)(2,1)S(1)}, u32[]{:S(2)}, u32[]{:S(2)}) collective-permute-start(bf16[2,768,256]{2,1,0:T(8,128)(2,1)S(1)} %get-tuple-element.83), channel_id=1, source_target_pairs={{16,0},{17,1},{18,2},{19,3},{20,4},{21,5},{22,6},{23,7},{24,8},{25... | collective-permute-start | bytes 2359304 | tf_op jit(solution)/shard_map/ppermute | solution.py:34
  105.7 18.5 %collective-permute-start.32 = (bf16[2,768,256]{2,1,0:T(8,128)(2,1)S(1)}, bf16[2,768,256]{2,1,0:T(8,128)(2,1)S(1)}, u32[]{:S(2)}, u32[]{:S(2)}) collective-permute-start(bf16[2,768,256]{2,1,0:T(8,128)(2,1)S(1)} %get-tuple-element.86), channel_id=1, source_target_pairs={{48,0},{49,1},{50,2},{51,3},{52,4},{53,5},{54,6},{55,7},{56,8},{57... | collective-permute-start | bytes 2359304 | tf_op jit(solution)/shard_map/ppermute | solution.py:34
  114.1 8.2 %collective-permute-start.30 = (bf16[1,768,256]{2,1,0:T(8,128)(2,1)S(1)}, bf16[1,768,256]{2,1,0:T(8,128)(2,1)S(1)}, u32[]{:S(2)}, u32[]{:S(2)}) collective-permute-start(bf16[1,768,256]{2,1,0:T(8,128)(2,1)S(1)} %get-tuple-element.84), channel_id=1, source_target_pairs={{48,0},{49,1},{50,2},{51,3},{52,4},{53,5},{54,6},{55,7},{56,8},{57... | collective-permute-start | bytes 1179656 | tf_op jit(solution)/shard_map/ppermute | solution.py:34
  114.2 10.2 %collective-permute-start.33 = (bf16[1,768,256]{2,1,0:T(8,128)(2,1)S(1)}, bf16[1,768,256]{2,1,0:T(8,128)(2,1)S(1)}, u32[]{:S(2)}, u32[]{:S(2)}) collective-permute-start(bf16[1,768,256]{2,1,0:T(8,128)(2,1)S(1)} %get-tuple-element.87), channel_id=1, source_target_pairs={{16,0},{17,1},{18,2},{19,3},{20,4},{21,5},{22,6},{23,7},{24,8},{25... | collective-permute-start | bytes 1179656 | tf_op jit(solution)/shard_map/ppermute | solution.py:34
  116.2 12.4 %collective-permute-start.35 = (bf16[1,768,256]{2,1,0:T(8,128)(2,1)S(1)}, bf16[1,768,256]{2,1,0:T(8,128)(2,1)S(1)}, u32[]{:S(2)}, u32[]{:S(2)}) collective-permute-start(bf16[1,768,256]{2,1,0:T(8,128)(2,1)S(1)} %get-tuple-element.88), channel_id=1, source_target_pairs={{16,0},{17,1},{18,2},{19,3},{20,4},{21,5},{22,6},{23,7},{24,8},{25... | collective-permute-start | bytes 1179656 | tf_op jit(solution)/shard_map/ppermute | solution.py:34
  120.2 12.0 %collective-permute-start.28 = (bf16[1,768,256]{2,1,0:T(8,128)(2,1)S(1)}, bf16[1,768,256]{2,1,0:T(8,128)(2,1)S(1)}, u32[]{:S(2)}, u32[]{:S(2)}) collective-permute-start(bf16[1,768,256]{2,1,0:T(8,128)(2,1)S(1)} %get-tuple-element.81), channel_id=1, source_target_pairs={{48,0},{49,1},{50,2},{51,3},{52,4},{53,5},{54,6},{55,7},{56,8},{57... | collective-permute-start | bytes 1179656 | tf_op jit(solution)/shard_map/ppermute | solution.py:34
  122.5 9.6 %collective-permute-start.31 = (bf16[768,256]{1,0:T(8,128)(2,1)S(1)}, bf16[768,256]{1,0:T(8,128)(2,1)S(1)}, u32[]{:S(2)}, u32[]{:S(2)}) collective-permute-start(bf16[768,256]{1,0:T(8,128)(2,1)S(1)} %fusion.4), channel_id=1, source_target_pairs={{136,0},{137,1},{138,2},{139,3},{140,4},{141,5},{142,6},{143,7},{1... | collective-permute-start | bytes 1179656 | tf_op jit(solution)/shard_map/ppermute | solution.py:38
  128.9 13.3 %collective-permute-start.34 = (bf16[768,256]{1,0:T(8,128)(2,1)S(1)}, bf16[768,256]{1,0:T(8,128)(2,1)S(1)}, u32[]{:S(2)}, u32[]{:S(2)}) collective-permute-start(bf16[768,256]{1,0:T(8,128)(2,1)S(1)} %get-tuple-element.89), channel_id=1, source_target_pairs={{128,0},{129,1},{130,2},{131,3},{132,4},{133,5},{134,6},{135,7},{1... | collective-permute-start | bytes 1179656 | tf_op jit(solution)/shard_map/ppermute | solution.py:38
  129.0 13.2 %collective-permute-start.36 = (bf16[768,256]{1,0:T(8,128)(2,1)S(1)}, bf16[768,256]{1,0:T(8,128)(2,1)S(1)}, u32[]{:S(2)}, u32[]{:S(2)}) collective-permute-start(bf16[768,256]{1,0:T(8,128)(2,1)S(1)} %get-tuple-element.90), channel_id=1, source_target_pairs={{8,0},{9,1},{10,2},{11,3},{12,4},{13,5},{14,6},{15,7},{0,8},{1,9},... | collective-permute-start | bytes 1179656 | tf_op jit(solution)/shard_map/ppermute | solution.py:38
  142.6 9.9 %collective-permute-start.37 = (bf16[2,96,256]{2,1,0:T(8,128)(2,1)S(1)}, bf16[2,96,256]{2,1,0:T(8,128)(2,1)S(1)}, u32[]{:S(2)}, u32[]{:S(2)}) collective-permute-start(bf16[2,96,256]{2,1,0:T(8,128)(2,1)S(1)} %get-tuple-element.91), channel_id=1, source_target_pairs={{4,0},{5,1},{6,2},{7,3},{0,4},{1,5},{2,6},{3,7},{12,8},{13,9},{14,... | collective-permute-start | bytes 294920 | tf_op jit(solution)/shard_map/ppermute | solution.py:42
  147.1 6.7 %collective-permute-start.38 = (bf16[2,96,256]{2,1,0:T(8,128)(2,1)S(1)}, bf16[2,96,256]{2,1,0:T(8,128)(2,1)S(1)}, u32[]{:S(2)}, u32[]{:S(2)}) collective-permute-start(bf16[2,96,256]{2,1,0:T(8,128)(2,1)S(1)} %get-tuple-element.93), channel_id=1, source_target_pairs={{6,0},{7,1},{0,2},{1,3},{2,4},{3,5},{4,6},{5,7},{14,8},{15,9},{8,1... | collective-permute-start | bytes 294920 | tf_op jit(solution)/shard_map/ppermute | solution.py:42
  147.2 9.0 %collective-permute-start.39 = (bf16[2,96,256]{2,1,0:T(8,128)(2,1)S(1)}, bf16[2,96,256]{2,1,0:T(8,128)(2,1)S(1)}, u32[]{:S(2)}, u32[]{:S(2)}) collective-permute-start(bf16[2,96,256]{2,1,0:T(8,128)(2,1)S(1)} %get-tuple-element.92), channel_id=1, source_target_pairs={{2,0},{3,1},{4,2},{5,3},{6,4},{7,5},{0,6},{1,7},{10,8},{11,9},{12,... | collective-permute-start | bytes 294920 | tf_op jit(solution)/shard_map/ppermute | solution.py:42
  (14 other events, 83.5 us)

commit v3 on v2

--- a/solution.py
+++ b/solution.py
@@ -260,12 +260,11 @@
     wg, wu, wd = w_gate[0], w_up[0], w_down[0]
 
     own = tokens.T
-    pair = z_pair(own)
-    pair = jnp.stack([jnp.where(zl == 0, own, pair), jnp.where(zl == 0, pair, own)])
-    start = jnp.zeros((NZ // 2, 2, feats, COLS), BF16)
+    quad = jnp.zeros((NZ // 2, feats, COLS), BF16)
     for s in range(NZ // 2):
-        piece = from_z(pair, 2 * s) if s else pair
-        start = put(start, piece[None], (zh + s) % 4)
+        quad = put(quad, (from_z(own, 2 * s) if s else own)[None], (zh + s) % 4)
+    pair = z_pair(quad)
+    start = jnp.stack([jnp.where(zl == 0, quad, pair), jnp.where(zl == 0, pair, quad)], axis=1)
     start = start.reshape(rows, COLS)
 
     experts = jnp.arange(4, dtype=jnp.int32)
@@ -279,14 +278,14 @@
 
     steps = {s: from_minor(start, s) for s in (1, 2, 3)}
     own = join(start, steps[1], steps[2], steps[3])
-    *own, w = lax.optimization_barrier((*own, w))
 
     through = [from_major(own[0], 1), from_major(own[1], 3)]
     direct = [from_major(own[1], 1), from_major(own[0], 3)]
     far = [from_major(through[0], 1), from_major(through[1], 3)]
     swap = lambda vs: [sibling(v) for v in vs]
     sums = hidden_of(at, wg, wu, OWN, own, swap(own))
-    *near, sums = lax.optimization_barrier((*through, *direct, sums))
+    *direct, sums, w = lax.optimization_barrier((*direct, sums, w))
+    near = [*through, *direct]
     sums = hidden_of(at, wg, wu, THROUGH + DIRECT, near, swap(near), sums)
     *far, sums = lax.optimization_barrier((*far, sums))
     h = hidden_of(at, wg, wu, FAR, far, swap(far), sums, w)
@@ -316,9 +315,10 @@
     c = total(c[0], came[1], came[3], came[2])
 
     c = c.reshape(NZ // 2, 2, feats, COLS)
-    chunk = lambda s: take(c, (zh + s) % 4)
+    half = lambda i: lax.dynamic_index_in_dim(c, i, axis=1, keepdims=False)
+    quad = total(half(zl), z_pair(half(1 - zl)))
+    chunk = lambda s: take(quad, (zh + s) % 4)
     c = total(chunk(0), *[from_z(chunk(s), -2 * s) for s in (2, 1, 3)])
-    c = total(take(c, zl), z_pair(take(c, 1 - zl)))
     return c.T
 
 

time: 162 us -> 160 us (0.988)
  starting transfers between devices: 49.2 us -> 56.6 us
  waiting for transfers between devices: 66.1 us -> 59 us
    ppermute x6, waiting for transfers between devices: 10.1 us -> 20.2 us  [from_minor(): return lax.ppermute(v, AXES, shift_perm(False, s))]
    ppermute x14, waiting for transfers between devices: 19.2 us -> 10.5 us  [from_major(): return lax.ppermute(v, AXES, shift_perm(True, s))]
    ppermute x6, waiting for transfers between devices: 11.6 us -> 6.15 us  [from_z(): return lax.ppermute(v, 'z', [((i + s) % NZ, i) for i in range(NZ)])]
    ppermute x12, starting transfers between devices: 2.93 us -> 7.89 us  [sibling(): return lax.ppermute(v, 'core', [(0, 1), (1, 0)])]
    ppermute x1, waiting for transfers between devices: 7.72 us -> 3.14 us  [body(): other = lax.ppermute(near, 'ylo', [(0, 1), (1, 0)])]
    ppermute x2, waiting for transfers between devices: 6.23 us -> 8.48 us  [z_pair(): return lax.ppermute(v, 'z', [(i, i ^ 1) for i in range(NZ)])]
    unnamed x10, local copies, waits for them, and re-layouts: 3.9 us -> 1.91 us
    convert_element_type x4, other arithmetic: 0.9 us -> 2.69 us  [total(): return out.astype(BF16)]
  transfers between devices with their start and end apart: 41 -> 41, of which waited for: 25 -> 22; matrix products, arithmetic and copies ran while one was open for 2% -> 1% of each run, Pallas kernels for 16% -> 17%
where the time goes in v3:
time: 160 us; the launch traced here: 158 us
  waiting for transfers between devices  59 us (37%)
  starting transfers between devices  56.6 us (35%)
  Pallas kernels  35.4 us (22%)
  other arithmetic  3.51 us (2%)
  local copies, waits for them, and re-layouts  2.81 us (2%)
    ppermute x6, waiting for transfers between devices, from_minor(): return lax.ppermute(v, AXES, shift_perm(False, s))  20.2 us
    ppermute x6, starting transfers between devices, from_z(): return lax.ppermute(v, 'z', [((i + s) % NZ, i) for i in range(NZ)])  18.5 us
    ppermute x14, starting transfers between devices, from_major(): return lax.ppermute(v, AXES, shift_perm(True, s))  17.2 us
    pallas_call x7, Pallas kernels, down_of(): pl.pallas_call(kernel, grid_spec=pltpu.PrefetchScalarGridSpec(num_scalar_...  17.1 us
    pallas_call x3, Pallas kernels, hidden_of(): pl.pallas_call(kernel, grid_spec=pltpu.PrefetchScalarGridSpec(num_scalar_...  17 us
    ppermute x12, waiting for transfers between devices, sibling(): return lax.ppermute(v, 'core', [(0, 1), (1, 0)])  10.5 us
    ppermute x14, waiting for transfers between devices, from_major(): return lax.ppermute(v, AXES, shift_perm(True, s))  10.5 us
    ppermute x6, starting transfers between devices, from_minor(): return lax.ppermute(v, AXES, shift_perm(False, s))  9.36 us
  transfers between devices with their start and end apart: 41, of which 22 were waited for; matrix products, arithmetic and copies ran while one was open for 1% of the time, Pallas kernels for 17%

profile of v3, /device:TPU:30, one launch (start us, length us, event | category | flops | bytes accessed | tf_op | source)
XLA Modules:
  0.0 157.6 jit_solution(4475645570457599233)
XLA Ops:
  0.0 6.4 %collective-permute-start = (bf16[96,256]{1,0:T(8,128)(2,1)}, bf16[96,256]{1,0:T(8,128)(2,1)S(1)}, u32[]{:S(2)}, u32[]{:S(2)}) collective-permute-start(bf16[96,256]{1,0:T(8,128)(2,1)} %bitcast.85), channel_id=1, source_target_pairs={{2,0},{3,1},{4,2},{5,3},{6,4},{7,5},{0,6},{1,7},{10,8},{11,9},{12,... | collective-permute-start | bytes 147464 | tf_op jit(solution)/shard_map/ppermute | solution.py:42
  7.4 2.8 %collective-permute-start.2 = (bf16[96,256]{1,0:T(8,128)(2,1)}, bf16[96,256]{1,0:T(8,128)(2,1)S(1)}, u32[]{:S(2)}, u32[]{:S(2)}) collective-permute-start(bf16[96,256]{1,0:T(8,128)(2,1)} %bitcast.87), channel_id=1, source_target_pairs={{6,0},{7,1},{0,2},{1,3},{2,4},{3,5},{4,6},{5,7},{14,8},{15,9},{8,1... | collective-permute-start | bytes 147464 | tf_op jit(solution)/shard_map/ppermute | solution.py:42
  11.1 3.9 %collective-permute-done.1 = bf16[96,256]{1,0:T(8,128)(2,1)S(1)} collective-permute-done((bf16[96,256]{1,0:T(8,128)(2,1)}, bf16[96,256]{1,0:T(8,128)(2,1)S(1)}, u32[]{:S(2)}, u32[]{:S(2)}) %collective-permute-start.1) | collective-permute-done | bytes 49184 | tf_op jit(solution)/shard_map/ppermute | solution.py:42
  16.5 4.2 %collective-permute-done.3 = bf16[4,96,256]{2,1,0:T(8,128)(2,1)S(1)} collective-permute-done((bf16[4,96,256]{2,1,0:T(8,128)(2,1)S(1)}, bf16[4,96,256]{2,1,0:T(8,128)(2,1)S(1)}, u32[]{:S(2)}, u32[]{:S(2)}) %collective-permute-start.3) | collective-permute-done | bytes 196640 | tf_op jit(solution)/shard_map/ppermute | solution.py:46
  22.5 2.2 %collective-permute-start.6 = (bf16[768,256]{1,0:T(8,128)(2,1)S(1)}, bf16[768,256]{1,0:T(8,128)(2,1)S(1)}, u32[]{:S(2)}, u32[]{:S(2)}) collective-permute-start(bf16[768,256]{1,0:T(8,128)(2,1)S(1)} %bitcast.81), channel_id=1, source_target_pairs={{136,0},{137,1},{138,2},{139,3},{140,4},{141,5},{142,6},{143,7},{1... | collective-permute-start | bytes 1179656 | tf_op jit(solution)/shard_map/ppermute | solution.py:38
  24.7 9.3 %collective-permute-done.4.b = bf16[768,256]{1,0:T(8,128)(2,1)S(1)} collective-permute-done((bf16[768,256]{1,0:T(8,128)(2,1)S(1)}, bf16[768,256]{1,0:T(8,128)(2,1)S(1)}, u32[]{:S(2)}, u32[]{:S(2)}) %collective-permute-start.4) | collective-permute-done | bytes 393248 | tf_op jit(solution)/shard_map/ppermute | solution.py:38
  37.6 2.4 %collective-permute-start.12 = (bf16[2,768,256]{2,1,0:T(8,128)(2,1)}, bf16[2,768,256]{2,1,0:T(8,128)(2,1)}, u32[]{:S(2)}, u32[]{:S(2)}) collective-permute-start(bf16[2,768,256]{2,1,0:T(8,128)(2,1)} %get-tuple-element.43.refs_5_), channel_id=1, source_target_pairs={{48,0},{49,1},{50,2},{51,3},{52,4},{53,5},{54,6},{55,7},{56,8},{57... | collective-permute-start | bytes 2359304 | tf_op jit(solution)/shard_map/ppermute | solution.py:34
  41.9 3.1 %collective-permute-done.16 = f32[2,4,256]{2,1,0:T(4,128)S(1)} collective-permute-done((f32[2,4,256]{2,1,0:T(4,128)S(1)}, f32[2,4,256]{2,1,0:T(4,128)S(1)}, u32[]{:S(2)}, u32[]{:S(2)}) %collective-permute-start.16) | collective-permute-done | bytes 8224 | tf_op jit(solution)/shard_map/ppermute | solution.py:275
  45.2 3.2 %collective-permute-start.9 = (bf16[2,768,256]{2,1,0:T(8,128)(2,1)}, bf16[2,768,256]{2,1,0:T(8,128)(2,1)S(1)}, u32[]{:S(2)}, u32[]{:S(2)}) collective-permute-start(bf16[2,768,256]{2,1,0:T(8,128)(2,1)} %get-tuple-element.44.refs_6_), channel_id=1, source_target_pairs={{48,0},{49,1},{50,2},{51,3},{52,4},{53,5},{54,6},{55,7},{56,8},{57... | collective-permute-start | bytes 2359304 | tf_op jit(solution)/shard_map/ppermute | solution.py:34
  50.3 5.2 %shard_map.65.refs_13_ = f32[2,2,2,256,256]{4,3,2,1,0:T(8,128)S(1)} custom-call(s32[3]{0:T(128)S(1)} %pad_add_fusion.refs_0_, bf16[6144,256]{1,0:T(8,128)(2,1)S(1)} %bitcast.67, bf16[6144,256]{1,0:T(8,128)(2,1)S(1)} %bitcast.73, bf16[6144,256]{1,0:T(8,128)(2,1)S(1)} %bitcast.68, bf16[6144,256]{1,0:T(8,128)(2,1)S(1)} %bitcast.74, ...), custom_call_target="tpu_custom_call" | custom-call | tf_op jit(solution)/shard_map/pallas_call | solution.py:149
  55.6 3.3 %collective-permute-start.19 = (bf16[2,768,256]{2,1,0:T(8,128)(2,1)}, bf16[2,768,256]{2,1,0:T(8,128)(2,1)S(1)}, u32[]{:S(2)}, u32[]{:S(2)}) collective-permute-start(bf16[2,768,256]{2,1,0:T(8,128)(2,1)} %collective-permute-done.11.refs_7_), channel_id=1, source_target_pairs={{0,64},{64,0},{1,65},{65,1},{2,66},{66,2},{3,67},{67,3},{4,68},{68... | collective-permute-start | bytes 2359304 | tf_op jit(solution)/shard_map/ppermute | solution.py:50
  59.0 2.0 %collective-permute-start.17 = (bf16[2,768,256]{2,1,0:T(8,128)(2,1)S(1)}, bf16[2,768,256]{2,1,0:T(8,128)(2,1)S(1)}, u32[]{:S(2)}, u32[]{:S(2)}) collective-permute-start(bf16[2,768,256]{2,1,0:T(8,128)(2,1)S(1)} %collective-permute-done.7.refs_5_), channel_id=1, source_target_pairs={{0,64},{64,0},{1,65},{65,1},{2,66},{66,2},{3,67},{67,3},{4,68},{68... | collective-permute-start | bytes 2359304 | tf_op jit(solution)/shard_map/ppermute | solution.py:50
  64.2 8.1 %shard_map.66.refs_9_ = f32[2,2,2,256,256]{4,3,2,1,0:T(8,128)S(1)} custom-call(s32[3]{0:T(128)S(1)} %pad_add_fusion.refs_0_, bf16[6144,256]{1,0:T(8,128)(2,1)S(1)} %bitcast.69, bf16[6144,256]{1,0:T(8,128)(2,1)S(1)} %bitcast.75, bf16[6144,256]{1,0:T(8,128)(2,1)S(1)} %bitcast.70, bf16[6144,256]{1,0:T(8,128)(2,1)S(1)} %bitcast.76, ...), custom_call_target="tpu_custom_call" | custom-call | tf_op jit(solution)/shard_map/pallas_call | solution.py:149
  78.8 3.7 %shard_map.67.refs_2_ = bf16[2,2,256,256]{3,2,1,0:T(8,128)(2,1)S(1)} custom-call(s32[3]{0:T(128)S(1)} %pad_add_fusion.refs_0_, bf16[6144,256]{1,0:T(8,128)(2,1)S(1)} %bitcast.71, bf16[6144,256]{1,0:T(8,128)(2,1)S(1)} %bitcast.77, bf16[6144,256]{1,0:T(8,128)(2,1)S(1)} %bitcast.72, bf16[6144,256]{1,0:T(8,128)(2,1)S(1)} %bitcast.78, ...), custom_call_target="tpu_custom_call" | custom-call | tf_op jit(solution)/shard_map/pallas_call | solution.py:149
  82.6 2.1 %shard_map.68 = bf16[4,768,256]{2,1,0:T(8,128)(2,1)S(1)} custom-call(s32[3]{0:T(128)S(1)} %pad_add_fusion.refs_0_, bf16[256,6144]{1,0:T(8,128)(2,1)S(1)} %bitcast.60, bf16[2,2,256,256]{3,2,1,0:T(8,128)(2,1)S(1)} %shard_map.67.refs_2_), custom_call_target="tpu_custom_call" | custom-call | tf_op jit(solution)/shard_map/pallas_call | solution.py:210
  85.1 3.7 %shard_map.70 = bf16[8,768,256]{2,1,0:T(8,128)(2,1)S(1)} custom-call(s32[3]{0:T(128)S(1)} %pad_add_fusion.refs_0_, bf16[256,6144]{1,0:T(8,128)(2,1)S(1)} %bitcast.61, bf16[2,2,256,256]{3,2,1,0:T(8,128)(2,1)S(1)} %shard_map.67.refs_2_), custom_call_target="tpu_custom_call" | custom-call | tf_op jit(solution)/shard_map/pallas_call | solution.py:210
  88.9 2.1 %shard_map.69 = bf16[4,768,256]{2,1,0:T(8,128)(2,1)S(1)} custom-call(s32[3]{0:T(128)S(1)} %pad_add_fusion.refs_0_, bf16[256,6144]{1,0:T(8,128)(2,1)S(1)} %bitcast.62, bf16[2,2,256,256]{3,2,1,0:T(8,128)(2,1)S(1)} %shard_map.67.refs_2_), custom_call_target="tpu_custom_call" | custom-call | tf_op jit(solution)/shard_map/pallas_call | solution.py:210
  91.0 2.2 %shard_map.71 = (bf16[2,768,256]{2,1,0:T(8,128)(2,1)S(1)}, bf16[2,768,256]{2,1,0:T(8,128)(2,1)S(1)}) custom-call(s32[3]{0:T(128)S(1)} %pad_add_fusion.refs_0_, bf16[256,6144]{1,0:T(8,128)(2,1)S(1)} %bitcast.63, bf16[2,2,256,256]{3,2,1,0:T(8,128)(2,1)S(1)} %shard_map.67.refs_2_, bf16[4,768,256]{2,1,0:T(8,128)(2,1)S(1)} %collective-permute-done.23.refs_3_), custom_call_target="tpu_custom_call" | custom-call | tf_op jit(solution)/shard_map/pallas_call | solution.py:210
  95.9 5.4 %collective-permute-done.24.refs_3_ = bf16[4,768,256]{2,1,0:T(8,128)(2,1)S(1)} collective-permute-done((bf16[4,768,256]{2,1,0:T(8,128)(2,1)S(1)}, bf16[4,768,256]{2,1,0:T(8,128)(2,1)S(1)}, u32[]{:S(2)}, u32[]{:S(2)}) %collective-permute-start.24) | collective-permute-done | bytes 1572896 | tf_op jit(solution)/shard_map/ppermute | solution.py:50
  101.3 2.3 %shard_map.74 = (bf16[2,768,256]{2,1,0:T(8,128)(2,1)S(1)}, bf16[2,768,256]{2,1,0:T(8,128)(2,1)S(1)}) custom-call(s32[3]{0:T(128)S(1)} %pad_add_fusion.refs_0_, bf16[256,6144]{1,0:T(8,128)(2,1)S(1)} %bitcast.64, bf16[2,2,256,256]{3,2,1,0:T(8,128)(2,1)S(1)} %shard_map.67.refs_2_, bf16[4,768,256]{2,1,0:T(8,128)(2,1)S(1)} %collective-permute-done.24.refs_3_), custom_call_target="tpu_custom_call" | custom-call | tf_op jit(solution)/shard_map/pallas_call | solution.py:210
  104.5 2.4 %collective-permute-start.32 = (bf16[2,768,256]{2,1,0:T(8,128)(2,1)S(1)}, bf16[2,768,256]{2,1,0:T(8,128)(2,1)S(1)}, u32[]{:S(2)}, u32[]{:S(2)}) collective-permute-start(bf16[2,768,256]{2,1,0:T(8,128)(2,1)S(1)} %get-tuple-element.78), channel_id=1, source_target_pairs={{48,0},{49,1},{50,2},{51,3},{52,4},{53,5},{54,6},{55,7},{56,8},{57... | collective-permute-start | bytes 2359304 | tf_op jit(solution)/shard_map/ppermute | solution.py:34
  108.0 2.4 %shard_map.72 = (bf16[1,768,256]{2,1,0:T(8,128)(2,1)S(1)}, bf16[1,768,256]{2,1,0:T(8,128)(2,1)S(1)}, bf16[1,768,256]{2,1,0:T(8,128)(2,1)S(1)}, bf16[1,768,256]{2,1,0:T(8,128)(2,1)S(1)}) custom-call(s32[3]{0:T(128)S(1)} %pad_add_fusion.refs_0_, bf16[256,6144]{1,0:T(8,128)(2,1)S(1)} %bitcast.65, bf16[2,2,256,256]{3,2,1,0:T(8,128)(2,1)S(1)} %shard_map.67.refs_2_, ...), custom_call_target="tpu_custom_call" | custom-call | tf_op jit(solution)/shard_map/pallas_call | solution.py:210
  112.5 2.2 %shard_map.73 = (bf16[2,768,256]{2,1,0:T(8,128)(2,1)S(1)}, bf16[2,768,256]{2,1,0:T(8,128)(2,1)S(1)}) custom-call(s32[3]{0:T(128)S(1)} %pad_add_fusion.refs_0_, bf16[256,6144]{1,0:T(8,128)(2,1)S(1)} %bitcast.66, bf16[2,2,256,256]{3,2,1,0:T(8,128)(2,1)S(1)} %shard_map.67.refs_2_, bf16[8,768,256]{2,1,0:T(8,128)(2,1)S(1)} %collective-permute-done.25.refs_3_), custom_call_target="tpu_custom_call" | custom-call | tf_op jit(solution)/shard_map/pallas_call | solution.py:210
  114.7 2.1 %collective-permute-done.29 = bf16[2,768,256]{2,1,0:T(8,128)(2,1)S(1)} collective-permute-done((bf16[2,768,256]{2,1,0:T(8,128)(2,1)S(1)}, bf16[2,768,256]{2,1,0:T(8,128)(2,1)S(1)}, u32[]{:S(2)}, u32[]{:S(2)}) %collective-permute-start.29) | collective-permute-done | bytes 786464 | tf_op jit(solution)/shard_map/ppermute | solution.py:34
  118.0 2.6 %collective-permute-done.30 = bf16[1,768,256]{2,1,0:T(8,128)(2,1)S(1)} collective-permute-done((bf16[1,768,256]{2,1,0:T(8,128)(2,1)S(1)}, bf16[1,768,256]{2,1,0:T(8,128)(2,1)S(1)}, u32[]{:S(2)}, u32[]{:S(2)}) %collective-permute-start.30) | collective-permute-done | bytes 393248 | tf_op jit(solution)/shard_map/ppermute | solution.py:34
  126.5 2.5 %collective-permute-start.36 = (bf16[768,256]{1,0:T(8,128)(2,1)S(1)}, bf16[768,256]{1,0:T(8,128)(2,1)S(1)}, u32[]{:S(2)}, u32[]{:S(2)}) collective-permute-start(bf16[768,256]{1,0:T(8,128)(2,1)S(1)} %get-tuple-element.82), channel_id=1, source_target_pairs={{8,0},{9,1},{10,2},{11,3},{12,4},{13,5},{14,6},{15,7},{0,8},{1,9},... | collective-permute-start | bytes 1179656 | tf_op jit(solution)/shard_map/ppermute | solution.py:38
  129.7 5.0 %collective-permute-done.34 = bf16[768,256]{1,0:T(8,128)(2,1)S(1)} collective-permute-done((bf16[768,256]{1,0:T(8,128)(2,1)S(1)}, bf16[768,256]{1,0:T(8,128)(2,1)S(1)}, u32[]{:S(2)}, u32[]{:S(2)}) %collective-permute-start.34) | collective-permute-done | bytes 393248 | tf_op jit(solution)/shard_map/ppermute | solution.py:38
  134.6 4.4 %collective-permute-done.36 = bf16[768,256]{1,0:T(8,128)(2,1)S(1)} collective-permute-done((bf16[768,256]{1,0:T(8,128)(2,1)S(1)}, bf16[768,256]{1,0:T(8,128)(2,1)S(1)}, u32[]{:S(2)}, u32[]{:S(2)}) %collective-permute-start.36) | collective-permute-done | bytes 393248 | tf_op jit(solution)/shard_map/ppermute | solution.py:38
  142.0 4.2 %collective-permute-done.37 = bf16[4,96,256]{2,1,0:T(8,128)(2,1)S(1)} collective-permute-done((bf16[4,96,256]{2,1,0:T(8,128)(2,1)S(1)}, bf16[4,96,256]{2,1,0:T(8,128)(2,1)S(1)}, u32[]{:S(2)}, u32[]{:S(2)}) %collective-permute-start.37) | collective-permute-done | bytes 196640 | tf_op jit(solution)/shard_map/ppermute | solution.py:46
  146.3 4.1 %collective-permute-start.38 = (bf16[96,256]{1,0:T(8,128)(2,1)S(1)}, bf16[96,256]{1,0:T(8,128)(2,1)S(1)}, u32[]{:S(2)}, u32[]{:S(2)}) collective-permute-start(bf16[96,256]{1,0:T(8,128)(2,1)S(1)} %get-tuple-element.85), channel_id=1, source_target_pairs={{4,0},{5,1},{6,2},{7,3},{0,4},{1,5},{2,6},{3,7},{12,8},{13,9},{14,... | collective-permute-start | bytes 147464 | tf_op jit(solution)/shard_map/ppermute | solution.py:42
  151.1 3.5 %collective-permute-start.40 = (bf16[96,256]{1,0:T(8,128)(2,1)S(1)}, bf16[96,256]{1,0:T(8,128)(2,1)S(1)}, u32[]{:S(2)}, u32[]{:S(2)}) collective-permute-start(bf16[96,256]{1,0:T(8,128)(2,1)S(1)} %get-tuple-element.86), channel_id=1, source_target_pairs={{2,0},{3,1},{4,2},{5,3},{6,4},{7,5},{0,6},{1,7},{10,8},{11,9},{12,... | collective-permute-start | bytes 147464 | tf_op jit(solution)/shard_map/ppermute | solution.py:42
  154.6 2.2 %collective-permute-done.39 = bf16[96,256]{1,0:T(8,128)(2,1)S(1)} collective-permute-done((bf16[96,256]{1,0:T(8,128)(2,1)S(1)}, bf16[96,256]{1,0:T(8,128)(2,1)S(1)}, u32[]{:S(2)}, u32[]{:S(2)}) %collective-permute-start.39) | collective-permute-done | bytes 49184 | tf_op jit(solution)/shard_map/ppermute | solution.py:42
  (89 shorter events, 41.7 us)
Async XLA Ops:
  0.0 11.0 %collective-permute-start = (bf16[96,256]{1,0:T(8,128)(2,1)}, bf16[96,256]{1,0:T(8,128)(2,1)S(1)}, u32[]{:S(2)}, u32[]{:S(2)}) collective-permute-start(bf16[96,256]{1,0:T(8,128)(2,1)} %bitcast.85), channel_id=1, source_target_pairs={{2,0},{3,1},{4,2},{5,3},{6,4},{7,5},{0,6},{1,7},{10,8},{11,9},{12,... | collective-permute-start | bytes 147464 | tf_op jit(solution)/shard_map/ppermute | solution.py:42
  6.4 8.5 %collective-permute-start.1 = (bf16[96,256]{1,0:T(8,128)(2,1)}, bf16[96,256]{1,0:T(8,128)(2,1)S(1)}, u32[]{:S(2)}, u32[]{:S(2)}) collective-permute-start(bf16[96,256]{1,0:T(8,128)(2,1)} %bitcast.86), channel_id=1, source_target_pairs={{4,0},{5,1},{6,2},{7,3},{0,4},{1,5},{2,6},{3,7},{12,8},{13,9},{14,... | collective-permute-start | bytes 147464 | tf_op jit(solution)/shard_map/ppermute | solution.py:42
  7.4 7.5 %collective-permute-start.2 = (bf16[96,256]{1,0:T(8,128)(2,1)}, bf16[96,256]{1,0:T(8,128)(2,1)S(1)}, u32[]{:S(2)}, u32[]{:S(2)}) collective-permute-start(bf16[96,256]{1,0:T(8,128)(2,1)} %bitcast.87), channel_id=1, source_target_pairs={{6,0},{7,1},{0,2},{1,3},{2,4},{3,5},{4,6},{5,7},{14,8},{15,9},{8,1... | collective-permute-start | bytes 147464 | tf_op jit(solution)/shard_map/ppermute | solution.py:42
  20.8 13.3 %collective-permute-start.4 = (bf16[768,256]{1,0:T(8,128)(2,1)S(1)}, bf16[768,256]{1,0:T(8,128)(2,1)S(1)}, u32[]{:S(2)}, u32[]{:S(2)}) collective-permute-start(bf16[768,256]{1,0:T(8,128)(2,1)S(1)} %bitcast.79), channel_id=1, source_target_pairs={{128,0},{129,1},{130,2},{131,3},{132,4},{133,5},{134,6},{135,7},{1... | collective-permute-start | bytes 1179656 | tf_op jit(solution)/shard_map/ppermute | solution.py:38
  21.6 12.5 %collective-permute-start.5 = (bf16[768,256]{1,0:T(8,128)(2,1)S(1)}, bf16[768,256]{1,0:T(8,128)(2,1)S(1)}, u32[]{:S(2)}, u32[]{:S(2)}) collective-permute-start(bf16[768,256]{1,0:T(8,128)(2,1)S(1)} %bitcast.80), channel_id=1, source_target_pairs={{8,0},{9,1},{10,2},{11,3},{12,4},{13,5},{14,6},{15,7},{0,8},{1,9},... | collective-permute-start | bytes 1179656 | tf_op jit(solution)/shard_map/ppermute | solution.py:38
  22.5 12.4 %collective-permute-start.6 = (bf16[768,256]{1,0:T(8,128)(2,1)S(1)}, bf16[768,256]{1,0:T(8,128)(2,1)S(1)}, u32[]{:S(2)}, u32[]{:S(2)}) collective-permute-start(bf16[768,256]{1,0:T(8,128)(2,1)S(1)} %bitcast.81), channel_id=1, source_target_pairs={{136,0},{137,1},{138,2},{139,3},{140,4},{141,5},{142,6},{143,7},{1... | collective-permute-start | bytes 1179656 | tf_op jit(solution)/shard_map/ppermute | solution.py:38
  36.2 8.9 %collective-permute-start.13 = (bf16[2,768,256]{2,1,0:T(8,128)(2,1)}, bf16[2,768,256]{2,1,0:T(8,128)(2,1)}, u32[]{:S(2)}, u32[]{:S(2)}) collective-permute-start(bf16[2,768,256]{2,1,0:T(8,128)(2,1)} %get-tuple-element.43.refs_5_), channel_id=1, source_target_pairs={{0,64},{64,0},{1,65},{65,1},{2,66},{66,2},{3,67},{67,3},{4,68},{68... | collective-permute-start | bytes 2359304 | tf_op jit(solution)/shard_map/ppermute | solution.py:50
  36.2 12.2 %collective-permute-start.14 = (bf16[2,768,256]{2,1,0:T(8,128)(2,1)}, bf16[2,768,256]{2,1,0:T(8,128)(2,1)}, u32[]{:S(2)}, u32[]{:S(2)}) collective-permute-start(bf16[2,768,256]{2,1,0:T(8,128)(2,1)} %get-tuple-element.44.refs_6_), channel_id=1, source_target_pairs={{0,64},{64,0},{1,65},{65,1},{2,66},{66,2},{3,67},{67,3},{4,68},{68... | collective-permute-start | bytes 2359304 | tf_op jit(solution)/shard_map/ppermute | solution.py:50
  36.7 18.8 %collective-permute-start.11 = (bf16[2,768,256]{2,1,0:T(8,128)(2,1)}, bf16[2,768,256]{2,1,0:T(8,128)(2,1)}, u32[]{:S(2)}, u32[]{:S(2)}) collective-permute-start(bf16[2,768,256]{2,1,0:T(8,128)(2,1)} %get-tuple-element.44.refs_6_), channel_id=1, source_target_pairs={{16,0},{17,1},{18,2},{19,3},{20,4},{21,5},{22,6},{23,7},{24,8},{25... | collective-permute-start | bytes 2359304 | tf_op jit(solution)/shard_map/ppermute | solution.py:34
  37.6 18.0 %collective-permute-start.12 = (bf16[2,768,256]{2,1,0:T(8,128)(2,1)}, bf16[2,768,256]{2,1,0:T(8,128)(2,1)}, u32[]{:S(2)}, u32[]{:S(2)}) collective-permute-start(bf16[2,768,256]{2,1,0:T(8,128)(2,1)} %get-tuple-element.43.refs_5_), channel_id=1, source_target_pairs={{48,0},{49,1},{50,2},{51,3},{52,4},{53,5},{54,6},{55,7},{56,8},{57... | collective-permute-start | bytes 2359304 | tf_op jit(solution)/shard_map/ppermute | solution.py:34
  45.1 13.9 %collective-permute-start.7 = (bf16[2,768,256]{2,1,0:T(8,128)(2,1)}, bf16[2,768,256]{2,1,0:T(8,128)(2,1)S(1)}, u32[]{:S(2)}, u32[]{:S(2)}) collective-permute-start(bf16[2,768,256]{2,1,0:T(8,128)(2,1)} %get-tuple-element.43.refs_5_), channel_id=1, source_target_pairs={{16,0},{17,1},{18,2},{19,3},{20,4},{21,5},{22,6},{23,7},{24,8},{25... | collective-permute-start | bytes 2359304 | tf_op jit(solution)/shard_map/ppermute | solution.py:34
  45.2 15.9 %collective-permute-start.9 = (bf16[2,768,256]{2,1,0:T(8,128)(2,1)}, bf16[2,768,256]{2,1,0:T(8,128)(2,1)S(1)}, u32[]{:S(2)}, u32[]{:S(2)}) collective-permute-start(bf16[2,768,256]{2,1,0:T(8,128)(2,1)} %get-tuple-element.44.refs_6_), channel_id=1, source_target_pairs={{48,0},{49,1},{50,2},{51,3},{52,4},{53,5},{54,6},{55,7},{56,8},{57... | collective-permute-start | bytes 2359304 | tf_op jit(solution)/shard_map/ppermute | solution.py:34
  55.6 6.4 %collective-permute-start.19 = (bf16[2,768,256]{2,1,0:T(8,128)(2,1)}, bf16[2,768,256]{2,1,0:T(8,128)(2,1)S(1)}, u32[]{:S(2)}, u32[]{:S(2)}) collective-permute-start(bf16[2,768,256]{2,1,0:T(8,128)(2,1)} %collective-permute-done.11.refs_7_), channel_id=1, source_target_pairs={{0,64},{64,0},{1,65},{65,1},{2,66},{66,2},{3,67},{67,3},{4,68},{68... | collective-permute-start | bytes 2359304 | tf_op jit(solution)/shard_map/ppermute | solution.py:50
  61.2 12.0 %collective-permute-start.10 = (bf16[2,768,256]{2,1,0:T(8,128)(2,1)S(1)}, bf16[2,768,256]{2,1,0:T(8,128)(2,1)S(1)}, u32[]{:S(2)}, u32[]{:S(2)}) collective-permute-start(bf16[2,768,256]{2,1,0:T(8,128)(2,1)S(1)} %collective-permute-done.9.refs_6_), channel_id=1, source_target_pairs={{48,0},{49,1},{50,2},{51,3},{52,4},{53,5},{54,6},{55,7},{56,8},{57... | collective-permute-start | bytes 2359304 | tf_op jit(solution)/shard_map/ppermute | solution.py:34
  61.9 13.2 %collective-permute-start.8 = (bf16[2,768,256]{2,1,0:T(8,128)(2,1)S(1)}, bf16[2,768,256]{2,1,0:T(8,128)(2,1)S(1)}, u32[]{:S(2)}, u32[]{:S(2)}) collective-permute-start(bf16[2,768,256]{2,1,0:T(8,128)(2,1)S(1)} %collective-permute-done.7.refs_5_), channel_id=1, source_target_pairs={{16,0},{17,1},{18,2},{19,3},{20,4},{21,5},{22,6},{23,7},{24,8},{25... | collective-permute-start | bytes 2359304 | tf_op jit(solution)/shard_map/ppermute | solution.py:34
  84.7 6.3 %collective-permute-start.23 = (bf16[4,768,256]{2,1,0:T(8,128)(2,1)S(1)}, bf16[4,768,256]{2,1,0:T(8,128)(2,1)S(1)}, u32[]{:S(2)}, u32[]{:S(2)}) collective-permute-start(bf16[4,768,256]{2,1,0:T(8,128)(2,1)S(1)} %shard_map.68), channel_id=1, source_target_pairs={{0,64},{64,0},{1,65},{65,1},{2,66},{66,2},{3,67},{67,3},{4,68},{68... | collective-permute-start | bytes 4718600 | tf_op jit(solution)/shard_map/ppermute | solution.py:50
  93.3 14.7 %collective-permute-start.25 = (bf16[8,768,256]{2,1,0:T(8,128)(2,1)S(1)}, bf16[8,768,256]{2,1,0:T(8,128)(2,1)S(1)}, u32[]{:S(2)}, u32[]{:S(2)}) collective-permute-start(bf16[8,768,256]{2,1,0:T(8,128)(2,1)S(1)} %shard_map.70), channel_id=1, source_target_pairs={{0,64},{64,0},{1,65},{65,1},{2,66},{66,2},{3,67},{67,3},{4,68},{68... | collective-permute-start | bytes 9437192 | tf_op jit(solution)/shard_map/ppermute | solution.py:50
  93.5 7.8 %collective-permute-start.24 = (bf16[4,768,256]{2,1,0:T(8,128)(2,1)S(1)}, bf16[4,768,256]{2,1,0:T(8,128)(2,1)S(1)}, u32[]{:S(2)}, u32[]{:S(2)}) collective-permute-start(bf16[4,768,256]{2,1,0:T(8,128)(2,1)S(1)} %shard_map.69), channel_id=1, source_target_pairs={{0,64},{64,0},{1,65},{65,1},{2,66},{66,2},{3,67},{67,3},{4,68},{68... | collective-permute-start | bytes 4718600 | tf_op jit(solution)/shard_map/ppermute | solution.py:50
  93.9 13.0 %collective-permute-start.26 = (bf16[2,768,256]{2,1,0:T(8,128)(2,1)S(1)}, bf16[2,768,256]{2,1,0:T(8,128)(2,1)S(1)}, u32[]{:S(2)}, u32[]{:S(2)}) collective-permute-start(bf16[2,768,256]{2,1,0:T(8,128)(2,1)S(1)} %get-tuple-element.65), channel_id=1, source_target_pairs={{48,0},{49,1},{50,2},{51,3},{52,4},{53,5},{54,6},{55,7},{56,8},{57... | collective-permute-start | bytes 2359304 | tf_op jit(solution)/shard_map/ppermute | solution.py:34
  94.8 13.2 %collective-permute-start.27 = (bf16[2,768,256]{2,1,0:T(8,128)(2,1)S(1)}, bf16[2,768,256]{2,1,0:T(8,128)(2,1)S(1)}, u32[]{:S(2)}, u32[]{:S(2)}) collective-permute-start(bf16[2,768,256]{2,1,0:T(8,128)(2,1)S(1)} %get-tuple-element.66), channel_id=1, source_target_pairs={{16,0},{17,1},{18,2},{19,3},{20,4},{21,5},{22,6},{23,7},{24,8},{25... | collective-permute-start | bytes 2359304 | tf_op jit(solution)/shard_map/ppermute | solution.py:34
  103.6 13.3 %collective-permute-start.29 = (bf16[2,768,256]{2,1,0:T(8,128)(2,1)S(1)}, bf16[2,768,256]{2,1,0:T(8,128)(2,1)S(1)}, u32[]{:S(2)}, u32[]{:S(2)}) collective-permute-start(bf16[2,768,256]{2,1,0:T(8,128)(2,1)S(1)} %get-tuple-element.75), channel_id=1, source_target_pairs={{16,0},{17,1},{18,2},{19,3},{20,4},{21,5},{22,6},{23,7},{24,8},{25... | collective-permute-start | bytes 2359304 | tf_op jit(solution)/shard_map/ppermute | solution.py:34
  104.5 19.0 %collective-permute-start.32 = (bf16[2,768,256]{2,1,0:T(8,128)(2,1)S(1)}, bf16[2,768,256]{2,1,0:T(8,128)(2,1)S(1)}, u32[]{:S(2)}, u32[]{:S(2)}) collective-permute-start(bf16[2,768,256]{2,1,0:T(8,128)(2,1)S(1)} %get-tuple-element.78), channel_id=1, source_target_pairs={{48,0},{49,1},{50,2},{51,3},{52,4},{53,5},{54,6},{55,7},{56,8},{57... | collective-permute-start | bytes 2359304 | tf_op jit(solution)/shard_map/ppermute | solution.py:34
  110.4 10.3 %collective-permute-start.30 = (bf16[1,768,256]{2,1,0:T(8,128)(2,1)S(1)}, bf16[1,768,256]{2,1,0:T(8,128)(2,1)S(1)}, u32[]{:S(2)}, u32[]{:S(2)}) collective-permute-start(bf16[1,768,256]{2,1,0:T(8,128)(2,1)S(1)} %get-tuple-element.76), channel_id=1, source_target_pairs={{48,0},{49,1},{50,2},{51,3},{52,4},{53,5},{54,6},{55,7},{56,8},{57... | collective-permute-start | bytes 1179656 | tf_op jit(solution)/shard_map/ppermute | solution.py:34
  110.5 13.0 %collective-permute-start.33 = (bf16[1,768,256]{2,1,0:T(8,128)(2,1)S(1)}, bf16[1,768,256]{2,1,0:T(8,128)(2,1)S(1)}, u32[]{:S(2)}, u32[]{:S(2)}) collective-permute-start(bf16[1,768,256]{2,1,0:T(8,128)(2,1)S(1)} %get-tuple-element.79), channel_id=1, source_target_pairs={{16,0},{17,1},{18,2},{19,3},{20,4},{21,5},{22,6},{23,7},{24,8},{25... | collective-permute-start | bytes 1179656 | tf_op jit(solution)/shard_map/ppermute | solution.py:34
  112.5 12.8 %collective-permute-start.35 = (bf16[1,768,256]{2,1,0:T(8,128)(2,1)S(1)}, bf16[1,768,256]{2,1,0:T(8,128)(2,1)S(1)}, u32[]{:S(2)}, u32[]{:S(2)}) collective-permute-start(bf16[1,768,256]{2,1,0:T(8,128)(2,1)S(1)} %get-tuple-element.80), channel_id=1, source_target_pairs={{16,0},{17,1},{18,2},{19,3},{20,4},{21,5},{22,6},{23,7},{24,8},{25... | collective-permute-start | bytes 1179656 | tf_op jit(solution)/shard_map/ppermute | solution.py:34
  116.8 12.2 %collective-permute-start.28 = (bf16[1,768,256]{2,1,0:T(8,128)(2,1)S(1)}, bf16[1,768,256]{2,1,0:T(8,128)(2,1)}, u32[]{:S(2)}, u32[]{:S(2)}) collective-permute-start(bf16[1,768,256]{2,1,0:T(8,128)(2,1)S(1)} %get-tuple-element.73), channel_id=1, source_target_pairs={{48,0},{49,1},{50,2},{51,3},{52,4},{53,5},{54,6},{55,7},{56,8},{57... | collective-permute-start | bytes 1179656 | tf_op jit(solution)/shard_map/ppermute | solution.py:34
  121.6 8.1 %collective-permute-start.31 = (bf16[768,256]{1,0:T(8,128)(2,1)}, bf16[768,256]{1,0:T(8,128)(2,1)}, u32[]{:S(2)}, u32[]{:S(2)}) collective-permute-start(bf16[768,256]{1,0:T(8,128)(2,1)} %fusion.4), channel_id=1, source_target_pairs={{136,0},{137,1},{138,2},{139,3},{140,4},{141,5},{142,6},{143,7},{1... | collective-permute-start | bytes 1179656 | tf_op jit(solution)/shard_map/ppermute | solution.py:38
  125.6 9.1 %collective-permute-start.34 = (bf16[768,256]{1,0:T(8,128)(2,1)S(1)}, bf16[768,256]{1,0:T(8,128)(2,1)S(1)}, u32[]{:S(2)}, u32[]{:S(2)}) collective-permute-start(bf16[768,256]{1,0:T(8,128)(2,1)S(1)} %get-tuple-element.81), channel_id=1, source_target_pairs={{128,0},{129,1},{130,2},{131,3},{132,4},{133,5},{134,6},{135,7},{1... | collective-permute-start | bytes 1179656 | tf_op jit(solution)/shard_map/ppermute | solution.py:38
  126.5 12.5 %collective-permute-start.36 = (bf16[768,256]{1,0:T(8,128)(2,1)S(1)}, bf16[768,256]{1,0:T(8,128)(2,1)S(1)}, u32[]{:S(2)}, u32[]{:S(2)}) collective-permute-start(bf16[768,256]{1,0:T(8,128)(2,1)S(1)} %get-tuple-element.82), channel_id=1, source_target_pairs={{8,0},{9,1},{10,2},{11,3},{12,4},{13,5},{14,6},{15,7},{0,8},{1,9},... | collective-permute-start | bytes 1179656 | tf_op jit(solution)/shard_map/ppermute | solution.py:38
  146.3 8.3 %collective-permute-start.38 = (bf16[96,256]{1,0:T(8,128)(2,1)S(1)}, bf16[96,256]{1,0:T(8,128)(2,1)S(1)}, u32[]{:S(2)}, u32[]{:S(2)}) collective-permute-start(bf16[96,256]{1,0:T(8,128)(2,1)S(1)} %get-tuple-element.85), channel_id=1, source_target_pairs={{4,0},{5,1},{6,2},{7,3},{0,4},{1,5},{2,6},{3,7},{12,8},{13,9},{14,... | collective-permute-start | bytes 147464 | tf_op jit(solution)/shard_map/ppermute | solution.py:42
  150.5 6.3 %collective-permute-start.39 = (bf16[96,256]{1,0:T(8,128)(2,1)S(1)}, bf16[96,256]{1,0:T(8,128)(2,1)S(1)}, u32[]{:S(2)}, u32[]{:S(2)}) collective-permute-start(bf16[96,256]{1,0:T(8,128)(2,1)S(1)} %get-tuple-element.87), channel_id=1, source_target_pairs={{6,0},{7,1},{0,2},{1,3},{2,4},{3,5},{4,6},{5,7},{14,8},{15,9},{8,1... | collective-permute-start | bytes 147464 | tf_op jit(solution)/shard_map/ppermute | solution.py:42
  151.1 5.8 %collective-permute-start.40 = (bf16[96,256]{1,0:T(8,128)(2,1)S(1)}, bf16[96,256]{1,0:T(8,128)(2,1)S(1)}, u32[]{:S(2)}, u32[]{:S(2)}) collective-permute-start(bf16[96,256]{1,0:T(8,128)(2,1)S(1)} %get-tuple-element.86), channel_id=1, source_target_pairs={{2,0},{3,1},{4,2},{5,3},{6,4},{7,5},{0,6},{1,7},{10,8},{11,9},{12,... | collective-permute-start | bytes 147464 | tf_op jit(solution)/shard_map/ppermute | solution.py:42
  (14 other events, 167.8 us)

commit v4 on v3

--- a/solution.py
+++ b/solution.py
@@ -279,12 +279,14 @@
     steps = {s: from_minor(start, s) for s in (1, 2, 3)}
     own = join(start, steps[1], steps[2], steps[3])
 
+    *own, w = lax.optimization_barrier((*own, w))
+
     through = [from_major(own[0], 1), from_major(own[1], 3)]
     direct = [from_major(own[1], 1), from_major(own[0], 3)]
     far = [from_major(through[0], 1), from_major(through[1], 3)]
     swap = lambda vs: [sibling(v) for v in vs]
     sums = hidden_of(at, wg, wu, OWN, own, swap(own))
-    *direct, sums, w = lax.optimization_barrier((*direct, sums, w))
+    *direct, sums = lax.optimization_barrier((*direct, sums))
     near = [*through, *direct]
     sums = hidden_of(at, wg, wu, THROUGH + DIRECT, near, swap(near), sums)
     *far, sums = lax.optimization_barrier((*far, sums))

time: 160 us -> 159 us (level); the launches traced: 158 us -> 158 us
  starting transfers between devices: 56.6 us -> 53.8 us
  waiting for transfers between devices: 59 us -> 60.6 us
    ppermute x6, waiting for transfers between devices: 20.2 us -> 10.2 us  [from_minor(): return lax.ppermute(v, AXES, shift_perm(False, s))]
    ppermute x14, waiting for transfers between devices: 10.5 us -> 19.2 us  [from_major(): return lax.ppermute(v, AXES, shift_perm(True, s))]
    ppermute x1, waiting for transfers between devices: 3.14 us -> 8.4 us  [body(): other = lax.ppermute(near, 'ylo', [(0, 1), (1, 0)])]
    ppermute x12, starting transfers between devices: 7.89 us -> 3.18 us  [sibling(): return lax.ppermute(v, 'core', [(0, 1), (1, 0)])]
    ppermute x14, starting transfers between devices: 17.2 us -> 20.2 us  [from_major(): return lax.ppermute(v, AXES, shift_perm(True, s))]
    ppermute x12, waiting for transfers between devices: 10.5 us -> 8.24 us  [sibling(): return lax.ppermute(v, 'core', [(0, 1), (1, 0)])]
  transfers between devices with their start and end apart: 41 -> 41, of which waited for: 22 -> 18; matrix products, arithmetic and copies ran while one was open for 1% -> 2% of each run, Pallas kernels for 17% -> 16%
where the time goes in v4:
time: 159 us; the launch traced here: 158 us
  waiting for transfers between devices  60.6 us (38%)
  starting transfers between devices  53.8 us (34%)
  Pallas kernels  36.6 us (23%)
  other arithmetic  4.18 us (3%)
  local copies, waits for them, and re-layouts  2.81 us (2%)
    ppermute x14, starting transfers between devices, from_major(): return lax.ppermute(v, AXES, shift_perm(True, s))  20.2 us
    ppermute x14, waiting for transfers between devices, from_major(): return lax.ppermute(v, AXES, shift_perm(True, s))  19.2 us
    ppermute x6, starting transfers between devices, from_z(): return lax.ppermute(v, 'z', [((i + s) % NZ, i) for i in range(NZ)])  18.4 us
    pallas_call x7, Pallas kernels, down_of(): pl.pallas_call(kernel, grid_spec=pltpu.PrefetchScalarGridSpec(num_scalar_...  17.1 us
    pallas_call x3, Pallas kernels, hidden_of(): pl.pallas_call(kernel, grid_spec=pltpu.PrefetchScalarGridSpec(num_scalar_...  17 us
    ppermute x6, waiting for transfers between devices, from_minor(): return lax.ppermute(v, AXES, shift_perm(False, s))  10.2 us
    ppermute x6, starting transfers between devices, from_minor(): return lax.ppermute(v, AXES, shift_perm(False, s))  8.74 us
    ppermute x2, waiting for transfers between devices, z_pair(): return lax.ppermute(v, 'z', [(i, i ^ 1) for i in range(NZ)])  8.49 us
  transfers between devices with their start and end apart: 41, of which 18 were waited for; matrix products, arithmetic and copies ran while one was open for 2% of the time, Pallas kernels for 16%

profile of v4, /device:TPU:30, one launch (start us, length us, event | category | flops | bytes accessed | tf_op | source)
XLA Modules:
  0.0 158.3 jit_solution(380588907307517553)
XLA Ops:
  0.0 6.4 %collective-permute-start = (bf16[96,256]{1,0:T(8,128)(2,1)}, bf16[96,256]{1,0:T(8,128)(2,1)S(1)}, u32[]{:S(2)}, u32[]{:S(2)}) collective-permute-start(bf16[96,256]{1,0:T(8,128)(2,1)} %bitcast.85), channel_id=1, source_target_pairs={{2,0},{3,1},{4,2},{5,3},{6,4},{7,5},{0,6},{1,7},{10,8},{11,9},{12,... | collective-permute-start | bytes 147464 | tf_op jit(solution)/shard_map/ppermute | solution.py:42
  7.4 2.8 %collective-permute-start.2 = (bf16[96,256]{1,0:T(8,128)(2,1)}, bf16[96,256]{1,0:T(8,128)(2,1)S(1)}, u32[]{:S(2)}, u32[]{:S(2)}) collective-permute-start(bf16[96,256]{1,0:T(8,128)(2,1)} %bitcast.87), channel_id=1, source_target_pairs={{6,0},{7,1},{0,2},{1,3},{2,4},{3,5},{4,6},{5,7},{14,8},{15,9},{8,1... | collective-permute-start | bytes 147464 | tf_op jit(solution)/shard_map/ppermute | solution.py:42
  11.1 3.9 %collective-permute-done.1 = bf16[96,256]{1,0:T(8,128)(2,1)S(1)} collective-permute-done((bf16[96,256]{1,0:T(8,128)(2,1)}, bf16[96,256]{1,0:T(8,128)(2,1)S(1)}, u32[]{:S(2)}, u32[]{:S(2)}) %collective-permute-start.1) | collective-permute-done | bytes 49184 | tf_op jit(solution)/shard_map/ppermute | solution.py:42
  16.5 4.2 %collective-permute-done.3 = bf16[4,96,256]{2,1,0:T(8,128)(2,1)S(1)} collective-permute-done((bf16[4,96,256]{2,1,0:T(8,128)(2,1)S(1)}, bf16[4,96,256]{2,1,0:T(8,128)(2,1)S(1)}, u32[]{:S(2)}, u32[]{:S(2)}) %collective-permute-start.3) | collective-permute-done | bytes 196640 | tf_op jit(solution)/shard_map/ppermute | solution.py:46
  22.5 2.2 %collective-permute-start.6 = (bf16[768,256]{1,0:T(8,128)(2,1)S(1)}, bf16[768,256]{1,0:T(8,128)(2,1)}, u32[]{:S(2)}, u32[]{:S(2)}) collective-permute-start(bf16[768,256]{1,0:T(8,128)(2,1)S(1)} %bitcast.81), channel_id=1, source_target_pairs={{136,0},{137,1},{138,2},{139,3},{140,4},{141,5},{142,6},{143,7},{1... | collective-permute-start | bytes 1179656 | tf_op jit(solution)/shard_map/ppermute | solution.py:38
  26.8 8.4 %collective-permute-done.8 = f32[2,4,256]{2,1,0:T(4,128)} collective-permute-done((f32[2,4,256]{2,1,0:T(4,128)}, f32[2,4,256]{2,1,0:T(4,128)}, u32[]{:S(2)}, u32[]{:S(2)}) %collective-permute-start.8) | collective-permute-done | bytes 8224 | tf_op jit(solution)/shard_map/ppermute | solution.py:275
  36.0 2.5 %shard_map.64 = (bf16[2,768,256]{2,1,0:T(8,128)(2,1)}, bf16[2,768,256]{2,1,0:T(8,128)(2,1)}) custom-call(bf16[768,256]{1,0:T(8,128)(2,1)S(1)} %bitcast.82, bf16[768,256]{1,0:T(8,128)(2,1)} %collective-permute-done.4.b, bf16[768,256]{1,0:T(8,128)(2,1)} %collective-permute-done.5.c, bf16[768,256]{1,0:T(8,128)(2,1)} %collective-permute-done.6.d), custom_call_target="tpu_custom_call" | custom-call | tf_op jit(solution)/shard_map/pallas_call | solution.py:228
  39.8 2.4 %collective-permute-start.14 = (bf16[2,768,256]{2,1,0:T(8,128)(2,1)}, bf16[2,768,256]{2,1,0:T(8,128)(2,1)}, u32[]{:S(2)}, u32[]{:S(2)}) collective-permute-start(bf16[2,768,256]{2,1,0:T(8,128)(2,1)} %get-tuple-element.47.refs_5_), channel_id=1, source_target_pairs={{48,0},{49,1},{50,2},{51,3},{52,4},{53,5},{54,6},{55,7},{56,8},{57... | collective-permute-start | bytes 2359304 | tf_op jit(solution)/shard_map/ppermute | solution.py:34
  42.3 3.2 %collective-permute-start.11 = (bf16[2,768,256]{2,1,0:T(8,128)(2,1)}, bf16[2,768,256]{2,1,0:T(8,128)(2,1)S(1)}, u32[]{:S(2)}, u32[]{:S(2)}) collective-permute-start(bf16[2,768,256]{2,1,0:T(8,128)(2,1)} %get-tuple-element.48.refs_6_), channel_id=1, source_target_pairs={{48,0},{49,1},{50,2},{51,3},{52,4},{53,5},{54,6},{55,7},{56,8},{57... | collective-permute-start | bytes 2359304 | tf_op jit(solution)/shard_map/ppermute | solution.py:34
  47.4 5.2 %shard_map.65.refs_13_ = f32[2,2,2,256,256]{4,3,2,1,0:T(8,128)S(1)} custom-call(s32[3]{0:T(128)S(1)} %pad_add_fusion.refs_0_, bf16[6144,256]{1,0:T(8,128)(2,1)S(1)} %bitcast.67, bf16[6144,256]{1,0:T(8,128)(2,1)S(1)} %bitcast.73, bf16[6144,256]{1,0:T(8,128)(2,1)S(1)} %bitcast.68, bf16[6144,256]{1,0:T(8,128)(2,1)S(1)} %bitcast.74, ...), custom_call_target="tpu_custom_call" | custom-call | tf_op jit(solution)/shard_map/pallas_call | solution.py:149
  53.4 7.3 %collective-permute-done.9.refs_5_ = bf16[2,768,256]{2,1,0:T(8,128)(2,1)S(1)} collective-permute-done((bf16[2,768,256]{2,1,0:T(8,128)(2,1)}, bf16[2,768,256]{2,1,0:T(8,128)(2,1)S(1)}, u32[]{:S(2)}, u32[]{:S(2)}) %collective-permute-start.9) | collective-permute-done | bytes 786464 | tf_op jit(solution)/shard_map/ppermute | solution.py:34
  61.3 3.2 %collective-permute-start.12 = (bf16[2,768,256]{2,1,0:T(8,128)(2,1)S(1)}, bf16[2,768,256]{2,1,0:T(8,128)(2,1)S(1)}, u32[]{:S(2)}, u32[]{:S(2)}) collective-permute-start(bf16[2,768,256]{2,1,0:T(8,128)(2,1)S(1)} %collective-permute-done.11.refs_6_), channel_id=1, source_target_pairs={{48,0},{49,1},{50,2},{51,3},{52,4},{53,5},{54,6},{55,7},{56,8},{57... | collective-permute-start | bytes 2359304 | tf_op jit(solution)/shard_map/ppermute | solution.py:34
  64.5 8.1 %shard_map.66.refs_9_ = f32[2,2,2,256,256]{4,3,2,1,0:T(8,128)S(1)} custom-call(s32[3]{0:T(128)S(1)} %pad_add_fusion.refs_0_, bf16[6144,256]{1,0:T(8,128)(2,1)S(1)} %bitcast.69, bf16[6144,256]{1,0:T(8,128)(2,1)S(1)} %bitcast.75, bf16[6144,256]{1,0:T(8,128)(2,1)S(1)} %bitcast.70, bf16[6144,256]{1,0:T(8,128)(2,1)S(1)} %bitcast.76, ...), custom_call_target="tpu_custom_call" | custom-call | tf_op jit(solution)/shard_map/pallas_call | solution.py:149
  77.9 3.7 %shard_map.67.refs_2_ = bf16[2,2,256,256]{3,2,1,0:T(8,128)(2,1)S(1)} custom-call(s32[3]{0:T(128)S(1)} %pad_add_fusion.refs_0_, bf16[6144,256]{1,0:T(8,128)(2,1)S(1)} %bitcast.71, bf16[6144,256]{1,0:T(8,128)(2,1)S(1)} %bitcast.77, bf16[6144,256]{1,0:T(8,128)(2,1)S(1)} %bitcast.72, bf16[6144,256]{1,0:T(8,128)(2,1)S(1)} %bitcast.78, ...), custom_call_target="tpu_custom_call" | custom-call | tf_op jit(solution)/shard_map/pallas_call | solution.py:149
  81.7 2.1 %shard_map.68 = bf16[4,768,256]{2,1,0:T(8,128)(2,1)S(1)} custom-call(s32[3]{0:T(128)S(1)} %pad_add_fusion.refs_0_, bf16[256,6144]{1,0:T(8,128)(2,1)S(1)} %bitcast.60, bf16[2,2,256,256]{3,2,1,0:T(8,128)(2,1)S(1)} %shard_map.67.refs_2_), custom_call_target="tpu_custom_call" | custom-call | tf_op jit(solution)/shard_map/pallas_call | solution.py:210
  84.0 3.7 %shard_map.70 = bf16[8,768,256]{2,1,0:T(8,128)(2,1)S(1)} custom-call(s32[3]{0:T(128)S(1)} %pad_add_fusion.refs_0_, bf16[256,6144]{1,0:T(8,128)(2,1)S(1)} %bitcast.61, bf16[2,2,256,256]{3,2,1,0:T(8,128)(2,1)S(1)} %shard_map.67.refs_2_), custom_call_target="tpu_custom_call" | custom-call | tf_op jit(solution)/shard_map/pallas_call | solution.py:210
  87.7 2.1 %shard_map.69 = bf16[4,768,256]{2,1,0:T(8,128)(2,1)S(1)} custom-call(s32[3]{0:T(128)S(1)} %pad_add_fusion.refs_0_, bf16[256,6144]{1,0:T(8,128)(2,1)S(1)} %bitcast.62, bf16[2,2,256,256]{3,2,1,0:T(8,128)(2,1)S(1)} %shard_map.67.refs_2_), custom_call_target="tpu_custom_call" | custom-call | tf_op jit(solution)/shard_map/pallas_call | solution.py:210
  89.8 2.2 %shard_map.71 = (bf16[2,768,256]{2,1,0:T(8,128)(2,1)S(1)}, bf16[2,768,256]{2,1,0:T(8,128)(2,1)S(1)}) custom-call(s32[3]{0:T(128)S(1)} %pad_add_fusion.refs_0_, bf16[256,6144]{1,0:T(8,128)(2,1)S(1)} %bitcast.63, bf16[2,2,256,256]{3,2,1,0:T(8,128)(2,1)S(1)} %shard_map.67.refs_2_, bf16[4,768,256]{2,1,0:T(8,128)(2,1)S(1)} %collective-permute-done.23.refs_3_), custom_call_target="tpu_custom_call" | custom-call | tf_op jit(solution)/shard_map/pallas_call | solution.py:210
  92.7 3.3 %collective-permute-start.26 = (bf16[2,768,256]{2,1,0:T(8,128)(2,1)S(1)}, bf16[2,768,256]{2,1,0:T(8,128)(2,1)S(1)}, u32[]{:S(2)}, u32[]{:S(2)}) collective-permute-start(bf16[2,768,256]{2,1,0:T(8,128)(2,1)S(1)} %get-tuple-element.69), channel_id=1, source_target_pairs={{48,0},{49,1},{50,2},{51,3},{52,4},{53,5},{54,6},{55,7},{56,8},{57... | collective-permute-start | bytes 2359304 | tf_op jit(solution)/shard_map/ppermute | solution.py:34
  96.0 4.2 %collective-permute-done.24.refs_3_ = bf16[4,768,256]{2,1,0:T(8,128)(2,1)S(1)} collective-permute-done((bf16[4,768,256]{2,1,0:T(8,128)(2,1)S(1)}, bf16[4,768,256]{2,1,0:T(8,128)(2,1)S(1)}, u32[]{:S(2)}, u32[]{:S(2)}) %collective-permute-start.24) | collective-permute-done | bytes 1572896 | tf_op jit(solution)/shard_map/ppermute | solution.py:50
  100.1 2.3 %shard_map.74 = (bf16[2,768,256]{2,1,0:T(8,128)(2,1)S(1)}, bf16[2,768,256]{2,1,0:T(8,128)(2,1)S(1)}) custom-call(s32[3]{0:T(128)S(1)} %pad_add_fusion.refs_0_, bf16[256,6144]{1,0:T(8,128)(2,1)S(1)} %bitcast.64, bf16[2,2,256,256]{3,2,1,0:T(8,128)(2,1)S(1)} %shard_map.67.refs_2_, bf16[4,768,256]{2,1,0:T(8,128)(2,1)S(1)} %collective-permute-done.24.refs_3_), custom_call_target="tpu_custom_call" | custom-call | tf_op jit(solution)/shard_map/pallas_call | solution.py:210
  103.4 2.4 %collective-permute-start.32 = (bf16[2,768,256]{2,1,0:T(8,128)(2,1)S(1)}, bf16[2,768,256]{2,1,0:T(8,128)(2,1)S(1)}, u32[]{:S(2)}, u32[]{:S(2)}) collective-permute-start(bf16[2,768,256]{2,1,0:T(8,128)(2,1)S(1)} %get-tuple-element.82), channel_id=1, source_target_pairs={{48,0},{49,1},{50,2},{51,3},{52,4},{53,5},{54,6},{55,7},{56,8},{57... | collective-permute-start | bytes 2359304 | tf_op jit(solution)/shard_map/ppermute | solution.py:34
  105.9 3.3 %collective-permute-done.27.refs_5_ = bf16[2,768,256]{2,1,0:T(8,128)(2,1)S(1)} collective-permute-done((bf16[2,768,256]{2,1,0:T(8,128)(2,1)S(1)}, bf16[2,768,256]{2,1,0:T(8,128)(2,1)S(1)}, u32[]{:S(2)}, u32[]{:S(2)}) %collective-permute-start.27) | collective-permute-done | bytes 786464 | tf_op jit(solution)/shard_map/ppermute | solution.py:34
  109.2 2.4 %shard_map.72 = (bf16[1,768,256]{2,1,0:T(8,128)(2,1)S(1)}, bf16[1,768,256]{2,1,0:T(8,128)(2,1)S(1)}, bf16[1,768,256]{2,1,0:T(8,128)(2,1)S(1)}, bf16[1,768,256]{2,1,0:T(8,128)(2,1)S(1)}) custom-call(s32[3]{0:T(128)S(1)} %pad_add_fusion.refs_0_, bf16[256,6144]{1,0:T(8,128)(2,1)S(1)} %bitcast.65, bf16[2,2,256,256]{3,2,1,0:T(8,128)(2,1)S(1)} %shard_map.67.refs_2_, ...), custom_call_target="tpu_custom_call" | custom-call | tf_op jit(solution)/shard_map/pallas_call | solution.py:210
  113.7 2.2 %shard_map.73 = (bf16[2,768,256]{2,1,0:T(8,128)(2,1)S(1)}, bf16[2,768,256]{2,1,0:T(8,128)(2,1)S(1)}) custom-call(s32[3]{0:T(128)S(1)} %pad_add_fusion.refs_0_, bf16[256,6144]{1,0:T(8,128)(2,1)S(1)} %bitcast.66, bf16[2,2,256,256]{3,2,1,0:T(8,128)(2,1)S(1)} %shard_map.67.refs_2_, bf16[8,768,256]{2,1,0:T(8,128)(2,1)S(1)} %collective-permute-done.25.refs_3_), custom_call_target="tpu_custom_call" | custom-call | tf_op jit(solution)/shard_map/pallas_call | solution.py:210
  121.8 4.2 %collective-permute-done.35 = bf16[1,768,256]{2,1,0:T(8,128)(2,1)S(1)} collective-permute-done((bf16[1,768,256]{2,1,0:T(8,128)(2,1)S(1)}, bf16[1,768,256]{2,1,0:T(8,128)(2,1)S(1)}, u32[]{:S(2)}, u32[]{:S(2)}) %collective-permute-start.35) | collective-permute-done | bytes 393248 | tf_op jit(solution)/shard_map/ppermute | solution.py:34
  126.4 3.1 %collective-permute-start.36 = (bf16[768,256]{1,0:T(8,128)(2,1)S(1)}, bf16[768,256]{1,0:T(8,128)(2,1)}, u32[]{:S(2)}, u32[]{:S(2)}) collective-permute-start(bf16[768,256]{1,0:T(8,128)(2,1)S(1)} %get-tuple-element.86), channel_id=1, source_target_pairs={{8,0},{9,1},{10,2},{11,3},{12,4},{13,5},{14,6},{15,7},{0,8},{1,9},... | collective-permute-start | bytes 1179656 | tf_op jit(solution)/shard_map/ppermute | solution.py:38
  129.5 10.2 %collective-permute-done.34 = bf16[768,256]{1,0:T(8,128)(2,1)} collective-permute-done((bf16[768,256]{1,0:T(8,128)(2,1)S(1)}, bf16[768,256]{1,0:T(8,128)(2,1)}, u32[]{:S(2)}, u32[]{:S(2)}) %collective-permute-start.34) | collective-permute-done | bytes 393248 | tf_op jit(solution)/shard_map/ppermute | solution.py:38
  142.8 4.3 %collective-permute-done.37 = bf16[4,96,256]{2,1,0:T(8,128)(2,1)S(1)} collective-permute-done((bf16[4,96,256]{2,1,0:T(8,128)(2,1)S(1)}, bf16[4,96,256]{2,1,0:T(8,128)(2,1)S(1)}, u32[]{:S(2)}, u32[]{:S(2)}) %collective-permute-start.37) | collective-permute-done | bytes 196640 | tf_op jit(solution)/shard_map/ppermute | solution.py:46
  147.1 4.1 %collective-permute-start.38 = (bf16[96,256]{1,0:T(8,128)(2,1)S(1)}, bf16[96,256]{1,0:T(8,128)(2,1)S(1)}, u32[]{:S(2)}, u32[]{:S(2)}) collective-permute-start(bf16[96,256]{1,0:T(8,128)(2,1)S(1)} %get-tuple-element.89), channel_id=1, source_target_pairs={{4,0},{5,1},{6,2},{7,3},{0,4},{1,5},{2,6},{3,7},{12,8},{13,9},{14,... | collective-permute-start | bytes 147464 | tf_op jit(solution)/shard_map/ppermute | solution.py:42
  151.9 3.5 %collective-permute-start.40 = (bf16[96,256]{1,0:T(8,128)(2,1)S(1)}, bf16[96,256]{1,0:T(8,128)(2,1)S(1)}, u32[]{:S(2)}, u32[]{:S(2)}) collective-permute-start(bf16[96,256]{1,0:T(8,128)(2,1)S(1)} %get-tuple-element.90), channel_id=1, source_target_pairs={{2,0},{3,1},{4,2},{5,3},{6,4},{7,5},{0,6},{1,7},{10,8},{11,9},{12,... | collective-permute-start | bytes 147464 | tf_op jit(solution)/shard_map/ppermute | solution.py:42
  155.4 2.2 %collective-permute-done.39 = bf16[96,256]{1,0:T(8,128)(2,1)S(1)} collective-permute-done((bf16[96,256]{1,0:T(8,128)(2,1)S(1)}, bf16[96,256]{1,0:T(8,128)(2,1)S(1)}, u32[]{:S(2)}, u32[]{:S(2)}) %collective-permute-start.39) | collective-permute-done | bytes 49184 | tf_op jit(solution)/shard_map/ppermute | solution.py:42
  (89 shorter events, 32.7 us)
Async XLA Ops:
  0.0 11.0 %collective-permute-start = (bf16[96,256]{1,0:T(8,128)(2,1)}, bf16[96,256]{1,0:T(8,128)(2,1)S(1)}, u32[]{:S(2)}, u32[]{:S(2)}) collective-permute-start(bf16[96,256]{1,0:T(8,128)(2,1)} %bitcast.85), channel_id=1, source_target_pairs={{2,0},{3,1},{4,2},{5,3},{6,4},{7,5},{0,6},{1,7},{10,8},{11,9},{12,... | collective-permute-start | bytes 147464 | tf_op jit(solution)/shard_map/ppermute | solution.py:42
  6.4 8.5 %collective-permute-start.1 = (bf16[96,256]{1,0:T(8,128)(2,1)}, bf16[96,256]{1,0:T(8,128)(2,1)S(1)}, u32[]{:S(2)}, u32[]{:S(2)}) collective-permute-start(bf16[96,256]{1,0:T(8,128)(2,1)} %bitcast.86), channel_id=1, source_target_pairs={{4,0},{5,1},{6,2},{7,3},{0,4},{1,5},{2,6},{3,7},{12,8},{13,9},{14,... | collective-permute-start | bytes 147464 | tf_op jit(solution)/shard_map/ppermute | solution.py:42
  7.4 7.5 %collective-permute-start.2 = (bf16[96,256]{1,0:T(8,128)(2,1)}, bf16[96,256]{1,0:T(8,128)(2,1)S(1)}, u32[]{:S(2)}, u32[]{:S(2)}) collective-permute-start(bf16[96,256]{1,0:T(8,128)(2,1)} %bitcast.87), channel_id=1, source_target_pairs={{6,0},{7,1},{0,2},{1,3},{2,4},{3,5},{4,6},{5,7},{14,8},{15,9},{8,1... | collective-permute-start | bytes 147464 | tf_op jit(solution)/shard_map/ppermute | solution.py:42
  20.8 15.2 %collective-permute-start.4 = (bf16[768,256]{1,0:T(8,128)(2,1)S(1)}, bf16[768,256]{1,0:T(8,128)(2,1)}, u32[]{:S(2)}, u32[]{:S(2)}) collective-permute-start(bf16[768,256]{1,0:T(8,128)(2,1)S(1)} %bitcast.79), channel_id=1, source_target_pairs={{128,0},{129,1},{130,2},{131,3},{132,4},{133,5},{134,6},{135,7},{1... | collective-permute-start | bytes 1179656 | tf_op jit(solution)/shard_map/ppermute | solution.py:38
  21.6 14.4 %collective-permute-start.5 = (bf16[768,256]{1,0:T(8,128)(2,1)S(1)}, bf16[768,256]{1,0:T(8,128)(2,1)}, u32[]{:S(2)}, u32[]{:S(2)}) collective-permute-start(bf16[768,256]{1,0:T(8,128)(2,1)S(1)} %bitcast.80), channel_id=1, source_target_pairs={{8,0},{9,1},{10,2},{11,3},{12,4},{13,5},{14,6},{15,7},{0,8},{1,9},... | collective-permute-start | bytes 1179656 | tf_op jit(solution)/shard_map/ppermute | solution.py:38
  22.5 13.4 %collective-permute-start.6 = (bf16[768,256]{1,0:T(8,128)(2,1)S(1)}, bf16[768,256]{1,0:T(8,128)(2,1)}, u32[]{:S(2)}, u32[]{:S(2)}) collective-permute-start(bf16[768,256]{1,0:T(8,128)(2,1)S(1)} %bitcast.81), channel_id=1, source_target_pairs={{136,0},{137,1},{138,2},{139,3},{140,4},{141,5},{142,6},{143,7},{1... | collective-permute-start | bytes 1179656 | tf_op jit(solution)/shard_map/ppermute | solution.py:38
  26.6 8.6 %collective-permute-start.8 = (f32[2,4,256]{2,1,0:T(4,128)}, f32[2,4,256]{2,1,0:T(4,128)}, u32[]{:S(2)}, u32[]{:S(2)}) collective-permute-start(f32[2,4,256]{2,1,0:T(4,128)} %get-tuple-element.92), channel_id=1, source_target_pairs={{0,128},{128,0},{1,129},{129,1},{2,130},{130,2},{3,131},{131,3},{4... | collective-permute-start | bytes 24584 | tf_op jit(solution)/shard_map/ppermute | solution.py:275
  38.4 7.1 %collective-permute-start.16 = (bf16[2,768,256]{2,1,0:T(8,128)(2,1)}, bf16[2,768,256]{2,1,0:T(8,128)(2,1)}, u32[]{:S(2)}, u32[]{:S(2)}) collective-permute-start(bf16[2,768,256]{2,1,0:T(8,128)(2,1)} %get-tuple-element.48.refs_6_), channel_id=1, source_target_pairs={{0,64},{64,0},{1,65},{65,1},{2,66},{66,2},{3,67},{67,3},{4,68},{68... | collective-permute-start | bytes 2359304 | tf_op jit(solution)/shard_map/ppermute | solution.py:50
  38.9 13.7 %collective-permute-start.13 = (bf16[2,768,256]{2,1,0:T(8,128)(2,1)}, bf16[2,768,256]{2,1,0:T(8,128)(2,1)}, u32[]{:S(2)}, u32[]{:S(2)}) collective-permute-start(bf16[2,768,256]{2,1,0:T(8,128)(2,1)} %get-tuple-element.48.refs_6_), channel_id=1, source_target_pairs={{16,0},{17,1},{18,2},{19,3},{20,4},{21,5},{22,6},{23,7},{24,8},{25... | collective-permute-start | bytes 2359304 | tf_op jit(solution)/shard_map/ppermute | solution.py:34
  39.8 12.9 %collective-permute-start.14 = (bf16[2,768,256]{2,1,0:T(8,128)(2,1)}, bf16[2,768,256]{2,1,0:T(8,128)(2,1)}, u32[]{:S(2)}, u32[]{:S(2)}) collective-permute-start(bf16[2,768,256]{2,1,0:T(8,128)(2,1)} %get-tuple-element.47.refs_5_), channel_id=1, source_target_pairs={{48,0},{49,1},{50,2},{51,3},{52,4},{53,5},{54,6},{55,7},{56,8},{57... | collective-permute-start | bytes 2359304 | tf_op jit(solution)/shard_map/ppermute | solution.py:34
  42.3 18.5 %collective-permute-start.9 = (bf16[2,768,256]{2,1,0:T(8,128)(2,1)}, bf16[2,768,256]{2,1,0:T(8,128)(2,1)S(1)}, u32[]{:S(2)}, u32[]{:S(2)}) collective-permute-start(bf16[2,768,256]{2,1,0:T(8,128)(2,1)} %get-tuple-element.47.refs_5_), channel_id=1, source_target_pairs={{16,0},{17,1},{18,2},{19,3},{20,4},{21,5},{22,6},{23,7},{24,8},{25... | collective-permute-start | bytes 2359304 | tf_op jit(solution)/shard_map/ppermute | solution.py:34
  42.3 18.5 %collective-permute-start.11 = (bf16[2,768,256]{2,1,0:T(8,128)(2,1)}, bf16[2,768,256]{2,1,0:T(8,128)(2,1)S(1)}, u32[]{:S(2)}, u32[]{:S(2)}) collective-permute-start(bf16[2,768,256]{2,1,0:T(8,128)(2,1)} %get-tuple-element.48.refs_6_), channel_id=1, source_target_pairs={{48,0},{49,1},{50,2},{51,3},{52,4},{53,5},{54,6},{55,7},{56,8},{57... | collective-permute-start | bytes 2359304 | tf_op jit(solution)/shard_map/ppermute | solution.py:34
  52.7 8.6 %collective-permute-start.19 = (bf16[2,768,256]{2,1,0:T(8,128)(2,1)}, bf16[2,768,256]{2,1,0:T(8,128)(2,1)S(1)}, u32[]{:S(2)}, u32[]{:S(2)}) collective-permute-start(bf16[2,768,256]{2,1,0:T(8,128)(2,1)} %collective-permute-done.13.refs_7_), channel_id=1, source_target_pairs={{0,64},{64,0},{1,65},{65,1},{2,66},{66,2},{3,67},{67,3},{4,68},{68... | collective-permute-start | bytes 2359304 | tf_op jit(solution)/shard_map/ppermute | solution.py:50
  52.9 11.6 %collective-permute-start.20 = (bf16[2,768,256]{2,1,0:T(8,128)(2,1)}, bf16[2,768,256]{2,1,0:T(8,128)(2,1)S(1)}, u32[]{:S(2)}, u32[]{:S(2)}) collective-permute-start(bf16[2,768,256]{2,1,0:T(8,128)(2,1)} %collective-permute-done.14.refs_8_), channel_id=1, source_target_pairs={{0,64},{64,0},{1,65},{65,1},{2,66},{66,2},{3,67},{67,3},{4,68},{68... | collective-permute-start | bytes 2359304 | tf_op jit(solution)/shard_map/ppermute | solution.py:50
  61.3 13.2 %collective-permute-start.10 = (bf16[2,768,256]{2,1,0:T(8,128)(2,1)S(1)}, bf16[2,768,256]{2,1,0:T(8,128)(2,1)S(1)}, u32[]{:S(2)}, u32[]{:S(2)}) collective-permute-start(bf16[2,768,256]{2,1,0:T(8,128)(2,1)S(1)} %collective-permute-done.9.refs_5_), channel_id=1, source_target_pairs={{16,0},{17,1},{18,2},{19,3},{20,4},{21,5},{22,6},{23,7},{24,8},{25... | collective-permute-start | bytes 2359304 | tf_op jit(solution)/shard_map/ppermute | solution.py:34
  61.3 13.2 %collective-permute-start.12 = (bf16[2,768,256]{2,1,0:T(8,128)(2,1)S(1)}, bf16[2,768,256]{2,1,0:T(8,128)(2,1)S(1)}, u32[]{:S(2)}, u32[]{:S(2)}) collective-permute-start(bf16[2,768,256]{2,1,0:T(8,128)(2,1)S(1)} %collective-permute-done.11.refs_6_), channel_id=1, source_target_pairs={{48,0},{49,1},{50,2},{51,3},{52,4},{53,5},{54,6},{55,7},{56,8},{57... | collective-permute-start | bytes 2359304 | tf_op jit(solution)/shard_map/ppermute | solution.py:34
  83.8 6.0 %collective-permute-start.23 = (bf16[4,768,256]{2,1,0:T(8,128)(2,1)S(1)}, bf16[4,768,256]{2,1,0:T(8,128)(2,1)S(1)}, u32[]{:S(2)}, u32[]{:S(2)}) collective-permute-start(bf16[4,768,256]{2,1,0:T(8,128)(2,1)S(1)} %shard_map.68), channel_id=1, source_target_pairs={{0,64},{64,0},{1,65},{65,1},{2,66},{66,2},{3,67},{67,3},{4,68},{68... | collective-permute-start | bytes 4718600 | tf_op jit(solution)/shard_map/ppermute | solution.py:50
  92.1 17.1 %collective-permute-start.25 = (bf16[8,768,256]{2,1,0:T(8,128)(2,1)S(1)}, bf16[8,768,256]{2,1,0:T(8,128)(2,1)S(1)}, u32[]{:S(2)}, u32[]{:S(2)}) collective-permute-start(bf16[8,768,256]{2,1,0:T(8,128)(2,1)S(1)} %shard_map.70), channel_id=1, source_target_pairs={{0,64},{64,0},{1,65},{65,1},{2,66},{66,2},{3,67},{67,3},{4,68},{68... | collective-permute-start | bytes 9437192 | tf_op jit(solution)/shard_map/ppermute | solution.py:50
  92.6 7.5 %collective-permute-start.24 = (bf16[4,768,256]{2,1,0:T(8,128)(2,1)S(1)}, bf16[4,768,256]{2,1,0:T(8,128)(2,1)S(1)}, u32[]{:S(2)}, u32[]{:S(2)}) collective-permute-start(bf16[4,768,256]{2,1,0:T(8,128)(2,1)S(1)} %shard_map.69), channel_id=1, source_target_pairs={{0,64},{64,0},{1,65},{65,1},{2,66},{66,2},{3,67},{67,3},{4,68},{68... | collective-permute-start | bytes 4718600 | tf_op jit(solution)/shard_map/ppermute | solution.py:50
  92.7 13.2 %collective-permute-start.26 = (bf16[2,768,256]{2,1,0:T(8,128)(2,1)S(1)}, bf16[2,768,256]{2,1,0:T(8,128)(2,1)S(1)}, u32[]{:S(2)}, u32[]{:S(2)}) collective-permute-start(bf16[2,768,256]{2,1,0:T(8,128)(2,1)S(1)} %get-tuple-element.69), channel_id=1, source_target_pairs={{48,0},{49,1},{50,2},{51,3},{52,4},{53,5},{54,6},{55,7},{56,8},{57... | collective-permute-start | bytes 2359304 | tf_op jit(solution)/shard_map/ppermute | solution.py:34
  95.9 13.2 %collective-permute-start.27 = (bf16[2,768,256]{2,1,0:T(8,128)(2,1)S(1)}, bf16[2,768,256]{2,1,0:T(8,128)(2,1)S(1)}, u32[]{:S(2)}, u32[]{:S(2)}) collective-permute-start(bf16[2,768,256]{2,1,0:T(8,128)(2,1)S(1)} %get-tuple-element.70), channel_id=1, source_target_pairs={{16,0},{17,1},{18,2},{19,3},{20,4},{21,5},{22,6},{23,7},{24,8},{25... | collective-permute-start | bytes 2359304 | tf_op jit(solution)/shard_map/ppermute | solution.py:34
  102.4 15.1 %collective-permute-start.29 = (bf16[2,768,256]{2,1,0:T(8,128)(2,1)S(1)}, bf16[2,768,256]{2,1,0:T(8,128)(2,1)S(1)}, u32[]{:S(2)}, u32[]{:S(2)}) collective-permute-start(bf16[2,768,256]{2,1,0:T(8,128)(2,1)S(1)} %get-tuple-element.79), channel_id=1, source_target_pairs={{16,0},{17,1},{18,2},{19,3},{20,4},{21,5},{22,6},{23,7},{24,8},{25... | collective-permute-start | bytes 2359304 | tf_op jit(solution)/shard_map/ppermute | solution.py:34
  103.4 18.0 %collective-permute-start.32 = (bf16[2,768,256]{2,1,0:T(8,128)(2,1)S(1)}, bf16[2,768,256]{2,1,0:T(8,128)(2,1)S(1)}, u32[]{:S(2)}, u32[]{:S(2)}) collective-permute-start(bf16[2,768,256]{2,1,0:T(8,128)(2,1)S(1)} %get-tuple-element.82), channel_id=1, source_target_pairs={{48,0},{49,1},{50,2},{51,3},{52,4},{53,5},{54,6},{55,7},{56,8},{57... | collective-permute-start | bytes 2359304 | tf_op jit(solution)/shard_map/ppermute | solution.py:34
  111.5 8.1 %collective-permute-start.30 = (bf16[1,768,256]{2,1,0:T(8,128)(2,1)S(1)}, bf16[1,768,256]{2,1,0:T(8,128)(2,1)S(1)}, u32[]{:S(2)}, u32[]{:S(2)}) collective-permute-start(bf16[1,768,256]{2,1,0:T(8,128)(2,1)S(1)} %get-tuple-element.80), channel_id=1, source_target_pairs={{48,0},{49,1},{50,2},{51,3},{52,4},{53,5},{54,6},{55,7},{56,8},{57... | collective-permute-start | bytes 1179656 | tf_op jit(solution)/shard_map/ppermute | solution.py:34
  111.6 10.2 %collective-permute-start.33 = (bf16[1,768,256]{2,1,0:T(8,128)(2,1)S(1)}, bf16[1,768,256]{2,1,0:T(8,128)(2,1)S(1)}, u32[]{:S(2)}, u32[]{:S(2)}) collective-permute-start(bf16[1,768,256]{2,1,0:T(8,128)(2,1)S(1)} %get-tuple-element.83), channel_id=1, source_target_pairs={{16,0},{17,1},{18,2},{19,3},{20,4},{21,5},{22,6},{23,7},{24,8},{25... | collective-permute-start | bytes 1179656 | tf_op jit(solution)/shard_map/ppermute | solution.py:34
  113.6 12.4 %collective-permute-start.35 = (bf16[1,768,256]{2,1,0:T(8,128)(2,1)S(1)}, bf16[1,768,256]{2,1,0:T(8,128)(2,1)S(1)}, u32[]{:S(2)}, u32[]{:S(2)}) collective-permute-start(bf16[1,768,256]{2,1,0:T(8,128)(2,1)S(1)} %get-tuple-element.84), channel_id=1, source_target_pairs={{16,0},{17,1},{18,2},{19,3},{20,4},{21,5},{22,6},{23,7},{24,8},{25... | collective-permute-start | bytes 1179656 | tf_op jit(solution)/shard_map/ppermute | solution.py:34
  117.6 11.9 %collective-permute-start.28 = (bf16[1,768,256]{2,1,0:T(8,128)(2,1)S(1)}, bf16[1,768,256]{2,1,0:T(8,128)(2,1)S(1)}, u32[]{:S(2)}, u32[]{:S(2)}) collective-permute-start(bf16[1,768,256]{2,1,0:T(8,128)(2,1)S(1)} %get-tuple-element.77), channel_id=1, source_target_pairs={{48,0},{49,1},{50,2},{51,3},{52,4},{53,5},{54,6},{55,7},{56,8},{57... | collective-permute-start | bytes 1179656 | tf_op jit(solution)/shard_map/ppermute | solution.py:34
  119.8 9.7 %collective-permute-start.31 = (bf16[768,256]{1,0:T(8,128)(2,1)S(1)}, bf16[768,256]{1,0:T(8,128)(2,1)}, u32[]{:S(2)}, u32[]{:S(2)}) collective-permute-start(bf16[768,256]{1,0:T(8,128)(2,1)S(1)} %fusion.4), channel_id=1, source_target_pairs={{136,0},{137,1},{138,2},{139,3},{140,4},{141,5},{142,6},{143,7},{1... | collective-permute-start | bytes 1179656 | tf_op jit(solution)/shard_map/ppermute | solution.py:38
  126.3 13.4 %collective-permute-start.34 = (bf16[768,256]{1,0:T(8,128)(2,1)S(1)}, bf16[768,256]{1,0:T(8,128)(2,1)}, u32[]{:S(2)}, u32[]{:S(2)}) collective-permute-start(bf16[768,256]{1,0:T(8,128)(2,1)S(1)} %get-tuple-element.85), channel_id=1, source_target_pairs={{128,0},{129,1},{130,2},{131,3},{132,4},{133,5},{134,6},{135,7},{1... | collective-permute-start | bytes 1179656 | tf_op jit(solution)/shard_map/ppermute | solution.py:38
  126.4 13.3 %collective-permute-start.36 = (bf16[768,256]{1,0:T(8,128)(2,1)S(1)}, bf16[768,256]{1,0:T(8,128)(2,1)}, u32[]{:S(2)}, u32[]{:S(2)}) collective-permute-start(bf16[768,256]{1,0:T(8,128)(2,1)S(1)} %get-tuple-element.86), channel_id=1, source_target_pairs={{8,0},{9,1},{10,2},{11,3},{12,4},{13,5},{14,6},{15,7},{0,8},{1,9},... | collective-permute-start | bytes 1179656 | tf_op jit(solution)/shard_map/ppermute | solution.py:38
  147.1 8.2 %collective-permute-start.38 = (bf16[96,256]{1,0:T(8,128)(2,1)S(1)}, bf16[96,256]{1,0:T(8,128)(2,1)S(1)}, u32[]{:S(2)}, u32[]{:S(2)}) collective-permute-start(bf16[96,256]{1,0:T(8,128)(2,1)S(1)} %get-tuple-element.89), channel_id=1, source_target_pairs={{4,0},{5,1},{6,2},{7,3},{0,4},{1,5},{2,6},{3,7},{12,8},{13,9},{14,... | collective-permute-start | bytes 147464 | tf_op jit(solution)/shard_map/ppermute | solution.py:42
  151.3 6.3 %collective-permute-start.39 = (bf16[96,256]{1,0:T(8,128)(2,1)S(1)}, bf16[96,256]{1,0:T(8,128)(2,1)S(1)}, u32[]{:S(2)}, u32[]{:S(2)}) collective-permute-start(bf16[96,256]{1,0:T(8,128)(2,1)S(1)} %get-tuple-element.91), channel_id=1, source_target_pairs={{6,0},{7,1},{0,2},{1,3},{2,4},{3,5},{4,6},{5,7},{14,8},{15,9},{8,1... | collective-permute-start | bytes 147464 | tf_op jit(solution)/shard_map/ppermute | solution.py:42
  (14 other events, 136.2 us)
